TPU v7x, 32 devices: a whole 2x2x4 slice. The times are simulated.
32 devices in a mesh: groups: 2 (over y), vocab: 4 (over z), rows: 2 (over x), cfg: 2 (over core).
Axes of the slice: x: 2, y: 2, z: 4, core: 2. Of those that a mesh axis runs over, the one named last changes fastest.
Arguments:
- final_hidden: bfloat16 [2, 512, 8192], P(None, ('groups', 'vocab'), ('rows', 'cfg')), parts along dimension 1
- positions: int32 [352], P('groups'), parts along dimension 0, may hold values from 0 to 255, as said below
- norm_gain: float32 [8192], P(('rows', 'cfg')), may hold values from 0.1 to 1.9
- unembedding: bfloat16 [8192, 19008], P(('rows', 'cfg'), 'vocab')
Outputs:
- guided_logprobs: float32 [352, 19008], P(('groups', 'rows', 'cfg'), 'vocab'), parts along dimension 0
There are 2 independent parts, one for each index of `groups`. A program takes and returns all parts, laid end to end along the dimension named above; an argument that names none is the same for every part. Nothing has to cross between parts.
Inputs may be any that keep to these rules, and one draw needn't show every extreme that they name: 176 distinct positions in increasing order; 0 and 255 are always among them.
All inputs are finite; a program needn't handle non-finite values.
Results may differ from a plain program's by a relative error of at most 0.0008.
Values may be sent and summed in bfloat16 or wider, within the bound.
No kernel may reach another device: no remote copies, remote signals or barrier semaphores. Data moves between devices by JAX's collectives and lax.ppermute only.
A program may use at most 128 MiB of HBM per device.

v0:
```python
import jax
import jax.numpy as jnp
from jax import lax
from jax.sharding import PartitionSpec as P

D = 8192


epsilon = 1e-06
guidance = 2.0


def joined(value, axis, join):
    pieces = jax.tree.map(lambda part: lax.all_gather(part, axis), value)
    head = jax.tree.map(lambda part: part[0], pieces)
    tail = jax.tree.map(lambda part: part[1:], pieces)
    so_far, _ = lax.scan(lambda so_far, slab: (join(so_far, slab), None), head, tail)
    return so_far


def choose_rows(positions, length):
    return (positions[:, None] == jnp.arange(length)[None, :]).astype(jnp.bfloat16)


def per_device(final_hidden, positions, norm_gain, unembedding):
    width_local = final_hidden.shape[2]
    masked = positions.shape[0]
    block_rows = lax.all_gather(final_hidden, "vocab", axis=1, tiled=True)
    chooser = choose_rows(positions, block_rows.shape[1])
    gathered = jnp.einsum("rs,bsd->brd", chooser, block_rows, preferred_element_type=jnp.float32)
    picked = gathered.astype(jnp.bfloat16)
    widened = picked.astype(jnp.float32)
    squares = jnp.sum(widened * widened, axis=2)
    totals = lax.psum(squares, ("rows", "cfg"))
    inv_rms = lax.rsqrt(totals / D + epsilon)
    normed = (widened * norm_gain).astype(jnp.bfloat16)
    own_rows = masked // lax.axis_size(("rows", "cfg"))
    products = jnp.dot(
        normed.reshape(2 * (lax.axis_size(("rows", "cfg")) * own_rows), width_local),
        unembedding,
        preferred_element_type=jnp.float32,
    )
    products = products.reshape(2, lax.axis_size(("rows", "cfg")) * own_rows, unembedding.shape[1])
    guided = lax.psum_scatter(
        (1.0 + guidance) * inv_rms[0][:, None] * products[0]
        - guidance * inv_rms[1][:, None] * products[1],
        ("rows", "cfg"),
        scatter_dimension=0,
        tiled=True,
    )
    local_top = jnp.max(guided, axis=1)
    local_total = jnp.sum(jnp.exp(guided - local_top[:, None]), axis=1)

    def combine(earlier, later):
        peak = jnp.maximum(earlier[0], later[0])
        return (peak, earlier[1] * jnp.exp(earlier[0] - peak) + later[1] * jnp.exp(later[0] - peak))

    row_top, row_total = joined((local_top, local_total), "vocab", combine)
    return guided - row_top[:, None] - jnp.log(row_total)[:, None]


def solution(mesh):
    placed = (
        P(None, ("groups", "vocab"), ("rows", "cfg")),
        P("groups"),
        P(("rows", "cfg")),
        P(("rows", "cfg"), "vocab"),
    )
    return jax.shard_map(
        per_device,
        mesh=mesh,
        in_specs=placed,
        out_specs=P(("groups", "rows", "cfg"), "vocab"),
        check_vma=False,
    )
```

profile of v0, /device:TPU:0, one launch (start us, length us, event | category | flops | bytes accessed | tf_op | source)
XLA Modules:
  0.0 149.6 jit_solution(293299678426957341)
XLA Ops:
  6.5 0.0 all-gather.4.cloned.1.call-start
  6.5 0.7 all-gather.4.cloned.1.call-update
  7.3 50.3 %all-gather.4.cloned.1.call-done = bf16[2,256,2048]{2,1,0:T(8,128)(2,1)} async-done(((bf16[2,64,2048]{2,1,0:T(8,128)(2,1)}), bf16[2,256,2048]{2,1,0:T(8,128)(2,1)}) %all-gather.4.cloned.1.call-update) | async-done | bytes 2097168 | tf_op jit(solution)/shard_map/all_gather | solution.py:28
  57.6 2.4 %fusion.7 = (f32[176,2]{0,1:T(2,128)S(1)}, bf16[176,2,2048]{2,0,1:T(8,128)(2,1)S(1)}) fusion(f32[2048]{0:T(1024)} %param.8, bf16[2,256,2048]{2,1,0:T(8,128)(2,1)} %all-gather.4.cloned.1.call-done, s32[176]{0:T(256)} %param.7), kind=kOutput, calls=%fused_computation.12 | convolution fusion | flops 373468832 | bytes 3549248 | tf_op jit(solution)/shard_map/rs,bsd->brd/dot_general | solution.py:30
  60.0 6.8 %psum.7 = f32[2,176]{1,0:T(2,128)S(1)} all-reduce(f32[2,176]{1,0:T(2,128)S(1)} %bitcast.35), channel_id=1, replica_groups=mesh['groups'=2,'vocab'=4,'rows'=2,'cfg'=2] {'rows','cfg'}, use_global_device_ids=true, to_apply=%region_1.0 | all-reduce | flops 352 | bytes 2816 | tf_op jit(solution)/shard_map/psum | solution.py:34
  66.8 14.1 %fusion.13 = f32[352,4752]{1,0:T(8,128)} fusion(bf16[352,2048]{1,0:T(8,128)(2,1)S(1)} %bitcast.36, bf16[2048,4752]{0,1:T(8,128)(2,1)} %param.9), kind=kOutput, calls=%fused_computation.24 | convolution fusion | flops 6851395584 | bytes 27596800 | tf_op jit(solution)/shard_map/dot_general | solution.py:38
  80.9 3.5 %fusion.6 = f32[176,4752]{1,0:T(8,128)S(1)} fusion(f32[352,4752]{1,0:T(8,128)} %fusion.13, f32[176]{0:T(256)S(1)} %bitcast.34, f32[176]{0:T(256)S(1)} %bitcast.33), kind=kLoop, calls=%fused_computation.10 | loop fusion | flops 2509056 | bytes 10037632 | tf_op jit(solution)/shard_map/sub | solution.py:45
  84.4 0.0 copy-start
  84.4 0.0 copy-start.1
  84.4 36.2 %fusion = f32[48,4752]{1,0:T(8,128)} fusion(f32[176,4752]{1,0:T(8,128)S(1)} %fusion.6), kind=kCustom, calls=%all-reduce-scatter | all-reduce-scatter fusion | flops 912385 | bytes 4258304
  120.6 1.0 slice.42
  121.6 1.3 collective-permute-start
  122.9 0.0 copy-done
  122.9 0.6 dynamic-slice.6
  124.1 0.0 copy-done.1
  124.1 0.6 dynamic-slice
  125.2 0.0 collective-permute-done
  125.2 5.6 %concatenate = f32[60,4752]{1,0:T(8,128)S(1)} concatenate(f32[12,4752]{1,0:T(8,128)S(1)} %collective-permute-done, f32[48,4752]{1,0:T(8,128)} %fusion), dimensions={0} | concatenate | bytes 2280960
  130.8 0.2 dynamic-slice_reduce_fusion
  131.0 0.3 exponential_reduce_fusion
  131.4 0.2 dynamic-update-slice
  131.6 0.2 dynamic-update-slice.1
  131.8 9.5 %all-reduce.4 = (f32[176]{0:T(256)S(1)}, f32[176]{0:T(256)S(1)}) all-reduce(f32[176]{0:T(256)S(1)} %dynamic-update-slice, f32[176]{0:T(256)S(1)} %dynamic-update-slice.1), channel_id=2, replica_groups=mesh['groups'=2,'vocab'=4,'rows'=2,'cfg'=2] {'vocab'}, use_global_device_ids=true, to_apply=%add | all-reduce | flops 352 | bytes 2816
  141.3 0.1 slice.36
  141.4 0.1 slice.37
  141.4 0.1 reshape.38
  141.5 0.1 reshape.39
  141.6 0.1 while.12
  141.7 1.1 subtract_subtract_fusion
  (10 shorter events, 0.1 us)
Async XLA Ops:
  6.5 51.1 %all-gather.4.cloned.1.call-start = ((), (), s32[]{:S(2)}) async-start(), calls=%async_computation | async-start | bytes 2621440 | tf_op jit(solution)/shard_map/all_gather | solution.py:28
  84.4 38.5 %copy-start = (u32[32]{0:T(128)S(1)}, u32[32]{0:T(128)}, u32[]{:S(2)}) copy-start(u32[32]{0:T(128)} %constant.37) | copy-start | bytes 388
  84.4 39.7 %copy-start.1 = (u32[32]{0:T(128)S(1)}, u32[32]{0:T(128)}, u32[]{:S(2)}) copy-start(u32[32]{0:T(128)} %constant.25) | copy-start | bytes 388
  121.6 3.6 %collective-permute-start = (f32[12,4752]{1,0:T(8,128)S(1)}, f32[12,4752]{1,0:T(8,128)S(1)}, u32[]{:S(2)}, u32[]{:S(2)}) collective-permute-start(f32[12,4752]{1,0:T(8,128)S(1)} %slice.42), channel_id=1, source_target_pairs={{0,1},{1,2},{2,3},{4,5},{5,6},{6,7},{8,9},{9,10},{10,11},{12,13},{... | collective-permute-start | bytes 684296
Sparse Core Ops, SparseCore 0:
  8.9 48.6 all-gather.3
where the time goes:
time: 152 us; the launch traced here: 150 us
  blocking collectives  52.5 us (35%)
  waiting for transfers between devices  51.1 us (34%)
  matrix products  16.4 us (11%)
  between operations  14.6 us (10%)
  local copies, waits for them, and re-layouts  8.49 us (6%)
  other arithmetic  5.21 us (3%)
    all_gather x1, waiting for transfers between devices, per_device(): block_rows = lax.all_gather(final_hidden, 'vocab', axis=1, tiled=True)  50.3 us
    unnamed x2, blocking collectives  45.6 us
    dot_general x1, matrix products, per_device(): jnp.dot(normed.reshape(2 * (lax.axis_size(('rows', 'cfg')) * own_rows), w...  14.1 us
    unnamed x12, local copies, waits for them, and re-layouts  8.17 us
    psum x1, blocking collectives, per_device(): totals = lax.psum(squares, ('rows', 'cfg'))  6.84 us
    sub x1, other arithmetic, per_device(): (1.0 + guidance) * inv_rms[0][:, None] * products[0]  3.47 us
  transfers between devices with their start and end apart: 2, of which 1 were waited for; matrix products, arithmetic and copies ran while one was open for 1% of the time, Pallas kernels for 0%

commit v1 on v0

v1 whole, which is shorter than its diff:
```python
import functools

import jax
import jax.numpy as jnp
from jax import lax
from jax.experimental import pallas as pl
from jax.experimental.pallas import tpu as pltpu
from jax.sharding import PartitionSpec as P

epsilon = 1e-06
guidance = 2.0
TILE = 256
LANES = 128
MIB = 1 << 20


def in_vmem(count):
    return [pl.BlockSpec(memory_space=pltpu.VMEM)] * count


def keep_in_vmem(*arrays):
    return [pltpu.with_memory_space_constraint(a, pltpu.VMEM) for a in arrays]


def call(body, outs, args, far=(), limit=8, cost=None, **kwargs):
    return pl.pallas_call(
        body,
        out_shape=[pltpu.VMEM(shape, dtype) for shape, dtype in outs],
        in_specs=[pl.BlockSpec(memory_space=pltpu.HBM)] * len(far) + in_vmem(len(args)),
        out_specs=in_vmem(len(outs)),
        compiler_params=pltpu.CompilerParams(vmem_limit_bytes=limit * MIB),
        cost_estimate=cost and pl.CostEstimate(flops=cost[0], bytes_accessed=cost[1], transcendentals=0),
        **kwargs,
    )(*[pltpu.with_memory_space_constraint(a, pltpu.HBM) for a in far], *keep_in_vmem(*args))


def diagonal(n):
    return lax.broadcasted_iota(jnp.int32, (n, n), 0) == lax.broadcasted_iota(jnp.int32, (n, n), 1)


def as_column(row):
    return jnp.sum(jnp.where(diagonal(row.shape[1]), row, 0.0), axis=1, keepdims=True)


def as_row(column):
    return jnp.sum(jnp.where(diagonal(column.shape[0]), column, 0.0), axis=0, keepdims=True)


def squares_kernel(hidden_far, gain_far, normed_ref, out_ref, hidden_ref, gain_ref, sems):
    copies = [
        pltpu.make_async_copy(hidden_far.at[0], hidden_ref.at[0], sems.at[0]),
        pltpu.make_async_copy(hidden_far.at[1], hidden_ref.at[1], sems.at[1]),
        pltpu.make_async_copy(gain_far, gain_ref, sems.at[2]),
    ]
    for copy in copies:
        copy.start()
    for b in range(2):
        copies[b].wait()
        widened = hidden_ref[b].astype(jnp.float32)
        out_ref[b : b + 1] = as_row(jnp.sum(widened * widened, axis=1, keepdims=True))
    copies[2].wait()
    gain = gain_ref[...]
    for b in range(2):
        normed_ref[b] = (hidden_ref[b].astype(jnp.float32) * gain).astype(jnp.bfloat16)


def combine_kernel(width, normed_ref, totals_ref, *out_refs):
    inv_rms = lax.rsqrt(totals_ref[...] / width + epsilon)
    factor = [as_column((1.0 + guidance) * inv_rms[0:1]), as_column(guidance * inv_rms[1:2])]
    piece = out_refs[0].shape[0]
    for i, out_ref in enumerate(out_refs):
        rows = slice(i * piece, (i + 1) * piece)
        terms = [factor[b][rows] * normed_ref[b, rows, :].astype(jnp.float32) for b in range(2)]
        out_ref[...] = (terms[0] - terms[1]).astype(jnp.bfloat16)


def load_kernel(weights_far, *refs):
    *chunk_refs, sems = refs
    copies, start = [], 0
    for j, ref in enumerate(chunk_refs):
        size = ref.shape[0]
        copies.append(pltpu.make_async_copy(weights_far.at[pl.ds(start, size)], ref, sems.at[j]))
        start += size
    for copy in copies:
        copy.start()
    for copy in copies:
        copy.wait()


def multiply(rows_ref, weights_ref, keep_ref, send_ref):
    half, width = keep_ref.shape
    for at in range(0, width, TILE):
        size = min(TILE, width - at)
        product = lax.dot_general(
            rows_ref[...],
            weights_ref[at : at + size, :],
            (((1,), (1,)), ((), ())),
            preferred_element_type=jnp.float32,
        )
        keep_ref[:, at : at + size] = product[:half]
        send_ref[:, at : at + size] = product[half:]


def first_kernel(chooser_ref, weights_ref, *refs):
    *block_refs, rows_ref, keep_ref, send_ref = refs
    blocks = jnp.concatenate([ref[...] for ref in block_refs], axis=0)
    rows_ref[...] = jnp.dot(chooser_ref[...], blocks, preferred_element_type=jnp.float32).astype(jnp.bfloat16)
    multiply(rows_ref, weights_ref, keep_ref, send_ref)


def later_kernel(rows_ref, weights_ref, keep_ref, send_ref):
    multiply(rows_ref, weights_ref, keep_ref, send_ref)


def lanes_diagonal(n):
    return lax.broadcasted_iota(jnp.int32, (n, LANES), 0) == lax.broadcasted_iota(jnp.int32, (n, LANES), 1)


def add_kernel(own, keep_ref, got_ref, own_ref, *out_refs):
    segment = own_ref.shape[0]
    own_ref[...] = keep_ref[:segment] + got_ref[:segment]
    for s, out_ref in enumerate(out_refs, 1):
        rows = slice(s * segment, (s + 1) * segment)
        value = keep_ref[rows] + got_ref[rows]
        peak = jnp.max(jnp.abs(value), axis=1, keepdims=True)
        exponent = jnp.clip(jnp.ceil(jnp.log2(jnp.maximum(peak, 1e-30))), -90.0, 127.0)
        scaled = jnp.clip(jnp.round(value * jnp.exp2(15.0 - exponent)), -32767.0, 32767.0)
        out_ref[:, LANES:] = scaled[:, LANES:].astype(jnp.int32).astype(jnp.int16)
        as_lanes = jnp.sum(jnp.where(lanes_diagonal(segment), exponent, 0.0), axis=0, keepdims=True)
        spare = lax.broadcasted_iota(jnp.int32, (segment, LANES), 0) == own
        out_ref[:, :LANES] = jnp.where(spare, as_lanes, scaled[:, :LANES]).astype(jnp.int32).astype(jnp.int16)


def restored(own, got_ref):
    value = got_ref[...].astype(jnp.int32).astype(jnp.float32)
    segment = value.shape[0]
    exponent = jnp.sum(
        jnp.where(lanes_diagonal(segment), value[own : own + 1, :LANES], 0.0), axis=1, keepdims=True
    )
    return value * jnp.exp2(exponent - 15.0)


def stats_kernel(chunks, own, *refs):
    ins, guided_refs, out_ref = refs[: -chunks - 1], refs[-chunks - 1 : -1], refs[-1]
    each = len(ins) // chunks
    top = None
    for j in range(chunks):
        guided = ins[j * each][...]
        for got in ins[j * each + 1 : (j + 1) * each]:
            guided = guided + restored(own, got)
        guided_refs[j][...] = guided
        peak = jnp.max(guided, axis=1, keepdims=True)
        top = peak if top is None else jnp.maximum(top, peak)
    total = sum(jnp.sum(jnp.exp(ref[...] - top), axis=1, keepdims=True) for ref in guided_refs)
    segment = top.shape[0]
    out_ref[0:1, :segment] = as_row(top)
    out_ref[1:2, :segment] = as_row(total)


def final_kernel(chunks, segment, *refs):
    guided_refs, stats, out_ref = refs[:chunks], refs[chunks:-1], refs[-1]
    top = functools.reduce(jnp.maximum, [ref[0:1, :segment] for ref in stats])
    total = sum(ref[1:2, :segment] * jnp.exp(ref[0:1, :segment] - top) for ref in stats)
    own = out_ref.shape[0]
    shift = as_column(top)[:own]
    log_total = as_column(jnp.log(total))[:own]
    at = 0
    for ref in guided_refs:
        out_ref[:, at : at + ref.shape[1]] = ref[:own] - shift - log_total
        at += ref.shape[1]


def shifted(value, axis, by):
    size = lax.axis_size(axis)
    return lax.ppermute(value, axis, [(i, (i + by) % size) for i in range(size)])


def chunk_starts(vocab):
    each = -(-vocab // (3 * TILE)) * TILE
    return list(range(0, vocab, each))


def per_device(final_hidden, positions, norm_gain, unembedding):
    bf16, f32 = jnp.bfloat16, jnp.float32
    _, block, width_local = final_hidden.shape
    masked = positions.shape[0]
    vocab = unembedding.shape[1]
    n_z, n_x, n_c = lax.axis_size("vocab"), lax.axis_size("rows"), lax.axis_size("cfg")
    z, x, c = lax.axis_index("vocab"), lax.axis_index("rows"), lax.axis_index("cfg")
    own = masked // (n_x * n_c)
    segment = -(-(own + 1) // 16) * 16

    normed, squares = call(
        squares_kernel,
        [((2, block, width_local), bf16), ((2, block), f32)],
        [],
        far=[final_hidden, norm_gain[None, :]],
        scratch_shapes=[
            pltpu.VMEM((2, block, width_local), bf16),
            pltpu.VMEM((1, width_local), f32),
            pltpu.SemaphoreType.DMA((3,)),
        ],
    )
    for axis in ("cfg", "rows"):
        squares = sum([shifted(squares, axis, s) for s in range(1, lax.axis_size(axis))], squares)
    (block_rows,) = call(
        functools.partial(combine_kernel, width_local * n_x * n_c),
        [((block, width_local), bf16)],
        [normed, squares],
    )

    arrivals, offsets = [block_rows], [0]
    ahead = behind = block_rows
    for step in range(1, n_z // 2 + 1):
        ahead = shifted(ahead, "vocab", 1)
        arrivals.append(ahead)
        offsets.append(step)
        if step == 1:
            first_arrival = ahead
        if 2 * step < n_z:
            behind = shifted(behind, "vocab", -1)
            arrivals.append(behind)
            offsets.append(-step)

    starts = chunk_starts(vocab)
    sizes = [end - start for start, end in zip(starts, starts[1:] + [vocab])]
    weights, positions, first_arrival = lax.optimization_barrier((unembedding.T, positions, first_arrival))
    chunks = call(
        load_kernel,
        [((size, width_local), bf16) for size in sizes],
        [],
        far=[weights],
        limit=2,
        cost=(0, 2 * vocab * width_local),
        scratch_shapes=[pltpu.SemaphoreType.DMA((len(sizes),))],
    )

    by_owner = positions.reshape(n_x, n_c, own)
    by_owner = jnp.take(by_owner, (x + jnp.arange(n_x)) % n_x, axis=0)
    by_owner = jnp.take(by_owner, (c + jnp.arange(n_c)) % n_c, axis=1)
    wanted = jnp.transpose(by_owner, (1, 0, 2)).reshape(n_x * n_c, own)
    wanted = jnp.pad(wanted, ((0, 0), (0, segment - own)), constant_values=-1).reshape(-1)
    arrived = (z - jnp.array(offsets)) % n_z
    held = (arrived[:, None] * block + jnp.arange(block)[None, :]).reshape(-1)
    chooser = (wanted[:, None] == held[None, :]).astype(bf16)

    half = n_x * segment
    parts = []
    for j, size in enumerate(sizes):
        outs = [((half, size), f32)] * 2
        cost = (4 * half * width_local * size, 2 * width_local * size)
        if j == 0:
            rows, keep, send = call(
                first_kernel,
                [((n_x * n_c * segment, width_local), bf16)] + outs,
                [chooser, chunks[0], *arrivals],
                cost=cost,
            )
        else:
            keep, send = call(later_kernel, outs, [rows, chunks[j]], cost=cost)
        got = shifted(send, "cfg", 1)
        own_sum, *sends = call(
            functools.partial(add_kernel, own),
            [((segment, size), f32)] + [((segment, size), jnp.int16)] * (n_x - 1),
            [keep, got],
        )
        parts += [own_sum] + [shifted(s_rows, "rows", s) for s, s_rows in enumerate(sends, 1)]
    *guided, stats = call(
        functools.partial(stats_kernel, len(starts), own),
        [((segment, size), f32) for size in sizes] + [((8, 128), f32)],
        parts,
    )
    all_stats = [stats] + [shifted(stats, "vocab", s) for s in range(1, n_z)]
    return pl.pallas_call(
        functools.partial(final_kernel, len(starts), segment),
        out_shape=jax.ShapeDtypeStruct((own, vocab), f32),
        in_specs=in_vmem(len(guided) + n_z),
        out_specs=pl.BlockSpec(memory_space=pltpu.VMEM),
        compiler_params=pltpu.CompilerParams(vmem_limit_bytes=16 * MIB),
    )(*keep_in_vmem(*guided, *all_stats))


def solution(mesh):
    placed = (
        P(None, ("groups", "vocab"), ("rows", "cfg")),
        P("groups"),
        P(("rows", "cfg")),
        P(("rows", "cfg"), "vocab"),
    )
    return jax.shard_map(
        per_device,
        mesh=mesh,
        in_specs=placed,
        out_specs=P(("groups", "rows", "cfg"), "vocab"),
        check_vma=False,
    )
```

time: 152 us -> 60.6 us (0.40); the launches traced: 150 us -> 60.4 us
  blocking collectives: 52.5 us -> 0 us
  waiting for transfers between devices: 51.1 us -> 22.6 us
  Pallas kernels: 0 us -> 17.2 us
  matrix products: 16.4 us -> 0 us
  starting transfers between devices: 1.31 us -> 17.3 us
  between operations: 14.6 us -> 0.13 us
  local copies, waits for them, and re-layouts: 8.49 us -> 2.08 us
  other arithmetic: 5.21 us -> 1.05 us
    all_gather x1 -> x0, waiting for transfers between devices: 50.3 us -> none  [per_device(): block_rows = lax.all_gather(final_hidden, 'vocab', axis=1, tiled=True)]
    unnamed x2 -> x0, blocking collectives: 45.6 us -> none
    ppermute x0 -> x14, waiting for transfers between devices: none -> 22.6 us  [shifted(): lax.ppermute(value, axis, [(i, (i + by) % size) for i in range(size)])]
    ppermute x0 -> x14, starting transfers between devices: none -> 17.3 us  [shifted(): lax.ppermute(value, axis, [(i, (i + by) % size) for i in range(size)])]
    pallas_call x0 -> x11, Pallas kernels: none -> 17.2 us  [the longest x10 16.1 us: call(): pl.pallas_call(body, out_shape=[pltpu.VMEM(shape, dtype) for shape, dtype...]
    dot_general x2 -> x0, matrix products: 16.4 us -> none  [the longest x1 14.1 us: per_device(): jnp.dot(normed.reshape(2 * (lax.axis_size(('rows', 'cfg')) * own_rows), w...]
    unnamed x12 -> x0, local copies, waits for them, and re-layouts: 8.17 us -> none
    psum x1 -> x0, blocking collectives: 6.84 us -> none  [per_device(): totals = lax.psum(squares, ('rows', 'cfg'))]
  transfers between devices with their start and end apart: 2 -> 14, of which waited for: 1 -> 6; matrix products, arithmetic and copies ran while one was open for 1% -> 5% of each run, Pallas kernels for 0% -> 19%
where the time goes in v1:
time: 60.6 us; the launch traced here: 60.4 us
  waiting for transfers between devices  22.6 us (37%)
  starting transfers between devices  17.3 us (29%)
  Pallas kernels  17.2 us (28%)
  local copies, waits for them, and re-layouts  2.08 us (3%)
  other arithmetic  1.05 us (2%)
    ppermute x14, waiting for transfers between devices, shifted(): lax.ppermute(value, axis, [(i, (i + by) % size) for i in range(size)])  22.6 us
    ppermute x14, starting transfers between devices, shifted(): lax.ppermute(value, axis, [(i, (i + by) % size) for i in range(size)])  17.3 us
    pallas_call x10, Pallas kernels, call(): pl.pallas_call(body, out_shape=[pltpu.VMEM(shape, dtype) for shape, dtype...  16.1 us
  transfers between devices with their start and end apart: 14, of which 6 were waited for; matrix products, arithmetic and copies ran while one was open for 5% of the time, Pallas kernels for 19%

profile of v1, /device:TPU:0, one launch (start us, length us, event | category | flops | bytes accessed | tf_op | source)
XLA Modules:
  0.0 60.4 jit_solution(13035968130109124512)
XLA Ops:
  0.0 1.3 %shard_map.55 = (bf16[2,64,2048]{2,1,0:T(8,128)(2,1)S(1)}, f32[2,64]{1,0:T(2,128)S(1)}) custom-call(bf16[2,64,2048]{2,1,0:T(8,128)(2,1)} %hidden_far.1, f32[1,2048]{1,0:T(1,128)} %bitcast.8), custom_call_target="tpu_custom_call" | custom-call | tf_op jit(solution)/shard_map/pallas_call | solution.py:26
  1.4 0.5 collective-permute-start
  1.9 0.7 %fusion.1 = s32[4]{0:T(128)S(1)} fusion(s32[4]{0:T(128)} %constant.83, s32[]{:T(128)S(6)} %axis_index.38), kind=kLoop, calls=%fused_computation.30 | loop fusion | flops 52 | bytes 36 | tf_op jit(solution)/shard_map/mul | solution.py:244
  2.6 0.1 iota_add_fusion
  2.6 0.0 collective-permute-done
  2.7 2.8 %collective-permute-start.1 = (f32[2,64]{1,0:T(2,128)S(1)}, f32[2,64]{1,0:T(2,128)S(1)}, u32[]{:S(2)}, u32[]{:S(2)}) collective-permute-start(f32[2,64]{1,0:T(2,128)S(1)} %add.142), channel_id=1, source_target_pairs={{0,2},{2,0},{1,3},{3,1},{4,6},{6,4},{5,7},{7,5},{8,10},{10,8},{9,1... | collective-permute-start | bytes 1544 | tf_op jit(solution)/shard_map/ppermute | solution.py:175
  5.5 1.5 %collective-permute-done.1 = f32[2,64]{1,0:T(2,128)S(1)} collective-permute-done((f32[2,64]{1,0:T(2,128)S(1)}, f32[2,64]{1,0:T(2,128)S(1)}, u32[]{:S(2)}, u32[]{:S(2)}) %collective-permute-start.1) | collective-permute-done | bytes 544 | tf_op jit(solution)/shard_map/ppermute | solution.py:175
  7.1 0.2 shard_map.56.refs_0_
  7.2 2.2 %collective-permute-start.2 = (bf16[64,2048]{1,0:T(8,128)(2,1)S(1)}, bf16[64,2048]{1,0:T(8,128)(2,1)S(1)}, u32[]{:S(2)}, u32[]{:S(2)}) collective-permute-start(bf16[64,2048]{1,0:T(8,128)(2,1)S(1)} %shard_map.56.refs_0_), channel_id=1, source_target_pairs={{0,4},{4,8},{8,12},{12,0},{1,5},{5,9},{9,13},{13,1},{2,6},{6,10},{... | collective-permute-start | bytes 786440 | tf_op jit(solution)/shard_map/ppermute | solution.py:175
  9.4 0.1 add.156
  9.5 2.1 %collective-permute-start.3 = (bf16[64,2048]{1,0:T(8,128)(2,1)S(1)}, bf16[64,2048]{1,0:T(8,128)(2,1)S(1)}, u32[]{:S(2)}, u32[]{:S(2)}) collective-permute-start(bf16[64,2048]{1,0:T(8,128)(2,1)S(1)} %shard_map.56.refs_0_), channel_id=1, source_target_pairs={{0,12},{4,0},{8,4},{12,8},{1,13},{5,1},{9,5},{13,9},{2,14},{6,2},{... | collective-permute-start | bytes 786440 | tf_op jit(solution)/shard_map/ppermute | solution.py:175
  11.6 7.1 %collective-permute-done.2.refs_1_ = bf16[64,2048]{1,0:T(8,128)(2,1)S(1)} collective-permute-done((bf16[64,2048]{1,0:T(8,128)(2,1)S(1)}, bf16[64,2048]{1,0:T(8,128)(2,1)S(1)}, u32[]{:S(2)}, u32[]{:S(2)}) %collective-permute-start.2) | collective-permute-done | bytes 262176 | tf_op jit(solution)/shard_map/ppermute | solution.py:175
  18.7 0.8 %reshape.131 = s32[2,2,44]{2,1,0:T(2,128)S(1)} reshape(s32[176]{0:T(256)} %param.6) | data formatting | bytes 1408 | tf_op jit(solution)/shard_map/reshape | solution.py:238
  19.5 0.6 gather_fusion
  20.0 0.1 broadcast_select_fusion.1
  20.1 0.6 gather_fusion.1
  20.7 0.0 collective-permute-start.4
  20.7 0.1 broadcast_select_fusion
  20.8 0.1 eq.20
  20.9 6.6 %shard_map.57 = (bf16[1792,2048]{1,0:T(8,128)(2,1)S(1)}, bf16[1792,2048]{1,0:T(8,128)(2,1)S(1)}, bf16[1168,2048]{1,0:T(8,128)(2,1)S(1)}) custom-call(bf16[4752,2048]{1,0:T(8,128)(2,1)} %bitcast.7), custom_call_target="tpu_custom_call" | custom-call | bytes 19464192 | tf_op jit(solution)/shard_map/pallas_call | solution.py:26
  27.5 0.1 compare_convert_fusion.chooser_ref
  27.6 0.0 collective-permute-done.3.refs_2_
  27.6 1.4 %collective-permute-done.4.refs_3_ = bf16[64,2048]{1,0:T(8,128)(2,1)S(1)} collective-permute-done((bf16[64,2048]{1,0:T(8,128)(2,1)S(1)}, bf16[64,2048]{1,0:T(8,128)(2,1)S(1)}, u32[]{:S(2)}, u32[]{:S(2)}) %collective-permute-start.4) | collective-permute-done | bytes 262176 | tf_op jit(solution)/shard_map/ppermute | solution.py:175
  28.9 2.8 %shard_map.58 = (bf16[192,2048]{1,0:T(8,128)(2,1)S(1)}, f32[96,1792]{1,0:T(8,128)S(1)}, f32[96,1792]{1,0:T(8,128)S(1)}) custom-call(bf16[192,256]{1,0:T(8,128)(2,1)S(1)} %compare_convert_fusion.chooser_ref, bf16[1792,2048]{1,0:T(8,128)(2,1)S(1)} %get-tuple-element.33.weights_ref, bf16[64,2048]{1,0:T(8,128)(2,1)S(1)} %shard_map.56.refs_0_, ...), custom_call_target="tpu_custom_call" | custom-call | flops 1409286144 | bytes 7340032 | tf_op jit(solution)/shard_map/pallas_call | solution.py:26
  31.7 0.1 collective-permute-start.5
  31.8 2.6 %shard_map.60 = (f32[96,1792]{1,0:T(8,128)S(1)}, f32[96,1792]{1,0:T(8,128)S(1)}) custom-call(bf16[192,2048]{1,0:T(8,128)(2,1)S(1)} %get-tuple-element.38.rows_ref, bf16[1792,2048]{1,0:T(8,128)(2,1)S(1)} %get-tuple-element.39.weights_ref), custom_call_target="tpu_custom_call" | custom-call | flops 1409286144 | bytes 7340032 | tf_op jit(solution)/shard_map/pallas_call | solution.py:26
  34.4 0.6 collective-permute-start.7
  34.9 1.7 %shard_map.62 = (f32[96,1168]{1,0:T(8,128)S(1)}, f32[96,1168]{1,0:T(8,128)S(1)}) custom-call(bf16[192,2048]{1,0:T(8,128)(2,1)S(1)} %get-tuple-element.38.rows_ref, bf16[1168,2048]{1,0:T(8,128)(2,1)S(1)} %get-tuple-element.44.weights_ref), custom_call_target="tpu_custom_call" | custom-call | flops 918552576 | bytes 4784128 | tf_op jit(solution)/shard_map/pallas_call | solution.py:26
  36.6 0.1 collective-permute-start.9
  36.7 0.0 collective-permute-done.5.got_ref
  36.7 0.2 shard_map.59
  36.9 1.7 %collective-permute-start.6 = (s16[48,1792]{1,0:T(8,128)(2,1)S(1)}, s16[48,1792]{1,0:T(8,128)(2,1)S(1)}, u32[]{:S(2)}, u32[]{:S(2)}) collective-permute-start(s16[48,1792]{1,0:T(8,128)(2,1)S(1)} %get-tuple-element.37), channel_id=1, source_target_pairs={{0,2},{2,0},{1,3},{3,1},{4,6},{6,4},{5,7},{7,5},{8,10},{10,8},{9,1... | collective-permute-start | bytes 516104 | tf_op jit(solution)/shard_map/ppermute | solution.py:175
  38.6 0.0 collective-permute-done.7.got_ref
  38.6 0.2 shard_map.61
  38.8 0.5 collective-permute-start.8
  39.3 0.0 collective-permute-done.9.got_ref
  39.3 0.2 shard_map.63
  39.4 1.7 %collective-permute-start.10 = (s16[48,1168]{1,0:T(8,128)(2,1)S(1)}, s16[48,1168]{1,0:T(8,128)(2,1)S(1)}, u32[]{:S(2)}, u32[]{:S(2)}) collective-permute-start(s16[48,1168]{1,0:T(8,128)(2,1)S(1)} %get-tuple-element.48), channel_id=1, source_target_pairs={{0,2},{2,0},{1,3},{3,1},{4,6},{6,4},{5,7},{7,5},{8,10},{10,8},{9,1... | collective-permute-start | bytes 336392 | tf_op jit(solution)/shard_map/ppermute | solution.py:175
  41.1 8.9 %collective-permute-done.10.refs_5_ = s16[48,1168]{1,0:T(8,128)(2,1)S(1)} collective-permute-done((s16[48,1168]{1,0:T(8,128)(2,1)S(1)}, s16[48,1168]{1,0:T(8,128)(2,1)S(1)}, u32[]{:S(2)}, u32[]{:S(2)}) %collective-permute-start.10) | collective-permute-done | bytes 112160 | tf_op jit(solution)/shard_map/ppermute | solution.py:175
  50.0 0.0 collective-permute-done.6.refs_1_
  50.1 0.0 collective-permute-done.8.refs_3_
  50.1 0.4 shard_map.64
  50.5 2.5 %collective-permute-start.13 = (f32[8,128]{1,0:T(8,128)S(1)}, f32[8,128]{1,0:T(8,128)S(1)}, u32[]{:S(2)}, u32[]{:S(2)}) collective-permute-start(f32[8,128]{1,0:T(8,128)S(1)} %get-tuple-element.52.refs_3_), channel_id=1, source_target_pairs={{0,12},{4,0},{8,4},{12,8},{1,13},{5,1},{9,5},{13,9},{2,14},{6,2},{... | collective-permute-start | bytes 12296 | tf_op jit(solution)/shard_map/ppermute | solution.py:175
  53.0 0.9 %collective-permute-start.12 = (f32[8,128]{1,0:T(8,128)S(1)}, f32[8,128]{1,0:T(8,128)S(1)}, u32[]{:S(2)}, u32[]{:S(2)}) collective-permute-start(f32[8,128]{1,0:T(8,128)S(1)} %get-tuple-element.52.refs_3_), channel_id=1, source_target_pairs={{0,8},{4,12},{8,0},{12,4},{1,9},{5,13},{9,1},{13,5},{2,10},{6,14},... | collective-permute-start | bytes 12296 | tf_op jit(solution)/shard_map/ppermute | solution.py:175
  53.9 1.7 %collective-permute-start.11 = (f32[8,128]{1,0:T(8,128)S(1)}, f32[8,128]{1,0:T(8,128)S(1)}, u32[]{:S(2)}, u32[]{:S(2)}) collective-permute-start(f32[8,128]{1,0:T(8,128)S(1)} %get-tuple-element.52.refs_3_), channel_id=1, source_target_pairs={{0,4},{4,8},{8,12},{12,0},{1,5},{5,9},{9,13},{13,1},{2,6},{6,10},{... | collective-permute-start | bytes 12296 | tf_op jit(solution)/shard_map/ppermute | solution.py:175
  55.6 0.0 collective-permute-done.13.refs_6_
  55.6 1.9 %collective-permute-done.12.refs_5_ = f32[8,128]{1,0:T(8,128)S(1)} collective-permute-done((f32[8,128]{1,0:T(8,128)S(1)}, f32[8,128]{1,0:T(8,128)S(1)}, u32[]{:S(2)}, u32[]{:S(2)}) %collective-permute-start.12) | collective-permute-done | bytes 4128 | tf_op jit(solution)/shard_map/ppermute | solution.py:175
  57.6 1.8 %collective-permute-done.11.refs_4_ = f32[8,128]{1,0:T(8,128)S(1)} collective-permute-done((f32[8,128]{1,0:T(8,128)S(1)}, f32[8,128]{1,0:T(8,128)S(1)}, u32[]{:S(2)}, u32[]{:S(2)}) %collective-permute-start.11) | collective-permute-done | bytes 4128 | tf_op jit(solution)/shard_map/ppermute | solution.py:175
  59.3 1.1 %shard_map.65 = f32[44,4752]{1,0:T(8,128)} custom-call(f32[48,1792]{1,0:T(8,128)S(1)} %get-tuple-element.49.refs_0_, f32[48,1792]{1,0:T(8,128)S(1)} %get-tuple-element.50.refs_1_, f32[48,1168]{1,0:T(8,128)S(1)} %get-tuple-element.51.refs_2_, f32[8,128]{1,0:T(8,128)S(1)} %get-tuple-element.52.refs_3_, f32[8,128]{1,0:T(8,128)S(1)} %collective-permute-done.11.refs_4_, ...), custom_call_target="tpu_custom_call" | custom-call | tf_op jit(solution)/shard_map/pallas_call | solution.py:274
  (10 shorter events, 0.1 us)
Async XLA Ops:
  1.4 1.3 %collective-permute-start = (f32[2,64]{1,0:T(2,128)S(1)}, f32[2,64]{1,0:T(2,128)S(1)}, u32[]{:S(2)}, u32[]{:S(2)}) collective-permute-start(f32[2,64]{1,0:T(2,128)S(1)} %get-tuple-element.30), channel_id=1, source_target_pairs={{0,1},{1,0},{2,3},{3,2},{4,5},{5,4},{6,7},{7,6},{8,9},{9,8},{10,11... | collective-permute-start | bytes 1544 | tf_op jit(solution)/shard_map/ppermute | solution.py:175
  2.7 4.4 %collective-permute-start.1 = (f32[2,64]{1,0:T(2,128)S(1)}, f32[2,64]{1,0:T(2,128)S(1)}, u32[]{:S(2)}, u32[]{:S(2)}) collective-permute-start(f32[2,64]{1,0:T(2,128)S(1)} %add.142), channel_id=1, source_target_pairs={{0,2},{2,0},{1,3},{3,1},{4,6},{6,4},{5,7},{7,5},{8,10},{10,8},{9,1... | collective-permute-start | bytes 1544 | tf_op jit(solution)/shard_map/ppermute | solution.py:175
  7.2 11.5 %collective-permute-start.2 = (bf16[64,2048]{1,0:T(8,128)(2,1)S(1)}, bf16[64,2048]{1,0:T(8,128)(2,1)S(1)}, u32[]{:S(2)}, u32[]{:S(2)}) collective-permute-start(bf16[64,2048]{1,0:T(8,128)(2,1)S(1)} %shard_map.56.refs_0_), channel_id=1, source_target_pairs={{0,4},{4,8},{8,12},{12,0},{1,5},{5,9},{9,13},{13,1},{2,6},{6,10},{... | collective-permute-start | bytes 786440 | tf_op jit(solution)/shard_map/ppermute | solution.py:175
  9.5 18.1 %collective-permute-start.3 = (bf16[64,2048]{1,0:T(8,128)(2,1)S(1)}, bf16[64,2048]{1,0:T(8,128)(2,1)S(1)}, u32[]{:S(2)}, u32[]{:S(2)}) collective-permute-start(bf16[64,2048]{1,0:T(8,128)(2,1)S(1)} %shard_map.56.refs_0_), channel_id=1, source_target_pairs={{0,12},{4,0},{8,4},{12,8},{1,13},{5,1},{9,5},{13,9},{2,14},{6,2},{... | collective-permute-start | bytes 786440 | tf_op jit(solution)/shard_map/ppermute | solution.py:175
  20.7 8.3 %collective-permute-start.4 = (bf16[64,2048]{1,0:T(8,128)(2,1)S(1)}, bf16[64,2048]{1,0:T(8,128)(2,1)S(1)}, u32[]{:S(2)}, u32[]{:S(2)}) collective-permute-start(bf16[64,2048]{1,0:T(8,128)(2,1)S(1)} %collective-permute-done.2.refs_1_), channel_id=1, source_target_pairs={{0,4},{4,8},{8,12},{12,0},{1,5},{5,9},{9,13},{13,1},{2,6},{6,10},{... | collective-permute-start | bytes 786440 | tf_op jit(solution)/shard_map/ppermute | solution.py:175
  31.7 5.0 %collective-permute-start.5 = (f32[96,1792]{1,0:T(8,128)S(1)}, f32[96,1792]{1,0:T(8,128)S(1)}, u32[]{:S(2)}, u32[]{:S(2)}) collective-permute-start(f32[96,1792]{1,0:T(8,128)S(1)} %get-tuple-element.35), channel_id=1, source_target_pairs={{0,1},{1,0},{2,3},{3,2},{4,5},{5,4},{6,7},{7,6},{8,9},{9,8},{10,11... | collective-permute-start | bytes 2064392 | tf_op jit(solution)/shard_map/ppermute | solution.py:175
  34.4 4.2 %collective-permute-start.7 = (f32[96,1792]{1,0:T(8,128)S(1)}, f32[96,1792]{1,0:T(8,128)S(1)}, u32[]{:S(2)}, u32[]{:S(2)}) collective-permute-start(f32[96,1792]{1,0:T(8,128)S(1)} %get-tuple-element.41), channel_id=1, source_target_pairs={{0,1},{1,0},{2,3},{3,2},{4,5},{5,4},{6,7},{7,6},{8,9},{9,8},{10,11... | collective-permute-start | bytes 2064392 | tf_op jit(solution)/shard_map/ppermute | solution.py:175
  36.6 2.7 %collective-permute-start.9 = (f32[96,1168]{1,0:T(8,128)S(1)}, f32[96,1168]{1,0:T(8,128)S(1)}, u32[]{:S(2)}, u32[]{:S(2)}) collective-permute-start(f32[96,1168]{1,0:T(8,128)S(1)} %get-tuple-element.46), channel_id=1, source_target_pairs={{0,1},{1,0},{2,3},{3,2},{4,5},{5,4},{6,7},{7,6},{8,9},{9,8},{10,11... | collective-permute-start | bytes 1345544 | tf_op jit(solution)/shard_map/ppermute | solution.py:175
  36.9 13.2 %collective-permute-start.6 = (s16[48,1792]{1,0:T(8,128)(2,1)S(1)}, s16[48,1792]{1,0:T(8,128)(2,1)S(1)}, u32[]{:S(2)}, u32[]{:S(2)}) collective-permute-start(s16[48,1792]{1,0:T(8,128)(2,1)S(1)} %get-tuple-element.37), channel_id=1, source_target_pairs={{0,2},{2,0},{1,3},{3,1},{4,6},{6,4},{5,7},{7,5},{8,10},{10,8},{9,1... | collective-permute-start | bytes 516104 | tf_op jit(solution)/shard_map/ppermute | solution.py:175
  38.8 11.2 %collective-permute-start.8 = (s16[48,1792]{1,0:T(8,128)(2,1)S(1)}, s16[48,1792]{1,0:T(8,128)(2,1)S(1)}, u32[]{:S(2)}, u32[]{:S(2)}) collective-permute-start(s16[48,1792]{1,0:T(8,128)(2,1)S(1)} %get-tuple-element.43), channel_id=1, source_target_pairs={{0,2},{2,0},{1,3},{3,1},{4,6},{6,4},{5,7},{7,5},{8,10},{10,8},{9,1... | collective-permute-start | bytes 516104 | tf_op jit(solution)/shard_map/ppermute | solution.py:175
  39.4 10.6 %collective-permute-start.10 = (s16[48,1168]{1,0:T(8,128)(2,1)S(1)}, s16[48,1168]{1,0:T(8,128)(2,1)S(1)}, u32[]{:S(2)}, u32[]{:S(2)}) collective-permute-start(s16[48,1168]{1,0:T(8,128)(2,1)S(1)} %get-tuple-element.48), channel_id=1, source_target_pairs={{0,2},{2,0},{1,3},{3,1},{4,6},{6,4},{5,7},{7,5},{8,10},{10,8},{9,1... | collective-permute-start | bytes 336392 | tf_op jit(solution)/shard_map/ppermute | solution.py:175
  50.5 5.1 %collective-permute-start.13 = (f32[8,128]{1,0:T(8,128)S(1)}, f32[8,128]{1,0:T(8,128)S(1)}, u32[]{:S(2)}, u32[]{:S(2)}) collective-permute-start(f32[8,128]{1,0:T(8,128)S(1)} %get-tuple-element.52.refs_3_), channel_id=1, source_target_pairs={{0,12},{4,0},{8,4},{12,8},{1,13},{5,1},{9,5},{13,9},{2,14},{6,2},{... | collective-permute-start | bytes 12296 | tf_op jit(solution)/shard_map/ppermute | solution.py:175
  53.0 4.5 %collective-permute-start.12 = (f32[8,128]{1,0:T(8,128)S(1)}, f32[8,128]{1,0:T(8,128)S(1)}, u32[]{:S(2)}, u32[]{:S(2)}) collective-permute-start(f32[8,128]{1,0:T(8,128)S(1)} %get-tuple-element.52.refs_3_), channel_id=1, source_target_pairs={{0,8},{4,12},{8,0},{12,4},{1,9},{5,13},{9,1},{13,5},{2,10},{6,14},... | collective-permute-start | bytes 12296 | tf_op jit(solution)/shard_map/ppermute | solution.py:175
  53.9 5.4 %collective-permute-start.11 = (f32[8,128]{1,0:T(8,128)S(1)}, f32[8,128]{1,0:T(8,128)S(1)}, u32[]{:S(2)}, u32[]{:S(2)}) collective-permute-start(f32[8,128]{1,0:T(8,128)S(1)} %get-tuple-element.52.refs_3_), channel_id=1, source_target_pairs={{0,4},{4,8},{8,12},{12,0},{1,5},{5,9},{9,13},{13,1},{2,6},{6,10},{... | collective-permute-start | bytes 12296 | tf_op jit(solution)/shard_map/ppermute | solution.py:175

commit v2 on v1

--- a/solution.py
+++ b/solution.py
@@ -74,28 +74,54 @@
         out_ref[...] = (terms[0] - terms[1]).astype(jnp.bfloat16)
 
 
-def load_kernel(weights_far, *refs):
-    *chunk_refs, sems = refs
-    copies, start = [], 0
-    for j, ref in enumerate(chunk_refs):
-        size = ref.shape[0]
-        copies.append(pltpu.make_async_copy(weights_far.at[pl.ds(start, size)], ref, sems.at[j]))
-        start += size
-    for copy in copies:
+def load_kernel(start, weights_far, *refs):
+    *_, out_ref, tiles_ref, sems = refs
+    size, slots = out_ref.shape[1], tiles_ref.shape[0]
+    tiles = [(at, min(TILE, size - at)) for at in range(0, size, TILE)]
+    copies = [
+        pltpu.make_async_copy(
+            weights_far.at[pl.ds(start + at, rows)],
+            tiles_ref.at[i % slots, pl.ds(0, rows)],
+            sems.at[i % slots],
+        )
+        for i, (at, rows) in enumerate(tiles)
+    ]
+    for copy in copies[:slots]:
         copy.start()
-    for copy in copies:
-        copy.wait()
+    for i, (at, rows) in enumerate(tiles):
+        copies[i].wait()
+        out_ref[:, at : at + rows] = tiles_ref[i % slots, :rows].T
+        if i + slots < len(tiles):
+            copies[i + slots].start()
+
+
+def chooser_kernel(own, offsets, n_z, n_x, n_c, block, positions_ref, out_ref):
+    z, x, c = (lax.axis_index(axis) for axis in ("vocab", "rows", "cfg"))
+    masked = positions_ref.shape[1]
+    segment = out_ref.shape[0] // (n_x * n_c)
+    places = (positions_ref[...] + 1).astype(jnp.float32)
+    i = lax.broadcasted_iota(jnp.int32, (segment, masked), 0)
+    rank = lax.broadcasted_iota(jnp.int32, (segment, masked), 1)
+    lane = lax.broadcasted_iota(jnp.int32, (segment, out_ref.shape[1]), 1)
+    held = lane
+    for k, offset in enumerate(offsets):
+        moved = lane + (lax.rem(z - offset + n_z, n_z) - k) * block
+        held = jnp.where(lane >= k * block, moved, held)
+    for t in range(n_c):
+        for s in range(n_x):
+            owner = lax.rem(x + s, n_x) * n_c + lax.rem(c + t, n_c)
+            match = (rank == owner * own + i) & (i < own)
+            wanted = jnp.sum(jnp.where(match, places, 0.0), axis=1, keepdims=True).astype(jnp.int32) - 1
+            at = (t * n_x + s) * segment
+            out_ref[at : at + segment] = (wanted == held).astype(jnp.float32).astype(jnp.bfloat16)
 
 
 def multiply(rows_ref, weights_ref, keep_ref, send_ref):
     half, width = keep_ref.shape
     for at in range(0, width, TILE):
         size = min(TILE, width - at)
-        product = lax.dot_general(
-            rows_ref[...],
-            weights_ref[at : at + size, :],
-            (((1,), (1,)), ((), ())),
-            preferred_element_type=jnp.float32,
+        product = jnp.dot(
+            rows_ref[...], weights_ref[:, at : at + size], preferred_element_type=jnp.float32
         )
         keep_ref[:, at : at + size] = product[:half]
         send_ref[:, at : at + size] = product[half:]
@@ -209,43 +235,54 @@
         [normed, squares],
     )
 
+    starts = chunk_starts(vocab)
+    sizes = [end - start for start, end in zip(starts, starts[1:] + [vocab])]
+    weights = unembedding.T
+    chunks = []
+
+    def load(after):
+        nonlocal weights
+        if len(chunks) == len(sizes):
+            return after
+        start, size = starts[len(chunks)], sizes[len(chunks)]
+        weights, after = lax.optimization_barrier((weights, after))
+        (chunk,) = call(
+            functools.partial(load_kernel, start),
+            [((width_local, size), bf16)],
+            [],
+            far=[weights],
+            cost=(0, 2 * size * width_local),
+            scratch_shapes=[pltpu.VMEM((3, TILE, width_local), bf16), pltpu.SemaphoreType.DMA((3,))],
+        )
+        chunk, after = lax.optimization_barrier((chunk, after))
+        chunks.append(chunk)
+        return after
+
     arrivals, offsets = [block_rows], [0]
-    ahead = behind = block_rows
+    ahead = shifted(block_rows, "vocab", 1)
+    behind = load(block_rows)
     for step in range(1, n_z // 2 + 1):
-        ahead = shifted(ahead, "vocab", 1)
+        if step > 1:
+            ahead = shifted(ahead, "vocab", 1)
         arrivals.append(ahead)
         offsets.append(step)
-        if step == 1:
-            first_arrival = ahead
         if 2 * step < n_z:
             behind = shifted(behind, "vocab", -1)
             arrivals.append(behind)
             offsets.append(-step)
-
-    starts = chunk_starts(vocab)
-    sizes = [end - start for start, end in zip(starts, starts[1:] + [vocab])]
-    weights, positions, first_arrival = lax.optimization_barrier((unembedding.T, positions, first_arrival))
-    chunks = call(
-        load_kernel,
-        [((size, width_local), bf16) for size in sizes],
-        [],
-        far=[weights],
-        limit=2,
-        cost=(0, 2 * vocab * width_local),
-        scratch_shapes=[pltpu.SemaphoreType.DMA((len(sizes),))],
-    )
-
-    by_owner = positions.reshape(n_x, n_c, own)
-    by_owner = jnp.take(by_owner, (x + jnp.arange(n_x)) % n_x, axis=0)
-    by_owner = jnp.take(by_owner, (c + jnp.arange(n_c)) % n_c, axis=1)
-    wanted = jnp.transpose(by_owner, (1, 0, 2)).reshape(n_x * n_c, own)
-    wanted = jnp.pad(wanted, ((0, 0), (0, segment - own)), constant_values=-1).reshape(-1)
-    arrived = (z - jnp.array(offsets)) % n_z
-    held = (arrived[:, None] * block + jnp.arange(block)[None, :]).reshape(-1)
-    chooser = (wanted[:, None] == held[None, :]).astype(bf16)
+        if step == 1:
+            chunks[-1], ahead = lax.optimization_barrier((chunks[-1], ahead))
+    while len(chunks) < len(sizes):
+        load(arrivals[1])
+    (chooser,) = call(
+        functools.partial(chooser_kernel, own, offsets, n_z, n_x, n_c, block),
+        [((n_x * n_c * segment, n_z * block), bf16)],
+        [lax.optimization_barrier((positions[None, :], chunks[0]))[0]],
+    )
+    chooser, *chunks = lax.optimization_barrier((chooser, *chunks))
 
     half = n_x * segment
-    parts = []
+    parts, leaving = [], []
     for j, size in enumerate(sizes):
         outs = [((half, size), f32)] * 2
         cost = (4 * half * width_local * size, 2 * width_local * size)
@@ -257,6 +294,8 @@
                 cost=cost,
             )
         else:
+            if j > 1:
+                rows, leaving[j - 2] = lax.optimization_barrier((rows, leaving[j - 2]))
             keep, send = call(later_kernel, outs, [rows, chunks[j]], cost=cost)
         got = shifted(send, "cfg", 1)
         own_sum, *sends = call(
@@ -264,7 +303,10 @@
             [((segment, size), f32)] + [((segment, size), jnp.int16)] * (n_x - 1),
             [keep, got],
         )
-        parts += [own_sum] + [shifted(s_rows, "rows", s) for s, s_rows in enumerate(sends, 1)]
+        parts.append(own_sum)
+        leaving.append(sends)
+    arrived = [[shifted(s_rows, "rows", s) for s, s_rows in enumerate(sends, 1)] for sends in leaving]
+    parts = [part for own_sum, got in zip(parts, arrived) for part in (own_sum, *got)]
     *guided, stats = call(
         functools.partial(stats_kernel, len(starts), own),
         [((segment, size), f32) for size in sizes] + [((8, 128), f32)],

time: 60.6 us -> 56.9 us (0.939)
  Pallas kernels: 17.2 us -> 21.7 us
  waiting for transfers between devices: 22.6 us -> 19.9 us
  starting transfers between devices: 17.3 us -> 14.9 us
  local copies, waits for them, and re-layouts: 2.08 us -> 0.01 us
  other arithmetic: 1.05 us -> 0.01 us
    pallas_call x10 -> x13, Pallas kernels: 16.1 us -> 20.6 us  [call(): pl.pallas_call(body, out_shape=[pltpu.VMEM(shape, dtype) for shape, dtype...]
    ppermute x14, waiting for transfers between devices: 22.6 us -> 19.9 us  [shifted(): lax.ppermute(value, axis, [(i, (i + by) % size) for i in range(size)])]
    ppermute x14, starting transfers between devices: 17.3 us -> 14.9 us  [shifted(): lax.ppermute(value, axis, [(i, (i + by) % size) for i in range(size)])]
    gather x2 -> x0, local copies, waits for them, and re-layouts: 1.14 us -> none  [the longest x1 0.57 us: per_device(): by_owner = jnp.take(by_owner, (c + jnp.arange(n_c)) % n_c, axis=1)]
    reshape x1 -> x0, local copies, waits for them, and re-layouts: 0.76 us -> none  [per_device(): by_owner = positions.reshape(n_x, n_c, own)]
    mul x1 -> x0, other arithmetic: 0.67 us -> none  [per_device(): held = (arrived[:, None] * block + jnp.arange(block)[None, :]).reshape(-1)]
  transfers between devices with their start and end apart: 14 -> 14, of which waited for: 6 -> 10; matrix products, arithmetic and copies ran while one was open for 5% -> 0% of each run, Pallas kernels for 19% -> 29%
where the time goes in v2:
time: 56.9 us; the launch traced here: 56.7 us
  Pallas kernels  21.7 us (38%)
  waiting for transfers between devices  19.9 us (35%)
  starting transfers between devices  14.9 us (26%)
    pallas_call x13, Pallas kernels, call(): pl.pallas_call(body, out_shape=[pltpu.VMEM(shape, dtype) for shape, dtype...  20.6 us
    ppermute x14, waiting for transfers between devices, shifted(): lax.ppermute(value, axis, [(i, (i + by) % size) for i in range(size)])  19.9 us
    ppermute x14, starting transfers between devices, shifted(): lax.ppermute(value, axis, [(i, (i + by) % size) for i in range(size)])  14.9 us
  transfers between devices with their start and end apart: 14, of which 10 were waited for; matrix products, arithmetic and copies ran while one was open for 0% of the time, Pallas kernels for 29%

profile of v2, /device:TPU:0, one launch (start us, length us, event | category | flops | bytes accessed | tf_op | source)
XLA Modules:
  0.0 56.7 jit_solution(891771150703416141)
XLA Ops:
  0.0 1.3 %shard_map.46 = (bf16[2,64,2048]{2,1,0:T(8,128)(2,1)S(1)}, f32[2,64]{1,0:T(2,128)S(1)}) custom-call(bf16[2,64,2048]{2,1,0:T(8,128)(2,1)} %hidden_far.1, f32[1,2048]{1,0:T(1,128)} %bitcast.7), custom_call_target="tpu_custom_call" | custom-call | tf_op jit(solution)/shard_map/pallas_call | solution.py:26
  1.4 0.5 collective-permute-start
  1.9 0.8 %collective-permute-done = f32[2,64]{1,0:T(2,128)S(1)} collective-permute-done((f32[2,64]{1,0:T(2,128)S(1)}, f32[2,64]{1,0:T(2,128)S(1)}, u32[]{:S(2)}, u32[]{:S(2)}) %collective-permute-start) | collective-permute-done | bytes 544 | tf_op jit(solution)/shard_map/ppermute | solution.py:201
  2.7 2.8 %collective-permute-start.1 = (f32[2,64]{1,0:T(2,128)S(1)}, f32[2,64]{1,0:T(2,128)S(1)}, u32[]{:S(2)}, u32[]{:S(2)}) collective-permute-start(f32[2,64]{1,0:T(2,128)S(1)} %add.6), channel_id=1, source_target_pairs={{0,2},{2,0},{1,3},{3,1},{4,6},{6,4},{5,7},{7,5},{8,10},{10,8},{9,1... | collective-permute-start | bytes 1544 | tf_op jit(solution)/shard_map/ppermute | solution.py:201
  5.5 1.5 %collective-permute-done.1 = f32[2,64]{1,0:T(2,128)S(1)} collective-permute-done((f32[2,64]{1,0:T(2,128)S(1)}, f32[2,64]{1,0:T(2,128)S(1)}, u32[]{:S(2)}, u32[]{:S(2)}) %collective-permute-start.1) | collective-permute-done | bytes 544 | tf_op jit(solution)/shard_map/ppermute | solution.py:201
  7.1 0.2 shard_map.47.refs_0_
  7.2 2.2 %collective-permute-start.2 = (bf16[64,2048]{1,0:T(8,128)(2,1)S(1)}, bf16[64,2048]{1,0:T(8,128)(2,1)S(1)}, u32[]{:S(2)}, u32[]{:S(2)}) collective-permute-start(bf16[64,2048]{1,0:T(8,128)(2,1)S(1)} %shard_map.47.refs_0_), channel_id=1, source_target_pairs={{0,4},{4,8},{8,12},{12,0},{1,5},{5,9},{9,13},{13,1},{2,6},{6,10},{... | collective-permute-start | bytes 786440 | tf_op jit(solution)/shard_map/ppermute | solution.py:201
  9.4 4.7 %shard_map.48.weights_ref = bf16[2048,1792]{1,0:T(8,128)(2,1)S(1)} custom-call(bf16[4752,2048]{1,0:T(8,128)(2,1)} %bitcast.4), custom_call_target="tpu_custom_call" | custom-call | bytes 7340032 | tf_op jit(solution)/shard_map/pallas_call | solution.py:26
  14.1 2.1 %collective-permute-start.3 = (bf16[64,2048]{1,0:T(8,128)(2,1)S(1)}, bf16[64,2048]{1,0:T(8,128)(2,1)S(1)}, u32[]{:S(2)}, u32[]{:S(2)}) collective-permute-start(bf16[64,2048]{1,0:T(8,128)(2,1)S(1)} %shard_map.47.refs_0_), channel_id=1, source_target_pairs={{0,12},{4,0},{8,4},{12,8},{1,13},{5,1},{9,5},{13,9},{2,14},{6,2},{... | collective-permute-start | bytes 786440 | tf_op jit(solution)/shard_map/ppermute | solution.py:201
  16.2 0.8 %collective-permute-done.2.refs_1_ = bf16[64,2048]{1,0:T(8,128)(2,1)S(1)} collective-permute-done((bf16[64,2048]{1,0:T(8,128)(2,1)S(1)}, bf16[64,2048]{1,0:T(8,128)(2,1)S(1)}, u32[]{:S(2)}, u32[]{:S(2)}) %collective-permute-start.2) | collective-permute-done | bytes 262176 | tf_op jit(solution)/shard_map/ppermute | solution.py:201
  17.0 0.0 collective-permute-start.4
  17.0 4.7 %shard_map.50.weights_ref = bf16[2048,1792]{1,0:T(8,128)(2,1)S(1)} custom-call(bf16[4752,2048]{1,0:T(8,128)(2,1)} %bitcast.5), custom_call_target="tpu_custom_call" | custom-call | bytes 7340032 | tf_op jit(solution)/shard_map/pallas_call | solution.py:26
  21.8 0.0 copy-start
  21.8 3.5 %shard_map.51.weights_ref = bf16[2048,1168]{1,0:T(8,128)(2,1)S(1)} custom-call(bf16[4752,2048]{1,0:T(8,128)(2,1)} %bitcast.6), custom_call_target="tpu_custom_call" | custom-call | bytes 4784128 | tf_op jit(solution)/shard_map/pallas_call | solution.py:26
  25.3 0.0 copy-done
  25.3 0.1 shard_map.49.chooser_ref
  25.4 0.0 collective-permute-done.3.refs_2_
  25.4 3.4 %collective-permute-done.4.refs_3_ = bf16[64,2048]{1,0:T(8,128)(2,1)S(1)} collective-permute-done((bf16[64,2048]{1,0:T(8,128)(2,1)S(1)}, bf16[64,2048]{1,0:T(8,128)(2,1)S(1)}, u32[]{:S(2)}, u32[]{:S(2)}) %collective-permute-start.4) | collective-permute-done | bytes 262176 | tf_op jit(solution)/shard_map/ppermute | solution.py:201
  28.8 2.0 %shard_map.52 = (bf16[192,2048]{1,0:T(8,128)(2,1)S(1)}, f32[96,1792]{1,0:T(8,128)S(1)}, f32[96,1792]{1,0:T(8,128)S(1)}) custom-call(bf16[192,256]{1,0:T(8,128)(2,1)S(1)} %shard_map.49.chooser_ref, bf16[2048,1792]{1,0:T(8,128)(2,1)S(1)} %shard_map.48.weights_ref, bf16[64,2048]{1,0:T(8,128)(2,1)S(1)} %shard_map.47.refs_0_, ...), custom_call_target="tpu_custom_call" | custom-call | flops 1409286144 | bytes 7340032 | tf_op jit(solution)/shard_map/pallas_call | solution.py:26
  30.8 0.1 collective-permute-start.5
  30.9 1.7 %shard_map.54 = (f32[96,1792]{1,0:T(8,128)S(1)}, f32[96,1792]{1,0:T(8,128)S(1)}) custom-call(bf16[192,2048]{1,0:T(8,128)(2,1)S(1)} %get-tuple-element.63.rows_ref, bf16[2048,1792]{1,0:T(8,128)(2,1)S(1)} %shard_map.50.weights_ref), custom_call_target="tpu_custom_call" | custom-call | flops 1409286144 | bytes 7340032 | tf_op jit(solution)/shard_map/pallas_call | solution.py:26
  32.6 0.6 collective-permute-start.7
  33.2 0.0 collective-permute-done.5.got_ref
  33.2 0.2 shard_map.53
  33.4 1.3 %shard_map.56 = (f32[96,1168]{1,0:T(8,128)S(1)}, f32[96,1168]{1,0:T(8,128)S(1)}) custom-call(bf16[192,2048]{1,0:T(8,128)(2,1)S(1)} %get-tuple-element.63.rows_ref, bf16[2048,1168]{1,0:T(8,128)(2,1)S(1)} %shard_map.51.weights_ref), custom_call_target="tpu_custom_call" | custom-call | flops 918552576 | bytes 4784128 | tf_op jit(solution)/shard_map/pallas_call | solution.py:26
  34.7 0.1 collective-permute-start.9
  34.8 1.6 %collective-permute-start.6 = (s16[48,1792]{1,0:T(8,128)(2,1)S(1)}, s16[48,1792]{1,0:T(8,128)(2,1)S(1)}, u32[]{:S(2)}, u32[]{:S(2)}) collective-permute-start(s16[48,1792]{1,0:T(8,128)(2,1)S(1)} %get-tuple-element.57), channel_id=1, source_target_pairs={{0,2},{2,0},{1,3},{3,1},{4,6},{6,4},{5,7},{7,5},{8,10},{10,8},{9,1... | collective-permute-start | bytes 516104 | tf_op jit(solution)/shard_map/ppermute | solution.py:201
  36.3 0.0 collective-permute-done.7.got_ref
  36.3 0.2 shard_map.55
  36.5 0.6 %collective-permute-start.8 = (s16[48,1792]{1,0:T(8,128)(2,1)S(1)}, s16[48,1792]{1,0:T(8,128)(2,1)S(1)}, u32[]{:S(2)}, u32[]{:S(2)}) collective-permute-start(s16[48,1792]{1,0:T(8,128)(2,1)S(1)} %get-tuple-element.62), channel_id=1, source_target_pairs={{0,2},{2,0},{1,3},{3,1},{4,6},{6,4},{5,7},{7,5},{8,10},{10,8},{9,1... | collective-permute-start | bytes 516104 | tf_op jit(solution)/shard_map/ppermute | solution.py:201
  37.1 0.0 collective-permute-done.9.got_ref
  37.1 0.2 shard_map.57
  37.3 1.6 %collective-permute-start.10 = (s16[48,1168]{1,0:T(8,128)(2,1)S(1)}, s16[48,1168]{1,0:T(8,128)(2,1)S(1)}, u32[]{:S(2)}, u32[]{:S(2)}) collective-permute-start(s16[48,1168]{1,0:T(8,128)(2,1)S(1)} %get-tuple-element.68), channel_id=1, source_target_pairs={{0,2},{2,0},{1,3},{3,1},{4,6},{6,4},{5,7},{7,5},{8,10},{10,8},{9,1... | collective-permute-start | bytes 336392 | tf_op jit(solution)/shard_map/ppermute | solution.py:201
  38.9 3.1 %collective-permute-done.6.refs_1_ = s16[48,1792]{1,0:T(8,128)(2,1)S(1)} collective-permute-done((s16[48,1792]{1,0:T(8,128)(2,1)S(1)}, s16[48,1792]{1,0:T(8,128)(2,1)S(1)}, u32[]{:S(2)}, u32[]{:S(2)}) %collective-permute-start.6) | collective-permute-done | bytes 172064 | tf_op jit(solution)/shard_map/ppermute | solution.py:201
  42.0 3.7 %collective-permute-done.8.refs_3_ = s16[48,1792]{1,0:T(8,128)(2,1)S(1)} collective-permute-done((s16[48,1792]{1,0:T(8,128)(2,1)S(1)}, s16[48,1792]{1,0:T(8,128)(2,1)S(1)}, u32[]{:S(2)}, u32[]{:S(2)}) %collective-permute-start.8) | collective-permute-done | bytes 172064 | tf_op jit(solution)/shard_map/ppermute | solution.py:201
  45.7 2.2 %collective-permute-done.10.refs_5_ = s16[48,1168]{1,0:T(8,128)(2,1)S(1)} collective-permute-done((s16[48,1168]{1,0:T(8,128)(2,1)S(1)}, s16[48,1168]{1,0:T(8,128)(2,1)S(1)}, u32[]{:S(2)}, u32[]{:S(2)}) %collective-permute-start.10) | collective-permute-done | bytes 112160 | tf_op jit(solution)/shard_map/ppermute | solution.py:201
  47.9 0.4 shard_map.58
  48.3 1.9 %collective-permute-start.13 = (f32[8,128]{1,0:T(8,128)S(1)}, f32[8,128]{1,0:T(8,128)S(1)}, u32[]{:S(2)}, u32[]{:S(2)}) collective-permute-start(f32[8,128]{1,0:T(8,128)S(1)} %get-tuple-element.72.refs_3_), channel_id=1, source_target_pairs={{0,12},{4,0},{8,4},{12,8},{1,13},{5,1},{9,5},{13,9},{2,14},{6,2},{... | collective-permute-start | bytes 12296 | tf_op jit(solution)/shard_map/ppermute | solution.py:201
  50.2 0.0 collective-permute-start.12
  50.2 1.0 %collective-permute-start.11 = (f32[8,128]{1,0:T(8,128)S(1)}, f32[8,128]{1,0:T(8,128)S(1)}, u32[]{:S(2)}, u32[]{:S(2)}) collective-permute-start(f32[8,128]{1,0:T(8,128)S(1)} %get-tuple-element.72.refs_3_), channel_id=1, source_target_pairs={{0,4},{4,8},{8,12},{12,0},{1,5},{5,9},{9,13},{13,1},{2,6},{6,10},{... | collective-permute-start | bytes 12296 | tf_op jit(solution)/shard_map/ppermute | solution.py:201
  51.2 0.7 %collective-permute-done.13.refs_6_ = f32[8,128]{1,0:T(8,128)S(1)} collective-permute-done((f32[8,128]{1,0:T(8,128)S(1)}, f32[8,128]{1,0:T(8,128)S(1)}, u32[]{:S(2)}, u32[]{:S(2)}) %collective-permute-start.13) | collective-permute-done | bytes 4128 | tf_op jit(solution)/shard_map/ppermute | solution.py:201
  52.0 2.7 %collective-permute-done.12.refs_5_ = f32[8,128]{1,0:T(8,128)S(1)} collective-permute-done((f32[8,128]{1,0:T(8,128)S(1)}, f32[8,128]{1,0:T(8,128)S(1)}, u32[]{:S(2)}, u32[]{:S(2)}) %collective-permute-start.12) | collective-permute-done | bytes 4128 | tf_op jit(solution)/shard_map/ppermute | solution.py:201
  54.7 0.9 %collective-permute-done.11.refs_4_ = f32[8,128]{1,0:T(8,128)S(1)} collective-permute-done((f32[8,128]{1,0:T(8,128)S(1)}, f32[8,128]{1,0:T(8,128)S(1)}, u32[]{:S(2)}, u32[]{:S(2)}) %collective-permute-start.11) | collective-permute-done | bytes 4128 | tf_op jit(solution)/shard_map/ppermute | solution.py:201
  55.6 1.1 %shard_map.59 = f32[44,4752]{1,0:T(8,128)} custom-call(f32[48,1792]{1,0:T(8,128)S(1)} %get-tuple-element.69.refs_0_, f32[48,1792]{1,0:T(8,128)S(1)} %get-tuple-element.70.refs_1_, f32[48,1168]{1,0:T(8,128)S(1)} %get-tuple-element.71.refs_2_, f32[8,128]{1,0:T(8,128)S(1)} %get-tuple-element.72.refs_3_, f32[8,128]{1,0:T(8,128)S(1)} %collective-permute-done.11.refs_4_, ...), custom_call_target="tpu_custom_call" | custom-call | tf_op jit(solution)/shard_map/pallas_call | solution.py:316
  (2 shorter events, 0.0 us)
Async XLA Ops:
  1.4 1.3 %collective-permute-start = (f32[2,64]{1,0:T(2,128)S(1)}, f32[2,64]{1,0:T(2,128)S(1)}, u32[]{:S(2)}, u32[]{:S(2)}) collective-permute-start(f32[2,64]{1,0:T(2,128)S(1)} %get-tuple-element.40), channel_id=1, source_target_pairs={{0,1},{1,0},{2,3},{3,2},{4,5},{5,4},{6,7},{7,6},{8,9},{9,8},{10,11... | collective-permute-start | bytes 1544 | tf_op jit(solution)/shard_map/ppermute | solution.py:201
  2.7 4.4 %collective-permute-start.1 = (f32[2,64]{1,0:T(2,128)S(1)}, f32[2,64]{1,0:T(2,128)S(1)}, u32[]{:S(2)}, u32[]{:S(2)}) collective-permute-start(f32[2,64]{1,0:T(2,128)S(1)} %add.6), channel_id=1, source_target_pairs={{0,2},{2,0},{1,3},{3,1},{4,6},{6,4},{5,7},{7,5},{8,10},{10,8},{9,1... | collective-permute-start | bytes 1544 | tf_op jit(solution)/shard_map/ppermute | solution.py:201
  7.2 9.8 %collective-permute-start.2 = (bf16[64,2048]{1,0:T(8,128)(2,1)S(1)}, bf16[64,2048]{1,0:T(8,128)(2,1)S(1)}, u32[]{:S(2)}, u32[]{:S(2)}) collective-permute-start(bf16[64,2048]{1,0:T(8,128)(2,1)S(1)} %shard_map.47.refs_0_), channel_id=1, source_target_pairs={{0,4},{4,8},{8,12},{12,0},{1,5},{5,9},{9,13},{13,1},{2,6},{6,10},{... | collective-permute-start | bytes 786440 | tf_op jit(solution)/shard_map/ppermute | solution.py:201
  14.1 11.3 %collective-permute-start.3 = (bf16[64,2048]{1,0:T(8,128)(2,1)S(1)}, bf16[64,2048]{1,0:T(8,128)(2,1)S(1)}, u32[]{:S(2)}, u32[]{:S(2)}) collective-permute-start(bf16[64,2048]{1,0:T(8,128)(2,1)S(1)} %shard_map.47.refs_0_), channel_id=1, source_target_pairs={{0,12},{4,0},{8,4},{12,8},{1,13},{5,1},{9,5},{13,9},{2,14},{6,2},{... | collective-permute-start | bytes 786440 | tf_op jit(solution)/shard_map/ppermute | solution.py:201
  17.0 11.7 %collective-permute-start.4 = (bf16[64,2048]{1,0:T(8,128)(2,1)S(1)}, bf16[64,2048]{1,0:T(8,128)(2,1)S(1)}, u32[]{:S(2)}, u32[]{:S(2)}) collective-permute-start(bf16[64,2048]{1,0:T(8,128)(2,1)S(1)} %collective-permute-done.2.refs_1_), channel_id=1, source_target_pairs={{0,4},{4,8},{8,12},{12,0},{1,5},{5,9},{9,13},{13,1},{2,6},{6,10},{... | collective-permute-start | bytes 786440 | tf_op jit(solution)/shard_map/ppermute | solution.py:201
  21.8 3.5 %copy-start = (s32[176]{0:T(256)S(1)}, s32[176]{0:T(256)}, u32[]{:S(2)}) copy-start(s32[176]{0:T(256)} %param.5) | copy-start | bytes 2116
  30.8 2.3 %collective-permute-start.5 = (f32[96,1792]{1,0:T(8,128)S(1)}, f32[96,1792]{1,0:T(8,128)S(1)}, u32[]{:S(2)}, u32[]{:S(2)}) collective-permute-start(f32[96,1792]{1,0:T(8,128)S(1)} %get-tuple-element.53), channel_id=1, source_target_pairs={{0,1},{1,0},{2,3},{3,2},{4,5},{5,4},{6,7},{7,6},{8,9},{9,8},{10,11... | collective-permute-start | bytes 2064392 | tf_op jit(solution)/shard_map/ppermute | solution.py:201
  32.6 3.7 %collective-permute-start.7 = (f32[96,1792]{1,0:T(8,128)S(1)}, f32[96,1792]{1,0:T(8,128)S(1)}, u32[]{:S(2)}, u32[]{:S(2)}) collective-permute-start(f32[96,1792]{1,0:T(8,128)S(1)} %get-tuple-element.60), channel_id=1, source_target_pairs={{0,1},{1,0},{2,3},{3,2},{4,5},{5,4},{6,7},{7,6},{8,9},{9,8},{10,11... | collective-permute-start | bytes 2064392 | tf_op jit(solution)/shard_map/ppermute | solution.py:201
  34.7 2.5 %collective-permute-start.9 = (f32[96,1168]{1,0:T(8,128)S(1)}, f32[96,1168]{1,0:T(8,128)S(1)}, u32[]{:S(2)}, u32[]{:S(2)}) collective-permute-start(f32[96,1168]{1,0:T(8,128)S(1)} %get-tuple-element.66), channel_id=1, source_target_pairs={{0,1},{1,0},{2,3},{3,2},{4,5},{5,4},{6,7},{7,6},{8,9},{9,8},{10,11... | collective-permute-start | bytes 1345544 | tf_op jit(solution)/shard_map/ppermute | solution.py:201
  34.8 7.2 %collective-permute-start.6 = (s16[48,1792]{1,0:T(8,128)(2,1)S(1)}, s16[48,1792]{1,0:T(8,128)(2,1)S(1)}, u32[]{:S(2)}, u32[]{:S(2)}) collective-permute-start(s16[48,1792]{1,0:T(8,128)(2,1)S(1)} %get-tuple-element.57), channel_id=1, source_target_pairs={{0,2},{2,0},{1,3},{3,1},{4,6},{6,4},{5,7},{7,5},{8,10},{10,8},{9,1... | collective-permute-start | bytes 516104 | tf_op jit(solution)/shard_map/ppermute | solution.py:201
  36.5 9.1 %collective-permute-start.8 = (s16[48,1792]{1,0:T(8,128)(2,1)S(1)}, s16[48,1792]{1,0:T(8,128)(2,1)S(1)}, u32[]{:S(2)}, u32[]{:S(2)}) collective-permute-start(s16[48,1792]{1,0:T(8,128)(2,1)S(1)} %get-tuple-element.62), channel_id=1, source_target_pairs={{0,2},{2,0},{1,3},{3,1},{4,6},{6,4},{5,7},{7,5},{8,10},{10,8},{9,1... | collective-permute-start | bytes 516104 | tf_op jit(solution)/shard_map/ppermute | solution.py:201
  37.3 10.5 %collective-permute-start.10 = (s16[48,1168]{1,0:T(8,128)(2,1)S(1)}, s16[48,1168]{1,0:T(8,128)(2,1)S(1)}, u32[]{:S(2)}, u32[]{:S(2)}) collective-permute-start(s16[48,1168]{1,0:T(8,128)(2,1)S(1)} %get-tuple-element.68), channel_id=1, source_target_pairs={{0,2},{2,0},{1,3},{3,1},{4,6},{6,4},{5,7},{7,5},{8,10},{10,8},{9,1... | collective-permute-start | bytes 336392 | tf_op jit(solution)/shard_map/ppermute | solution.py:201
  48.3 3.7 %collective-permute-start.13 = (f32[8,128]{1,0:T(8,128)S(1)}, f32[8,128]{1,0:T(8,128)S(1)}, u32[]{:S(2)}, u32[]{:S(2)}) collective-permute-start(f32[8,128]{1,0:T(8,128)S(1)} %get-tuple-element.72.refs_3_), channel_id=1, source_target_pairs={{0,12},{4,0},{8,4},{12,8},{1,13},{5,1},{9,5},{13,9},{2,14},{6,2},{... | collective-permute-start | bytes 12296 | tf_op jit(solution)/shard_map/ppermute | solution.py:201
  50.2 4.5 %collective-permute-start.12 = (f32[8,128]{1,0:T(8,128)S(1)}, f32[8,128]{1,0:T(8,128)S(1)}, u32[]{:S(2)}, u32[]{:S(2)}) collective-permute-start(f32[8,128]{1,0:T(8,128)S(1)} %get-tuple-element.72.refs_3_), channel_id=1, source_target_pairs={{0,8},{4,12},{8,0},{12,4},{1,9},{5,13},{9,1},{13,5},{2,10},{6,14},... | collective-permute-start | bytes 12296 | tf_op jit(solution)/shard_map/ppermute | solution.py:201
  50.2 5.4 %collective-permute-start.11 = (f32[8,128]{1,0:T(8,128)S(1)}, f32[8,128]{1,0:T(8,128)S(1)}, u32[]{:S(2)}, u32[]{:S(2)}) collective-permute-start(f32[8,128]{1,0:T(8,128)S(1)} %get-tuple-element.72.refs_3_), channel_id=1, source_target_pairs={{0,4},{4,8},{8,12},{12,0},{1,5},{5,9},{9,13},{13,1},{2,6},{6,10},{... | collective-permute-start | bytes 12296 | tf_op jit(solution)/shard_map/ppermute | solution.py:201

commit v3 on v2

--- a/solution.py
+++ b/solution.py
@@ -12,6 +12,10 @@
 TILE = 256
 LANES = 128
 MIB = 1 << 20
+LOADS = (5, 3, 5)
+LOADS_BEHIND = 1
+LOADS_AHEAD = 1
+CHUNKS = (10,)
 
 
 def in_vmem(count):
@@ -116,26 +120,30 @@
             out_ref[at : at + segment] = (wanted == held).astype(jnp.float32).astype(jnp.bfloat16)
 
 
-def multiply(rows_ref, weights_ref, keep_ref, send_ref):
+def multiply(start, rows_ref, weights_refs, keep_ref, send_ref):
     half, width = keep_ref.shape
-    for at in range(0, width, TILE):
-        size = min(TILE, width - at)
-        product = jnp.dot(
-            rows_ref[...], weights_ref[:, at : at + size], preferred_element_type=jnp.float32
-        )
-        keep_ref[:, at : at + size] = product[:half]
-        send_ref[:, at : at + size] = product[half:]
-
-
-def first_kernel(chooser_ref, weights_ref, *refs):
-    *block_refs, rows_ref, keep_ref, send_ref = refs
+    at, skip = 0, start
+    for ref in weights_refs:
+        held = ref.shape[1]
+        while at < width and skip < held:
+            size = min(TILE, width - at, held - skip)
+            product = jnp.dot(rows_ref[...], ref[:, skip : skip + size], preferred_element_type=jnp.float32)
+            keep_ref[:, at : at + size] = product[:half]
+            send_ref[:, at : at + size] = product[half:]
+            at, skip = at + size, skip + size
+        skip = max(0, skip - held)
+
+
+def first_kernel(start, loads, chooser_ref, *refs):
+    weights_refs, block_refs, (rows_ref, keep_ref, send_ref) = refs[:loads], refs[loads:-3], refs[-3:]
     blocks = jnp.concatenate([ref[...] for ref in block_refs], axis=0)
     rows_ref[...] = jnp.dot(chooser_ref[...], blocks, preferred_element_type=jnp.float32).astype(jnp.bfloat16)
-    multiply(rows_ref, weights_ref, keep_ref, send_ref)
-
-
-def later_kernel(rows_ref, weights_ref, keep_ref, send_ref):
-    multiply(rows_ref, weights_ref, keep_ref, send_ref)
+    multiply(start, rows_ref, weights_refs, keep_ref, send_ref)
+
+
+def later_kernel(start, rows_ref, *refs):
+    *weights_refs, keep_ref, send_ref = refs
+    multiply(start, rows_ref, weights_refs, keep_ref, send_ref)
 
 
 def lanes_diagonal(n):
@@ -166,19 +174,21 @@
     return value * jnp.exp2(exponent - 15.0)
 
 
-def stats_kernel(chunks, own, *refs):
-    ins, guided_refs, out_ref = refs[: -chunks - 1], refs[-chunks - 1 : -1], refs[-1]
-    each = len(ins) // chunks
-    top = None
-    for j in range(chunks):
-        guided = ins[j * each][...]
-        for got in ins[j * each + 1 : (j + 1) * each]:
-            guided = guided + restored(own, got)
-        guided_refs[j][...] = guided
-        peak = jnp.max(guided, axis=1, keepdims=True)
-        top = peak if top is None else jnp.maximum(top, peak)
-    total = sum(jnp.sum(jnp.exp(ref[...] - top), axis=1, keepdims=True) for ref in guided_refs)
-    segment = top.shape[0]
+def stats_kernel(own, *refs):
+    *in_refs, guided_ref, out_ref = refs
+    before = in_refs.pop(0) if in_refs[0].shape == out_ref.shape else None
+    guided = in_refs[0][...]
+    for got in in_refs[1:]:
+        guided = guided + restored(own, got)
+    guided_ref[...] = guided
+    segment = guided.shape[0]
+    top = jnp.max(guided, axis=1, keepdims=True)
+    if before is not None:
+        earlier = as_column(before[0:1, :segment])
+        top = jnp.maximum(top, earlier)
+    total = jnp.sum(jnp.exp(guided - top), axis=1, keepdims=True)
+    if before is not None:
+        total = total + as_column(before[1:2, :segment]) * jnp.exp(earlier - top)
     out_ref[0:1, :segment] = as_row(top)
     out_ref[1:2, :segment] = as_row(total)
 
@@ -201,9 +211,12 @@
     return lax.ppermute(value, axis, [(i, (i + by) % size) for i in range(size)])
 
 
-def chunk_starts(vocab):
-    each = -(-vocab // (3 * TILE)) * TILE
-    return list(range(0, vocab, each))
+def cut(vocab, tiles):
+    edges = [0]
+    for count in tiles:
+        edges.append(min(vocab, edges[-1] + count * TILE))
+    edges.append(vocab)
+    return [(start, end - start) for start, end in zip(edges, edges[1:]) if end > start]
 
 
 def per_device(final_hidden, positions, norm_gain, unembedding):
@@ -235,68 +248,66 @@
         [normed, squares],
     )
 
-    starts = chunk_starts(vocab)
-    sizes = [end - start for start, end in zip(starts, starts[1:] + [vocab])]
     weights = unembedding.T
-    chunks = []
-
-    def load(after):
+    loads, loaded = cut(vocab, LOADS), []
+
+    def load(count, after):
         nonlocal weights
-        if len(chunks) == len(sizes):
-            return after
-        start, size = starts[len(chunks)], sizes[len(chunks)]
-        weights, after = lax.optimization_barrier((weights, after))
-        (chunk,) = call(
-            functools.partial(load_kernel, start),
-            [((width_local, size), bf16)],
-            [],
-            far=[weights],
-            cost=(0, 2 * size * width_local),
-            scratch_shapes=[pltpu.VMEM((3, TILE, width_local), bf16), pltpu.SemaphoreType.DMA((3,))],
-        )
-        chunk, after = lax.optimization_barrier((chunk, after))
-        chunks.append(chunk)
+        for start, size in loads[len(loaded) : len(loaded) + count]:
+            weights, after = lax.optimization_barrier((weights, after))
+            (piece,) = call(
+                functools.partial(load_kernel, start),
+                [((width_local, size), bf16)],
+                [],
+                far=[weights],
+                cost=(0, 2 * size * width_local),
+                scratch_shapes=[pltpu.VMEM((3, TILE, width_local), bf16), pltpu.SemaphoreType.DMA((3,))],
+            )
+            piece, after = lax.optimization_barrier((piece, after))
+            loaded.append(piece)
         return after
 
-    arrivals, offsets = [block_rows], [0]
     ahead = shifted(block_rows, "vocab", 1)
-    behind = load(block_rows)
-    for step in range(1, n_z // 2 + 1):
-        if step > 1:
-            ahead = shifted(ahead, "vocab", 1)
+    arrivals, offsets = [block_rows, ahead], [0, 1]
+    behind = load(LOADS_BEHIND, block_rows)
+    for step in range(1, (n_z - 1) // 2 + 1):
+        behind = shifted(behind, "vocab", -1)
+        arrivals.append(behind)
+        offsets.append(-step)
+    if LOADS_AHEAD:
+        load(LOADS_AHEAD, loaded[-1] if loaded else block_rows)
+        ahead, loaded[-1] = lax.optimization_barrier((ahead, loaded[-1]))
+    load_after = ahead
+    for step in range(2, n_z // 2 + 1):
+        ahead = shifted(ahead, "vocab", 1)
         arrivals.append(ahead)
         offsets.append(step)
-        if 2 * step < n_z:
-            behind = shifted(behind, "vocab", -1)
-            arrivals.append(behind)
-            offsets.append(-step)
-        if step == 1:
-            chunks[-1], ahead = lax.optimization_barrier((chunks[-1], ahead))
-    while len(chunks) < len(sizes):
-        load(arrivals[1])
+    load(len(loads), load_after)
     (chooser,) = call(
         functools.partial(chooser_kernel, own, offsets, n_z, n_x, n_c, block),
         [((n_x * n_c * segment, n_z * block), bf16)],
-        [lax.optimization_barrier((positions[None, :], chunks[0]))[0]],
-    )
-    chooser, *chunks = lax.optimization_barrier((chooser, *chunks))
+        [lax.optimization_barrier((positions[None, :], loaded[0]))[0]],
+    )
+    chooser, *loaded = lax.optimization_barrier((chooser, *loaded))
 
     half = n_x * segment
+    chunks = cut(vocab, CHUNKS)
     parts, leaving = [], []
-    for j, size in enumerate(sizes):
+    for j, (start, size) in enumerate(chunks):
         outs = [((half, size), f32)] * 2
         cost = (4 * half * width_local * size, 2 * width_local * size)
+        needed = [i for i, (at, held) in enumerate(loads) if at < start + size and start < at + held]
+        skip = start - loads[needed[0]][0]
+        pieces = [loaded[i] for i in needed]
         if j == 0:
             rows, keep, send = call(
-                first_kernel,
+                functools.partial(first_kernel, skip, len(pieces)),
                 [((n_x * n_c * segment, width_local), bf16)] + outs,
-                [chooser, chunks[0], *arrivals],
+                [chooser, *pieces, *arrivals],
                 cost=cost,
             )
         else:
-            if j > 1:
-                rows, leaving[j - 2] = lax.optimization_barrier((rows, leaving[j - 2]))
-            keep, send = call(later_kernel, outs, [rows, chunks[j]], cost=cost)
+            keep, send = call(functools.partial(later_kernel, skip), outs, [rows, *pieces], cost=cost)
         got = shifted(send, "cfg", 1)
         own_sum, *sends = call(
             functools.partial(add_kernel, own),
@@ -305,16 +316,18 @@
         )
         parts.append(own_sum)
         leaving.append(sends)
-    arrived = [[shifted(s_rows, "rows", s) for s, s_rows in enumerate(sends, 1)] for sends in leaving]
-    parts = [part for own_sum, got in zip(parts, arrived) for part in (own_sum, *got)]
-    *guided, stats = call(
-        functools.partial(stats_kernel, len(starts), own),
-        [((segment, size), f32) for size in sizes] + [((8, 128), f32)],
-        parts,
-    )
+    guided, stats = [], None
+    for own_sum, sends in zip(parts, leaving):
+        got = [shifted(s_rows, "rows", s) for s, s_rows in enumerate(sends, 1)]
+        chunk, stats = call(
+            functools.partial(stats_kernel, own),
+            [(own_sum.shape, f32), ((8, LANES), f32)],
+            ([] if stats is None else [stats]) + [own_sum, *got],
+        )
+        guided.append(chunk)
     all_stats = [stats] + [shifted(stats, "vocab", s) for s in range(1, n_z)]
     return pl.pallas_call(
-        functools.partial(final_kernel, len(starts), segment),
+        functools.partial(final_kernel, len(chunks), segment),
         out_shape=jax.ShapeDtypeStruct((own, vocab), f32),
         in_specs=in_vmem(len(guided) + n_z),
         out_specs=pl.BlockSpec(memory_space=pltpu.VMEM),

time: 56.9 us -> 56.1 us (0.986)
  waiting for transfers between devices: 19.9 us -> 18.7 us
  starting transfers between devices: 14.9 us -> 15.8 us
    ppermute x14 -> x12, waiting for transfers between devices: 19.9 us -> 18.7 us  [shifted(): lax.ppermute(value, axis, [(i, (i + by) % size) for i in range(size)])]
    ppermute x14 -> x12, starting transfers between devices: 14.9 us -> 15.8 us  [shifted(): lax.ppermute(value, axis, [(i, (i + by) % size) for i in range(size)])]
  transfers between devices with their start and end apart: 14 -> 12, of which waited for: 10 -> 9; matrix products, arithmetic and copies ran while one was open for 0% -> 0% of each run, Pallas kernels for 29% -> 28%
where the time goes in v3:
time: 56.1 us; the launch traced here: 55.9 us
  Pallas kernels  21.3 us (38%)
  waiting for transfers between devices  18.7 us (33%)
  starting transfers between devices  15.8 us (28%)
    pallas_call x13, Pallas kernels, call(): pl.pallas_call(body, out_shape=[pltpu.VMEM(shape, dtype) for shape, dtype...  20.2 us
    ppermute x12, waiting for transfers between devices, shifted(): lax.ppermute(value, axis, [(i, (i + by) % size) for i in range(size)])  18.7 us
    ppermute x12, starting transfers between devices, shifted(): lax.ppermute(value, axis, [(i, (i + by) % size) for i in range(size)])  15.8 us
  transfers between devices with their start and end apart: 12, of which 9 were waited for; matrix products, arithmetic and copies ran while one was open for 0% of the time, Pallas kernels for 28%

profile of v3, /device:TPU:0, one launch (start us, length us, event | category | flops | bytes accessed | tf_op | source)
XLA Modules:
  0.0 55.9 jit_solution(2417896842517275011)
XLA Ops:
  0.0 1.3 %shard_map.46 = (bf16[2,64,2048]{2,1,0:T(8,128)(2,1)S(1)}, f32[2,64]{1,0:T(2,128)S(1)}) custom-call(bf16[2,64,2048]{2,1,0:T(8,128)(2,1)} %hidden_far.1, f32[1,2048]{1,0:T(1,128)} %bitcast.8), custom_call_target="tpu_custom_call" | custom-call | tf_op jit(solution)/shard_map/pallas_call | solution.py:30
  1.4 0.5 collective-permute-start
  1.9 0.8 %collective-permute-done = f32[2,64]{1,0:T(2,128)S(1)} collective-permute-done((f32[2,64]{1,0:T(2,128)S(1)}, f32[2,64]{1,0:T(2,128)S(1)}, u32[]{:S(2)}, u32[]{:S(2)}) %collective-permute-start) | collective-permute-done | bytes 544 | tf_op jit(solution)/shard_map/ppermute | solution.py:211
  2.7 2.8 %collective-permute-start.1 = (f32[2,64]{1,0:T(2,128)S(1)}, f32[2,64]{1,0:T(2,128)S(1)}, u32[]{:S(2)}, u32[]{:S(2)}) collective-permute-start(f32[2,64]{1,0:T(2,128)S(1)} %add.6), channel_id=1, source_target_pairs={{0,2},{2,0},{1,3},{3,1},{4,6},{6,4},{5,7},{7,5},{8,10},{10,8},{9,1... | collective-permute-start | bytes 1544 | tf_op jit(solution)/shard_map/ppermute | solution.py:211
  5.5 1.5 %collective-permute-done.1 = f32[2,64]{1,0:T(2,128)S(1)} collective-permute-done((f32[2,64]{1,0:T(2,128)S(1)}, f32[2,64]{1,0:T(2,128)S(1)}, u32[]{:S(2)}, u32[]{:S(2)}) %collective-permute-start.1) | collective-permute-done | bytes 544 | tf_op jit(solution)/shard_map/ppermute | solution.py:211
  7.1 0.2 shard_map.47.refs_3_
  7.2 2.2 %collective-permute-start.2 = (bf16[64,2048]{1,0:T(8,128)(2,1)S(1)}, bf16[64,2048]{1,0:T(8,128)(2,1)S(1)}, u32[]{:S(2)}, u32[]{:S(2)}) collective-permute-start(bf16[64,2048]{1,0:T(8,128)(2,1)S(1)} %shard_map.47.refs_3_), channel_id=1, source_target_pairs={{0,4},{4,8},{8,12},{12,0},{1,5},{5,9},{9,13},{13,1},{2,6},{6,10},{... | collective-permute-start | bytes 786440 | tf_op jit(solution)/shard_map/ppermute | solution.py:211
  9.4 3.5 %shard_map.48.refs_0_ = bf16[2048,1280]{1,0:T(8,128)(2,1)S(1)} custom-call(bf16[4752,2048]{1,0:T(8,128)(2,1)} %bitcast.4), custom_call_target="tpu_custom_call" | custom-call | bytes 5242880 | tf_op jit(solution)/shard_map/pallas_call | solution.py:30
  12.9 0.0 copy-start
  12.9 2.1 %collective-permute-start.3 = (bf16[64,2048]{1,0:T(8,128)(2,1)S(1)}, bf16[64,2048]{1,0:T(8,128)(2,1)S(1)}, u32[]{:S(2)}, u32[]{:S(2)}) collective-permute-start(bf16[64,2048]{1,0:T(8,128)(2,1)S(1)} %shard_map.47.refs_3_), channel_id=1, source_target_pairs={{0,12},{4,0},{8,4},{12,8},{1,13},{5,1},{9,5},{13,9},{2,14},{6,2},{... | collective-permute-start | bytes 786440 | tf_op jit(solution)/shard_map/ppermute | solution.py:211
  15.0 2.2 %shard_map.50.refs_1_ = bf16[2048,768]{1,0:T(8,128)(2,1)S(1)} custom-call(bf16[4752,2048]{1,0:T(8,128)(2,1)} %bitcast.5), custom_call_target="tpu_custom_call" | custom-call | bytes 3145728 | tf_op jit(solution)/shard_map/pallas_call | solution.py:30
  17.2 0.3 collective-permute-done.2.refs_4_
  17.5 0.0 collective-permute-start.4
  17.5 0.0 copy-done
  17.5 0.1 shard_map.49.chooser_ref
  17.6 3.5 %shard_map.51.refs_2_.refs_0_ = bf16[2048,1280]{1,0:T(8,128)(2,1)S(1)} custom-call(bf16[4752,2048]{1,0:T(8,128)(2,1)} %bitcast.6), custom_call_target="tpu_custom_call" | custom-call | bytes 5242880 | tf_op jit(solution)/shard_map/pallas_call | solution.py:30
  21.1 3.8 %shard_map.52.refs_1_ = bf16[2048,1424]{1,0:T(8,128)(2,1)S(1)} custom-call(bf16[4752,2048]{1,0:T(8,128)(2,1)} %bitcast.7), custom_call_target="tpu_custom_call" | custom-call | bytes 5832704 | tf_op jit(solution)/shard_map/pallas_call | solution.py:30
  24.9 0.0 collective-permute-done.3.refs_5_
  24.9 3.2 %collective-permute-done.4.refs_6_ = bf16[64,2048]{1,0:T(8,128)(2,1)S(1)} collective-permute-done((bf16[64,2048]{1,0:T(8,128)(2,1)S(1)}, bf16[64,2048]{1,0:T(8,128)(2,1)S(1)}, u32[]{:S(2)}, u32[]{:S(2)}) %collective-permute-start.4) | collective-permute-done | bytes 262176 | tf_op jit(solution)/shard_map/ppermute | solution.py:211
  28.2 2.4 %shard_map.53 = (bf16[192,2048]{1,0:T(8,128)(2,1)S(1)}, f32[96,2560]{1,0:T(8,128)S(1)}, f32[96,2560]{1,0:T(8,128)S(1)}) custom-call(bf16[192,256]{1,0:T(8,128)(2,1)S(1)} %shard_map.49.chooser_ref, bf16[2048,1280]{1,0:T(8,128)(2,1)S(1)} %shard_map.48.refs_0_, bf16[2048,768]{1,0:T(8,128)(2,1)S(1)} %shard_map.50.refs_1_, ...), custom_call_target="tpu_custom_call" | custom-call | flops 2013265920 | bytes 10485760 | tf_op jit(solution)/shard_map/pallas_call | solution.py:30
  30.6 0.1 collective-permute-start.5
  30.7 2.0 %shard_map.56 = (f32[96,2192]{1,0:T(8,128)S(1)}, f32[96,2192]{1,0:T(8,128)S(1)}) custom-call(bf16[192,2048]{1,0:T(8,128)(2,1)S(1)} %get-tuple-element.55.rows_ref, bf16[2048,1280]{1,0:T(8,128)(2,1)S(1)} %shard_map.51.refs_2_.refs_0_, bf16[2048,1424]{1,0:T(8,128)(2,1)S(1)} %shard_map.52.refs_1_), custom_call_target="tpu_custom_call" | custom-call | flops 1723858944 | bytes 8978432 | tf_op jit(solution)/shard_map/pallas_call | solution.py:30
  32.7 0.6 %collective-permute-start.7 = (f32[96,2192]{1,0:T(8,128)S(1)}, f32[96,2192]{1,0:T(8,128)S(1)}, u32[]{:S(2)}, u32[]{:S(2)}) collective-permute-start(f32[96,2192]{1,0:T(8,128)S(1)} %get-tuple-element.58), channel_id=1, source_target_pairs={{0,1},{1,0},{2,3},{3,2},{4,5},{5,4},{6,7},{7,6},{8,9},{9,8},{10,11... | collective-permute-start | bytes 2525192 | tf_op jit(solution)/shard_map/ppermute | solution.py:211
  33.3 0.0 collective-permute-done.5.got_ref
  33.3 0.2 shard_map.54
  33.5 1.6 %collective-permute-start.6 = (s16[48,2560]{1,0:T(8,128)(2,1)S(1)}, s16[48,2560]{1,0:T(8,128)(2,1)S(1)}, u32[]{:S(2)}, u32[]{:S(2)}) collective-permute-start(s16[48,2560]{1,0:T(8,128)(2,1)S(1)} %get-tuple-element.52), channel_id=1, source_target_pairs={{0,2},{2,0},{1,3},{3,1},{4,6},{6,4},{5,7},{7,5},{8,10},{10,8},{9,1... | collective-permute-start | bytes 737288 | tf_op jit(solution)/shard_map/ppermute | solution.py:211
  35.1 0.2 collective-permute-done.7.got_ref
  35.3 0.2 shard_map.57
  35.5 1.6 %collective-permute-start.8 = (s16[48,2192]{1,0:T(8,128)(2,1)S(1)}, s16[48,2192]{1,0:T(8,128)(2,1)S(1)}, u32[]{:S(2)}, u32[]{:S(2)}) collective-permute-start(s16[48,2192]{1,0:T(8,128)(2,1)S(1)} %get-tuple-element.60), channel_id=1, source_target_pairs={{0,2},{2,0},{1,3},{3,1},{4,6},{6,4},{5,7},{7,5},{8,10},{10,8},{9,1... | collective-permute-start | bytes 631304 | tf_op jit(solution)/shard_map/ppermute | solution.py:211
  37.1 5.3 %collective-permute-done.6.refs_1_ = s16[48,2560]{1,0:T(8,128)(2,1)S(1)} collective-permute-done((s16[48,2560]{1,0:T(8,128)(2,1)S(1)}, s16[48,2560]{1,0:T(8,128)(2,1)S(1)}, u32[]{:S(2)}, u32[]{:S(2)}) %collective-permute-start.6) | collective-permute-done | bytes 245792 | tf_op jit(solution)/shard_map/ppermute | solution.py:211
  42.4 0.3 shard_map.55
  42.7 3.6 %collective-permute-done.8.refs_2_ = s16[48,2192]{1,0:T(8,128)(2,1)S(1)} collective-permute-done((s16[48,2192]{1,0:T(8,128)(2,1)S(1)}, s16[48,2192]{1,0:T(8,128)(2,1)S(1)}, u32[]{:S(2)}, u32[]{:S(2)}) %collective-permute-start.8) | collective-permute-done | bytes 210464 | tf_op jit(solution)/shard_map/ppermute | solution.py:211
  46.3 0.3 shard_map.58
  46.6 1.9 %collective-permute-start.11 = (f32[8,128]{1,0:T(8,128)S(1)}, f32[8,128]{1,0:T(8,128)S(1)}, u32[]{:S(2)}, u32[]{:S(2)}) collective-permute-start(f32[8,128]{1,0:T(8,128)S(1)} %get-tuple-element.62.refs_2_), channel_id=1, source_target_pairs={{0,12},{4,0},{8,4},{12,8},{1,13},{5,1},{9,5},{13,9},{2,14},{6,2},{... | collective-permute-start | bytes 12296 | tf_op jit(solution)/shard_map/ppermute | solution.py:211
  48.5 0.9 %collective-permute-start.10 = (f32[8,128]{1,0:T(8,128)S(1)}, f32[8,128]{1,0:T(8,128)S(1)}, u32[]{:S(2)}, u32[]{:S(2)}) collective-permute-start(f32[8,128]{1,0:T(8,128)S(1)} %get-tuple-element.62.refs_2_), channel_id=1, source_target_pairs={{0,8},{4,12},{8,0},{12,4},{1,9},{5,13},{9,1},{13,5},{2,10},{6,14},... | collective-permute-start | bytes 12296 | tf_op jit(solution)/shard_map/ppermute | solution.py:211
  49.4 1.7 %collective-permute-start.9 = (f32[8,128]{1,0:T(8,128)S(1)}, f32[8,128]{1,0:T(8,128)S(1)}, u32[]{:S(2)}, u32[]{:S(2)}) collective-permute-start(f32[8,128]{1,0:T(8,128)S(1)} %get-tuple-element.62.refs_2_), channel_id=1, source_target_pairs={{0,4},{4,8},{8,12},{12,0},{1,5},{5,9},{9,13},{13,1},{2,6},{6,10},{... | collective-permute-start | bytes 12296 | tf_op jit(solution)/shard_map/ppermute | solution.py:211
  51.1 0.0 collective-permute-done.11.refs_5_
  51.1 1.9 %collective-permute-done.10.refs_4_ = f32[8,128]{1,0:T(8,128)S(1)} collective-permute-done((f32[8,128]{1,0:T(8,128)S(1)}, f32[8,128]{1,0:T(8,128)S(1)}, u32[]{:S(2)}, u32[]{:S(2)}) %collective-permute-start.10) | collective-permute-done | bytes 4128 | tf_op jit(solution)/shard_map/ppermute | solution.py:211
  53.0 1.8 %collective-permute-done.9.refs_3_ = f32[8,128]{1,0:T(8,128)S(1)} collective-permute-done((f32[8,128]{1,0:T(8,128)S(1)}, f32[8,128]{1,0:T(8,128)S(1)}, u32[]{:S(2)}, u32[]{:S(2)}) %collective-permute-start.9) | collective-permute-done | bytes 4128 | tf_op jit(solution)/shard_map/ppermute | solution.py:211
  54.8 1.1 %shard_map.59 = f32[44,4752]{1,0:T(8,128)} custom-call(f32[48,2560]{1,0:T(8,128)S(1)} %get-tuple-element.53.refs_0_, f32[48,2192]{1,0:T(8,128)S(1)} %get-tuple-element.61.refs_1_, f32[8,128]{1,0:T(8,128)S(1)} %get-tuple-element.62.refs_2_, f32[8,128]{1,0:T(8,128)S(1)} %collective-permute-done.9.refs_3_, f32[8,128]{1,0:T(8,128)S(1)} %collective-permute-done.10.refs_4_, ...), custom_call_target="tpu_custom_call" | custom-call | tf_op jit(solution)/shard_map/pallas_call | solution.py:329
  (2 shorter events, 0.0 us)
Async XLA Ops:
  1.4 1.3 %collective-permute-start = (f32[2,64]{1,0:T(2,128)S(1)}, f32[2,64]{1,0:T(2,128)S(1)}, u32[]{:S(2)}, u32[]{:S(2)}) collective-permute-start(f32[2,64]{1,0:T(2,128)S(1)} %get-tuple-element.35), channel_id=1, source_target_pairs={{0,1},{1,0},{2,3},{3,2},{4,5},{5,4},{6,7},{7,6},{8,9},{9,8},{10,11... | collective-permute-start | bytes 1544 | tf_op jit(solution)/shard_map/ppermute | solution.py:211
  2.7 4.4 %collective-permute-start.1 = (f32[2,64]{1,0:T(2,128)S(1)}, f32[2,64]{1,0:T(2,128)S(1)}, u32[]{:S(2)}, u32[]{:S(2)}) collective-permute-start(f32[2,64]{1,0:T(2,128)S(1)} %add.6), channel_id=1, source_target_pairs={{0,2},{2,0},{1,3},{3,1},{4,6},{6,4},{5,7},{7,5},{8,10},{10,8},{9,1... | collective-permute-start | bytes 1544 | tf_op jit(solution)/shard_map/ppermute | solution.py:211
  7.2 10.2 %collective-permute-start.2 = (bf16[64,2048]{1,0:T(8,128)(2,1)S(1)}, bf16[64,2048]{1,0:T(8,128)(2,1)S(1)}, u32[]{:S(2)}, u32[]{:S(2)}) collective-permute-start(bf16[64,2048]{1,0:T(8,128)(2,1)S(1)} %shard_map.47.refs_3_), channel_id=1, source_target_pairs={{0,4},{4,8},{8,12},{12,0},{1,5},{5,9},{9,13},{13,1},{2,6},{6,10},{... | collective-permute-start | bytes 786440 | tf_op jit(solution)/shard_map/ppermute | solution.py:211
  12.9 4.6 %copy-start = (s32[176]{0:T(256)S(1)}, s32[176]{0:T(256)}, u32[]{:S(2)}) copy-start(s32[176]{0:T(256)} %param.5) | copy-start | bytes 2116
  12.9 12.0 %collective-permute-start.3 = (bf16[64,2048]{1,0:T(8,128)(2,1)S(1)}, bf16[64,2048]{1,0:T(8,128)(2,1)S(1)}, u32[]{:S(2)}, u32[]{:S(2)}) collective-permute-start(bf16[64,2048]{1,0:T(8,128)(2,1)S(1)} %shard_map.47.refs_3_), channel_id=1, source_target_pairs={{0,12},{4,0},{8,4},{12,8},{1,13},{5,1},{9,5},{13,9},{2,14},{6,2},{... | collective-permute-start | bytes 786440 | tf_op jit(solution)/shard_map/ppermute | solution.py:211
  17.5 10.7 %collective-permute-start.4 = (bf16[64,2048]{1,0:T(8,128)(2,1)S(1)}, bf16[64,2048]{1,0:T(8,128)(2,1)S(1)}, u32[]{:S(2)}, u32[]{:S(2)}) collective-permute-start(bf16[64,2048]{1,0:T(8,128)(2,1)S(1)} %collective-permute-done.2.refs_4_), channel_id=1, source_target_pairs={{0,4},{4,8},{8,12},{12,0},{1,5},{5,9},{9,13},{13,1},{2,6},{6,10},{... | collective-permute-start | bytes 786440 | tf_op jit(solution)/shard_map/ppermute | solution.py:211
  30.6 2.6 %collective-permute-start.5 = (f32[96,2560]{1,0:T(8,128)S(1)}, f32[96,2560]{1,0:T(8,128)S(1)}, u32[]{:S(2)}, u32[]{:S(2)}) collective-permute-start(f32[96,2560]{1,0:T(8,128)S(1)} %get-tuple-element.50), channel_id=1, source_target_pairs={{0,1},{1,0},{2,3},{3,2},{4,5},{5,4},{6,7},{7,6},{8,9},{9,8},{10,11... | collective-permute-start | bytes 2949128 | tf_op jit(solution)/shard_map/ppermute | solution.py:211
  32.7 2.6 %collective-permute-start.7 = (f32[96,2192]{1,0:T(8,128)S(1)}, f32[96,2192]{1,0:T(8,128)S(1)}, u32[]{:S(2)}, u32[]{:S(2)}) collective-permute-start(f32[96,2192]{1,0:T(8,128)S(1)} %get-tuple-element.58), channel_id=1, source_target_pairs={{0,1},{1,0},{2,3},{3,2},{4,5},{5,4},{6,7},{7,6},{8,9},{9,8},{10,11... | collective-permute-start | bytes 2525192 | tf_op jit(solution)/shard_map/ppermute | solution.py:211
  33.5 8.9 %collective-permute-start.6 = (s16[48,2560]{1,0:T(8,128)(2,1)S(1)}, s16[48,2560]{1,0:T(8,128)(2,1)S(1)}, u32[]{:S(2)}, u32[]{:S(2)}) collective-permute-start(s16[48,2560]{1,0:T(8,128)(2,1)S(1)} %get-tuple-element.52), channel_id=1, source_target_pairs={{0,2},{2,0},{1,3},{3,1},{4,6},{6,4},{5,7},{7,5},{8,10},{10,8},{9,1... | collective-permute-start | bytes 737288 | tf_op jit(solution)/shard_map/ppermute | solution.py:211
  35.5 10.8 %collective-permute-start.8 = (s16[48,2192]{1,0:T(8,128)(2,1)S(1)}, s16[48,2192]{1,0:T(8,128)(2,1)S(1)}, u32[]{:S(2)}, u32[]{:S(2)}) collective-permute-start(s16[48,2192]{1,0:T(8,128)(2,1)S(1)} %get-tuple-element.60), channel_id=1, source_target_pairs={{0,2},{2,0},{1,3},{3,1},{4,6},{6,4},{5,7},{7,5},{8,10},{10,8},{9,1... | collective-permute-start | bytes 631304 | tf_op jit(solution)/shard_map/ppermute | solution.py:211
  46.6 4.5 %collective-permute-start.11 = (f32[8,128]{1,0:T(8,128)S(1)}, f32[8,128]{1,0:T(8,128)S(1)}, u32[]{:S(2)}, u32[]{:S(2)}) collective-permute-start(f32[8,128]{1,0:T(8,128)S(1)} %get-tuple-element.62.refs_2_), channel_id=1, source_target_pairs={{0,12},{4,0},{8,4},{12,8},{1,13},{5,1},{9,5},{13,9},{2,14},{6,2},{... | collective-permute-start | bytes 12296 | tf_op jit(solution)/shard_map/ppermute | solution.py:211
  48.5 4.5 %collective-permute-start.10 = (f32[8,128]{1,0:T(8,128)S(1)}, f32[8,128]{1,0:T(8,128)S(1)}, u32[]{:S(2)}, u32[]{:S(2)}) collective-permute-start(f32[8,128]{1,0:T(8,128)S(1)} %get-tuple-element.62.refs_2_), channel_id=1, source_target_pairs={{0,8},{4,12},{8,0},{12,4},{1,9},{5,13},{9,1},{13,5},{2,10},{6,14},... | collective-permute-start | bytes 12296 | tf_op jit(solution)/shard_map/ppermute | solution.py:211
  49.4 5.4 %collective-permute-start.9 = (f32[8,128]{1,0:T(8,128)S(1)}, f32[8,128]{1,0:T(8,128)S(1)}, u32[]{:S(2)}, u32[]{:S(2)}) collective-permute-start(f32[8,128]{1,0:T(8,128)S(1)} %get-tuple-element.62.refs_2_), channel_id=1, source_target_pairs={{0,4},{4,8},{8,12},{12,0},{1,5},{5,9},{9,13},{13,1},{2,6},{6,10},{... | collective-permute-start | bytes 12296 | tf_op jit(solution)/shard_map/ppermute | solution.py:211

commit v4 on v3

--- a/solution.py
+++ b/solution.py
@@ -12,10 +12,11 @@
 TILE = 256
 LANES = 128
 MIB = 1 << 20
-LOADS = (5, 3, 5)
+LOADS = (1280, 512, 704, 1280)
 LOADS_BEHIND = 1
 LOADS_AHEAD = 1
-CHUNKS = (10,)
+CHUNKS = (2496,)
+ROWS = 8
 
 
 def in_vmem(count):
@@ -120,90 +121,119 @@
             out_ref[at : at + segment] = (wanted == held).astype(jnp.float32).astype(jnp.bfloat16)
 
 
-def multiply(start, rows_ref, weights_refs, keep_ref, send_ref):
+def multiply(start, size, rows_ref, weights_refs, keep_ref, send_ref):
     half, width = keep_ref.shape
     at, skip = 0, start
     for ref in weights_refs:
         held = ref.shape[1]
-        while at < width and skip < held:
-            size = min(TILE, width - at, held - skip)
-            product = jnp.dot(rows_ref[...], ref[:, skip : skip + size], preferred_element_type=jnp.float32)
-            keep_ref[:, at : at + size] = product[:half]
-            send_ref[:, at : at + size] = product[half:]
-            at, skip = at + size, skip + size
+        while at < size and skip < held:
+            step = min(TILE, size - at, held - skip)
+            product = jnp.dot(rows_ref[...], ref[:, skip : skip + step], preferred_element_type=jnp.float32)
+            keep_ref[:, at : at + step] = product[:half]
+            send_ref[:, at : at + step] = product[half:]
+            at, skip = at + step, skip + step
         skip = max(0, skip - held)
-
-
-def first_kernel(start, loads, chooser_ref, *refs):
+    for ref in (keep_ref, send_ref):
+        ref[:, size:] = jnp.zeros((half, width - size), jnp.float32)
+
+
+def first_kernel(start, size, loads, chooser_ref, *refs):
     weights_refs, block_refs, (rows_ref, keep_ref, send_ref) = refs[:loads], refs[loads:-3], refs[-3:]
     blocks = jnp.concatenate([ref[...] for ref in block_refs], axis=0)
     rows_ref[...] = jnp.dot(chooser_ref[...], blocks, preferred_element_type=jnp.float32).astype(jnp.bfloat16)
-    multiply(start, rows_ref, weights_refs, keep_ref, send_ref)
-
-
-def later_kernel(start, rows_ref, *refs):
+    multiply(start, size, rows_ref, weights_refs, keep_ref, send_ref)
+
+
+def later_kernel(start, size, rows_ref, *refs):
     *weights_refs, keep_ref, send_ref = refs
-    multiply(start, rows_ref, weights_refs, keep_ref, send_ref)
-
-
-def lanes_diagonal(n):
-    return lax.broadcasted_iota(jnp.int32, (n, LANES), 0) == lax.broadcasted_iota(jnp.int32, (n, LANES), 1)
-
-
-def add_kernel(own, keep_ref, got_ref, own_ref, *out_refs):
-    segment = own_ref.shape[0]
+    multiply(start, size, rows_ref, weights_refs, keep_ref, send_ref)
+
+
+def add_kernel(own, size, keep_ref, got_ref, own_ref, *out_refs):
+    segment, width = own_ref.shape
     own_ref[...] = keep_ref[:segment] + got_ref[:segment]
+    last = width - TILE
+    spare = lax.broadcasted_iota(jnp.int32, (ROWS, TILE), 1) >= size - last
     for s, out_ref in enumerate(out_refs, 1):
-        rows = slice(s * segment, (s + 1) * segment)
-        value = keep_ref[rows] + got_ref[rows]
-        peak = jnp.max(jnp.abs(value), axis=1, keepdims=True)
-        exponent = jnp.clip(jnp.ceil(jnp.log2(jnp.maximum(peak, 1e-30))), -90.0, 127.0)
-        scaled = jnp.clip(jnp.round(value * jnp.exp2(15.0 - exponent)), -32767.0, 32767.0)
-        out_ref[:, LANES:] = scaled[:, LANES:].astype(jnp.int32).astype(jnp.int16)
-        as_lanes = jnp.sum(jnp.where(lanes_diagonal(segment), exponent, 0.0), axis=0, keepdims=True)
-        spare = lax.broadcasted_iota(jnp.int32, (segment, LANES), 0) == own
-        out_ref[:, :LANES] = jnp.where(spare, as_lanes, scaled[:, :LANES]).astype(jnp.int32).astype(jnp.int16)
-
-
-def restored(own, got_ref):
-    value = got_ref[...].astype(jnp.int32).astype(jnp.float32)
-    segment = value.shape[0]
-    exponent = jnp.sum(
-        jnp.where(lanes_diagonal(segment), value[own : own + 1, :LANES], 0.0), axis=1, keepdims=True
-    )
-    return value * jnp.exp2(exponent - 15.0)
-
-
-def stats_kernel(own, *refs):
+        for t in range(-(-own // ROWS)):
+            rows = slice(s * segment + t * ROWS, s * segment + (t + 1) * ROWS)
+            value = keep_ref[rows] + got_ref[rows]
+            peak = jnp.max(jnp.abs(value), axis=1, keepdims=True)
+            exponent = jnp.clip(jnp.ceil(jnp.log2(jnp.maximum(peak, 1e-30))), -90.0, 127.0)
+            scaled = jnp.clip(jnp.round(value * jnp.exp2(15.0 - exponent)), -32767.0, 32767.0)
+            ending = jnp.where(spare, exponent, scaled[:, last:])
+            scaled = jnp.concatenate([scaled[:, :last], ending], axis=1) if last else ending
+            if own - t * ROWS <= ROWS // 2:
+                half = ROWS // 2
+                scaled = jnp.concatenate([scaled[:half, : width // 2], scaled[:half, width // 2 :]], axis=0)
+            out_ref[:, t * width : t * width + scaled.shape[1]] = scaled.astype(jnp.int32).astype(jnp.int16)
+
+
+def restored(own, size, width, got_ref, t):
+    half = own - t * ROWS <= ROWS // 2
+    value = got_ref[:, t * width : t * width + (width // 2 if half else width)]
+    value = value.astype(jnp.int32).astype(jnp.float32)
+    if half:
+        value = jnp.concatenate([value[: ROWS // 2], value[ROWS // 2 :]], axis=1)
+        value = jnp.concatenate([value, jnp.zeros_like(value)], axis=0)
+    return value * jnp.exp2(value[:, size : size + 1] - 15.0)
+
+
+def stats_kernel(own, size, *refs):
     *in_refs, guided_ref, out_ref = refs
     before = in_refs.pop(0) if in_refs[0].shape == out_ref.shape else None
-    guided = in_refs[0][...]
-    for got in in_refs[1:]:
-        guided = guided + restored(own, got)
-    guided_ref[...] = guided
-    segment = guided.shape[0]
-    top = jnp.max(guided, axis=1, keepdims=True)
+    segment, width = guided_ref.shape
+    real = lax.broadcasted_iota(jnp.int32, (ROWS, width), 1) < size
+    tops, totals = [], []
+    for t in range(segment // ROWS):
+        rows = slice(t * ROWS, (t + 1) * ROWS)
+        guided = in_refs[0][rows]
+        if t * ROWS < own:
+            for got in in_refs[1:]:
+                guided = guided + restored(own, size, width, got, t)
+        guided_ref[rows] = guided
+        top = jnp.max(jnp.where(real, guided, -jnp.inf), axis=1, keepdims=True)
+        tops.append(top)
+        totals.append(jnp.sum(jnp.where(real, jnp.exp(guided - top), 0.0), axis=1, keepdims=True))
+    top, total = as_row(jnp.concatenate(tops, axis=0)), as_row(jnp.concatenate(totals, axis=0))
     if before is not None:
-        earlier = as_column(before[0:1, :segment])
-        top = jnp.maximum(top, earlier)
-    total = jnp.sum(jnp.exp(guided - top), axis=1, keepdims=True)
-    if before is not None:
-        total = total + as_column(before[1:2, :segment]) * jnp.exp(earlier - top)
-    out_ref[0:1, :segment] = as_row(top)
-    out_ref[1:2, :segment] = as_row(total)
-
-
-def final_kernel(chunks, segment, *refs):
-    guided_refs, stats, out_ref = refs[:chunks], refs[chunks:-1], refs[-1]
-    top = functools.reduce(jnp.maximum, [ref[0:1, :segment] for ref in stats])
-    total = sum(ref[1:2, :segment] * jnp.exp(ref[0:1, :segment] - top) for ref in stats)
+        top, total = merged((top, total), (before[0:1, :segment], before[1:2, :segment]))
+    out_ref[0:1, :segment] = top
+    out_ref[1:2, :segment] = total
+
+
+def merged(one, other):
+    top = jnp.maximum(one[0], other[0])
+    return top, one[1] * jnp.exp(one[0] - top) + other[1] * jnp.exp(other[0] - top)
+
+
+def merge_kernel(one_ref, *refs):
+    *other_refs, out_ref = refs
+    top, total = one_ref[0:1], one_ref[1:2]
+    for ref in other_refs:
+        top, total = merged((top, total), (ref[0:1], ref[1:2]))
+    out_ref[0:1] = top
+    out_ref[1:2] = total
+
+
+def final_kernel(sizes, segment, *refs):
+    guided_refs, stats, (out_far, out_ref, sems) = refs[: len(sizes)], refs[len(sizes) : -3], refs[-3:]
+    top, total = stats[0][0:1, :segment], stats[0][1:2, :segment]
+    for ref in stats[1:]:
+        top, total = merged((top, total), (ref[0:1, :segment], ref[1:2, :segment]))
     own = out_ref.shape[0]
-    shift = as_column(top)[:own]
-    log_total = as_column(jnp.log(total))[:own]
-    at = 0
-    for ref in guided_refs:
-        out_ref[:, at : at + ref.shape[1]] = ref[:own] - shift - log_total
-        at += ref.shape[1]
+    shift, log_total = as_column(top), as_column(jnp.log(total))
+    copies = []
+    for t, first in enumerate(range(0, own, ROWS)):
+        rows = slice(first, min(first + ROWS, own))
+        at = 0
+        for ref, size in zip(guided_refs, sizes):
+            out_ref[rows, at : at + size] = ref[rows, :size] - shift[rows] - log_total[rows]
+            at += size
+        copies.append(pltpu.make_async_copy(out_ref.at[rows], out_far.at[rows], sems.at[t]))
+        copies[-1].start()
+    for copy in copies:
+        copy.wait()
 
 
 def shifted(value, axis, by):
@@ -211,12 +241,22 @@
     return lax.ppermute(value, axis, [(i, (i + by) % size) for i in range(size)])
 
 
-def cut(vocab, tiles):
+def cut(vocab, widths):
     edges = [0]
-    for count in tiles:
-        edges.append(min(vocab, edges[-1] + count * TILE))
+    for width in widths:
+        edges.append(min(vocab, edges[-1] + width))
     edges.append(vocab)
     return [(start, end - start) for start, end in zip(edges, edges[1:]) if end > start]
+
+
+def padded(size):
+    return -(-(size + 1) // TILE) * TILE
+
+
+def packed_shape(own, width):
+    blocks, rest = divmod(own, ROWS)
+    lanes = blocks * width + (0 if rest == 0 else width // 2 if rest <= ROWS // 2 else width)
+    return (ROWS, lanes)
 
 
 def per_device(final_hidden, positions, norm_gain, unembedding):
@@ -294,44 +334,51 @@
     chunks = cut(vocab, CHUNKS)
     parts, leaving = [], []
     for j, (start, size) in enumerate(chunks):
-        outs = [((half, size), f32)] * 2
+        width = padded(size)
+        outs = [((half, width), f32)] * 2
         cost = (4 * half * width_local * size, 2 * width_local * size)
         needed = [i for i, (at, held) in enumerate(loads) if at < start + size and start < at + held]
         skip = start - loads[needed[0]][0]
         pieces = [loaded[i] for i in needed]
         if j == 0:
             rows, keep, send = call(
-                functools.partial(first_kernel, skip, len(pieces)),
+                functools.partial(first_kernel, skip, size, len(pieces)),
                 [((n_x * n_c * segment, width_local), bf16)] + outs,
                 [chooser, *pieces, *arrivals],
                 cost=cost,
             )
         else:
-            keep, send = call(functools.partial(later_kernel, skip), outs, [rows, *pieces], cost=cost)
+            keep, send = call(functools.partial(later_kernel, skip, size), outs, [rows, *pieces], cost=cost)
         got = shifted(send, "cfg", 1)
         own_sum, *sends = call(
-            functools.partial(add_kernel, own),
-            [((segment, size), f32)] + [((segment, size), jnp.int16)] * (n_x - 1),
+            functools.partial(add_kernel, own, size),
+            [((segment, width), f32)] + [(packed_shape(own, width), jnp.int16)] * (n_x - 1),
             [keep, got],
         )
         parts.append(own_sum)
         leaving.append(sends)
     guided, stats = [], None
-    for own_sum, sends in zip(parts, leaving):
+    for (_, size), own_sum, sends in zip(chunks, parts, leaving):
         got = [shifted(s_rows, "rows", s) for s, s_rows in enumerate(sends, 1)]
         chunk, stats = call(
-            functools.partial(stats_kernel, own),
-            [(own_sum.shape, f32), ((8, LANES), f32)],
+            functools.partial(stats_kernel, own, size),
+            [(own_sum.shape, f32), ((2, LANES), f32)],
             ([] if stats is None else [stats]) + [own_sum, *got],
         )
         guided.append(chunk)
-    all_stats = [stats] + [shifted(stats, "vocab", s) for s in range(1, n_z)]
+    if n_z & (n_z - 1) == 0:
+        all_stats = [stats] + [
+            lax.ppermute(stats, "vocab", [(i, i ^ far) for i in range(n_z)]) for far in range(1, n_z)
+        ]
+    else:
+        all_stats = [stats] + [shifted(stats, "vocab", s) for s in range(1, n_z)]
     return pl.pallas_call(
-        functools.partial(final_kernel, len(chunks), segment),
+        functools.partial(final_kernel, [size for _, size in chunks], segment),
         out_shape=jax.ShapeDtypeStruct((own, vocab), f32),
-        in_specs=in_vmem(len(guided) + n_z),
-        out_specs=pl.BlockSpec(memory_space=pltpu.VMEM),
-        compiler_params=pltpu.CompilerParams(vmem_limit_bytes=16 * MIB),
+        in_specs=in_vmem(len(guided) + len(all_stats)),
+        out_specs=pl.BlockSpec(memory_space=pltpu.HBM),
+        scratch_shapes=[pltpu.VMEM((own, vocab), f32), pltpu.SemaphoreType.DMA((-(-own // ROWS),))],
+        compiler_params=pltpu.CompilerParams(vmem_limit_bytes=8 * MIB),
     )(*keep_in_vmem(*guided, *all_stats))
 
 

time: 56.1 us -> 55.2 us (0.984)
  waiting for transfers between devices: 18.7 us -> 16.2 us
  Pallas kernels: 21.3 us -> 22.7 us
    ppermute x12 -> x9, waiting for transfers between devices: 18.7 us -> 12.8 us  [shifted(): lax.ppermute(value, axis, [(i, (i + by) % size) for i in range(size)])]
    ppermute x0 -> x3, starting transfers between devices: none -> 4.58 us  [per_device(): lax.ppermute(stats, 'vocab', [(i, i ^ far) for i in range(n_z)])]
    ppermute x12 -> x9, starting transfers between devices: 15.8 us -> 11.3 us  [shifted(): lax.ppermute(value, axis, [(i, (i + by) % size) for i in range(size)])]
    ppermute x0 -> x3, waiting for transfers between devices: none -> 3.36 us  [per_device(): lax.ppermute(stats, 'vocab', [(i, i ^ far) for i in range(n_z)])]
    pallas_call x13 -> x14, Pallas kernels: 20.2 us -> 21.5 us  [call(): pl.pallas_call(body, out_shape=[pltpu.VMEM(shape, dtype) for shape, dtype...]
  transfers between devices with their start and end apart: 12 -> 12, of which waited for: 9 -> 9; matrix products, arithmetic and copies ran while one was open for 0% -> 0% of each run, Pallas kernels for 28% -> 31%
where the time goes in v4:
time: 55.2 us; the launch traced here: 55 us
  Pallas kernels  22.7 us (41%)
  waiting for transfers between devices  16.2 us (29%)
  starting transfers between devices  15.9 us (29%)
    pallas_call x14, Pallas kernels, call(): pl.pallas_call(body, out_shape=[pltpu.VMEM(shape, dtype) for shape, dtype...  21.5 us
    ppermute x9, waiting for transfers between devices, shifted(): lax.ppermute(value, axis, [(i, (i + by) % size) for i in range(size)])  12.8 us
    ppermute x9, starting transfers between devices, shifted(): lax.ppermute(value, axis, [(i, (i + by) % size) for i in range(size)])  11.3 us
    ppermute x3, starting transfers between devices, per_device(): lax.ppermute(stats, 'vocab', [(i, i ^ far) for i in range(n_z)])  4.58 us
    ppermute x3, waiting for transfers between devices, per_device(): lax.ppermute(stats, 'vocab', [(i, i ^ far) for i in range(n_z)])  3.36 us
    pallas_call x1, Pallas kernels, per_device(): pl.pallas_call(functools.partial(final_kernel, [size for _, size in chunk...  1.16 us
  transfers between devices with their start and end apart: 12, of which 9 were waited for; matrix products, arithmetic and copies ran while one was open for 0% of the time, Pallas kernels for 31%

profile of v4, /device:TPU:0, one launch (start us, length us, event | category | flops | bytes accessed | tf_op | source)
XLA Modules:
  0.0 55.0 jit_solution(8738011993196679232)
XLA Ops:
  0.0 1.3 %shard_map.46 = (bf16[2,64,2048]{2,1,0:T(8,128)(2,1)S(1)}, f32[2,64]{1,0:T(2,128)S(1)}) custom-call(bf16[2,64,2048]{2,1,0:T(8,128)(2,1)} %hidden_far.1, f32[1,2048]{1,0:T(1,128)} %bitcast.9), custom_call_target="tpu_custom_call" | custom-call | tf_op jit(solution)/shard_map/pallas_call | solution.py:31
  1.4 0.5 collective-permute-start
  1.9 0.8 %collective-permute-done = f32[2,64]{1,0:T(2,128)S(1)} collective-permute-done((f32[2,64]{1,0:T(2,128)S(1)}, f32[2,64]{1,0:T(2,128)S(1)}, u32[]{:S(2)}, u32[]{:S(2)}) %collective-permute-start) | collective-permute-done | bytes 544 | tf_op jit(solution)/shard_map/ppermute | solution.py:241
  2.7 2.8 %collective-permute-start.1 = (f32[2,64]{1,0:T(2,128)S(1)}, f32[2,64]{1,0:T(2,128)S(1)}, u32[]{:S(2)}, u32[]{:S(2)}) collective-permute-start(f32[2,64]{1,0:T(2,128)S(1)} %add.6), channel_id=1, source_target_pairs={{0,2},{2,0},{1,3},{3,1},{4,6},{6,4},{5,7},{7,5},{8,10},{10,8},{9,1... | collective-permute-start | bytes 1544 | tf_op jit(solution)/shard_map/ppermute | solution.py:241
  5.5 1.5 %collective-permute-done.1 = f32[2,64]{1,0:T(2,128)S(1)} collective-permute-done((f32[2,64]{1,0:T(2,128)S(1)}, f32[2,64]{1,0:T(2,128)S(1)}, u32[]{:S(2)}, u32[]{:S(2)}) %collective-permute-start.1) | collective-permute-done | bytes 544 | tf_op jit(solution)/shard_map/ppermute | solution.py:241
  7.1 0.2 shard_map.47.refs_3_
  7.2 2.2 %collective-permute-start.2 = (bf16[64,2048]{1,0:T(8,128)(2,1)S(1)}, bf16[64,2048]{1,0:T(8,128)(2,1)S(1)}, u32[]{:S(2)}, u32[]{:S(2)}) collective-permute-start(bf16[64,2048]{1,0:T(8,128)(2,1)S(1)} %shard_map.47.refs_3_), channel_id=1, source_target_pairs={{0,4},{4,8},{8,12},{12,0},{1,5},{5,9},{9,13},{13,1},{2,6},{6,10},{... | collective-permute-start | bytes 786440 | tf_op jit(solution)/shard_map/ppermute | solution.py:241
  9.4 3.5 %shard_map.48.refs_0_ = bf16[2048,1280]{1,0:T(8,128)(2,1)S(1)} custom-call(bf16[4752,2048]{1,0:T(8,128)(2,1)} %bitcast.4), custom_call_target="tpu_custom_call" | custom-call | bytes 5242880 | tf_op jit(solution)/shard_map/pallas_call | solution.py:31
  12.9 0.0 copy-start
  12.9 2.1 %collective-permute-start.3 = (bf16[64,2048]{1,0:T(8,128)(2,1)S(1)}, bf16[64,2048]{1,0:T(8,128)(2,1)S(1)}, u32[]{:S(2)}, u32[]{:S(2)}) collective-permute-start(bf16[64,2048]{1,0:T(8,128)(2,1)S(1)} %shard_map.47.refs_3_), channel_id=1, source_target_pairs={{0,12},{4,0},{8,4},{12,8},{1,13},{5,1},{9,5},{13,9},{2,14},{6,2},{... | collective-permute-start | bytes 786440 | tf_op jit(solution)/shard_map/ppermute | solution.py:241
  15.0 1.9 %shard_map.50.refs_1_ = bf16[2048,512]{1,0:T(8,128)(2,1)S(1)} custom-call(bf16[4752,2048]{1,0:T(8,128)(2,1)} %bitcast.5), custom_call_target="tpu_custom_call" | custom-call | bytes 2097152 | tf_op jit(solution)/shard_map/pallas_call | solution.py:31
  16.9 0.6 %collective-permute-done.2.refs_4_ = bf16[64,2048]{1,0:T(8,128)(2,1)S(1)} collective-permute-done((bf16[64,2048]{1,0:T(8,128)(2,1)S(1)}, bf16[64,2048]{1,0:T(8,128)(2,1)S(1)}, u32[]{:S(2)}, u32[]{:S(2)}) %collective-permute-start.2) | collective-permute-done | bytes 262176 | tf_op jit(solution)/shard_map/ppermute | solution.py:241
  17.5 0.0 collective-permute-start.4
  17.5 0.0 copy-done
  17.5 0.1 shard_map.49.chooser_ref
  17.6 2.2 %shard_map.51.refs_2_ = bf16[2048,704]{1,0:T(8,128)(2,1)S(1)} custom-call(bf16[4752,2048]{1,0:T(8,128)(2,1)} %bitcast.6), custom_call_target="tpu_custom_call" | custom-call | bytes 2883584 | tf_op jit(solution)/shard_map/pallas_call | solution.py:31
  19.9 3.5 %shard_map.52.refs_0_ = bf16[2048,1280]{1,0:T(8,128)(2,1)S(1)} custom-call(bf16[4752,2048]{1,0:T(8,128)(2,1)} %bitcast.7), custom_call_target="tpu_custom_call" | custom-call | bytes 5242880 | tf_op jit(solution)/shard_map/pallas_call | solution.py:31
  23.4 3.1 %shard_map.53.refs_1_ = bf16[2048,976]{1,0:T(8,128)(2,1)S(1)} custom-call(bf16[4752,2048]{1,0:T(8,128)(2,1)} %bitcast.8), custom_call_target="tpu_custom_call" | custom-call | bytes 3997696 | tf_op jit(solution)/shard_map/pallas_call | solution.py:31
  26.5 0.0 collective-permute-done.3.refs_5_
  26.5 1.7 %collective-permute-done.4.refs_6_ = bf16[64,2048]{1,0:T(8,128)(2,1)S(1)} collective-permute-done((bf16[64,2048]{1,0:T(8,128)(2,1)S(1)}, bf16[64,2048]{1,0:T(8,128)(2,1)S(1)}, u32[]{:S(2)}, u32[]{:S(2)}) %collective-permute-start.4) | collective-permute-done | bytes 262176 | tf_op jit(solution)/shard_map/ppermute | solution.py:241
  28.2 2.4 %shard_map.54 = (bf16[192,2048]{1,0:T(8,128)(2,1)S(1)}, f32[96,2560]{1,0:T(8,128)S(1)}, f32[96,2560]{1,0:T(8,128)S(1)}) custom-call(bf16[192,256]{1,0:T(8,128)(2,1)S(1)} %shard_map.49.chooser_ref, bf16[2048,1280]{1,0:T(8,128)(2,1)S(1)} %shard_map.48.refs_0_, bf16[2048,512]{1,0:T(8,128)(2,1)S(1)} %shard_map.50.refs_1_, ...), custom_call_target="tpu_custom_call" | custom-call | flops 1962934272 | bytes 10223616 | tf_op jit(solution)/shard_map/pallas_call | solution.py:31
  30.6 0.1 collective-permute-start.5
  30.7 2.0 %shard_map.57 = (f32[96,2304]{1,0:T(8,128)S(1)}, f32[96,2304]{1,0:T(8,128)S(1)}) custom-call(bf16[192,2048]{1,0:T(8,128)(2,1)S(1)} %get-tuple-element.56.rows_ref, bf16[2048,1280]{1,0:T(8,128)(2,1)S(1)} %shard_map.52.refs_0_, bf16[2048,976]{1,0:T(8,128)(2,1)S(1)} %shard_map.53.refs_1_), custom_call_target="tpu_custom_call" | custom-call | flops 1774190592 | bytes 9240576 | tf_op jit(solution)/shard_map/pallas_call | solution.py:31
  32.7 0.6 %collective-permute-start.7 = (f32[96,2304]{1,0:T(8,128)S(1)}, f32[96,2304]{1,0:T(8,128)S(1)}, u32[]{:S(2)}, u32[]{:S(2)}) collective-permute-start(f32[96,2304]{1,0:T(8,128)S(1)} %get-tuple-element.60), channel_id=1, source_target_pairs={{0,1},{1,0},{2,3},{3,2},{4,5},{5,4},{6,7},{7,6},{8,9},{9,8},{10,11... | collective-permute-start | bytes 2654216 | tf_op jit(solution)/shard_map/ppermute | solution.py:241
  33.2 0.0 collective-permute-done.5.got_ref
  33.2 0.2 shard_map.55
  33.5 1.6 %collective-permute-start.6 = (s16[8,14080]{1,0:T(8,128)(2,1)S(1)}, s16[8,14080]{1,0:T(8,128)(2,1)S(1)}, u32[]{:S(2)}, u32[]{:S(2)}) collective-permute-start(s16[8,14080]{1,0:T(8,128)(2,1)S(1)} %get-tuple-element.53), channel_id=1, source_target_pairs={{0,2},{2,0},{1,3},{3,1},{4,6},{6,4},{5,7},{7,5},{8,10},{10,8},{9,1... | collective-permute-start | bytes 675848 | tf_op jit(solution)/shard_map/ppermute | solution.py:241
  35.0 0.3 collective-permute-done.7.got_ref
  35.3 0.2 shard_map.58
  35.5 1.6 %collective-permute-start.8 = (s16[8,12672]{1,0:T(8,128)(2,1)S(1)}, s16[8,12672]{1,0:T(8,128)(2,1)S(1)}, u32[]{:S(2)}, u32[]{:S(2)}) collective-permute-start(s16[8,12672]{1,0:T(8,128)(2,1)S(1)} %get-tuple-element.62), channel_id=1, source_target_pairs={{0,2},{2,0},{1,3},{3,1},{4,6},{6,4},{5,7},{7,5},{8,10},{10,8},{9,1... | collective-permute-start | bytes 608264 | tf_op jit(solution)/shard_map/ppermute | solution.py:241
  37.1 4.8 %collective-permute-done.6.refs_1_ = s16[8,14080]{1,0:T(8,128)(2,1)S(1)} collective-permute-done((s16[8,14080]{1,0:T(8,128)(2,1)S(1)}, s16[8,14080]{1,0:T(8,128)(2,1)S(1)}, u32[]{:S(2)}, u32[]{:S(2)}) %collective-permute-start.6) | collective-permute-done | bytes 225312 | tf_op jit(solution)/shard_map/ppermute | solution.py:241
  41.9 0.4 shard_map.56
  42.3 3.1 %collective-permute-done.8.refs_2_ = s16[8,12672]{1,0:T(8,128)(2,1)S(1)} collective-permute-done((s16[8,12672]{1,0:T(8,128)(2,1)S(1)}, s16[8,12672]{1,0:T(8,128)(2,1)S(1)}, u32[]{:S(2)}, u32[]{:S(2)}) %collective-permute-start.8) | collective-permute-done | bytes 202784 | tf_op jit(solution)/shard_map/ppermute | solution.py:241
  45.4 0.4 shard_map.59
  45.8 3.5 %collective-permute-start.11 = (f32[2,128]{1,0:T(2,128)S(1)}, f32[2,128]{1,0:T(2,128)S(1)}, u32[]{:S(2)}, u32[]{:S(2)}) collective-permute-start(f32[2,128]{1,0:T(2,128)S(1)} %get-tuple-element.64.refs_2_), channel_id=1, source_target_pairs={{0,12},{4,8},{8,4},{12,0},{1,13},{5,9},{9,5},{13,1},{2,14},{6,10},... | collective-permute-start | bytes 3080 | tf_op jit(solution)/shard_map/ppermute | solution.py:371
  49.3 0.9 %collective-permute-start.10 = (f32[2,128]{1,0:T(2,128)S(1)}, f32[2,128]{1,0:T(2,128)S(1)}, u32[]{:S(2)}, u32[]{:S(2)}) collective-permute-start(f32[2,128]{1,0:T(2,128)S(1)} %get-tuple-element.64.refs_2_), channel_id=1, source_target_pairs={{0,8},{4,12},{8,0},{12,4},{1,9},{5,13},{9,1},{13,5},{2,10},{6,14},... | collective-permute-start | bytes 3080 | tf_op jit(solution)/shard_map/ppermute | solution.py:371
  50.2 0.2 collective-permute-start.9
  50.4 0.8 %collective-permute-done.11.refs_5_ = f32[2,128]{1,0:T(2,128)S(1)} collective-permute-done((f32[2,128]{1,0:T(2,128)S(1)}, f32[2,128]{1,0:T(2,128)S(1)}, u32[]{:S(2)}, u32[]{:S(2)}) %collective-permute-start.11) | collective-permute-done | bytes 1056 | tf_op jit(solution)/shard_map/ppermute | solution.py:371
  51.3 2.5 %collective-permute-done.10.refs_4_ = f32[2,128]{1,0:T(2,128)S(1)} collective-permute-done((f32[2,128]{1,0:T(2,128)S(1)}, f32[2,128]{1,0:T(2,128)S(1)}, u32[]{:S(2)}, u32[]{:S(2)}) %collective-permute-start.10) | collective-permute-done | bytes 1056 | tf_op jit(solution)/shard_map/ppermute | solution.py:371
  53.8 0.0 collective-permute-done.9.refs_3_
  53.8 1.2 %shard_map.60 = f32[44,4752]{1,0:T(8,128)} custom-call(f32[48,2560]{1,0:T(8,128)S(1)} %get-tuple-element.54.refs_0_, f32[48,2304]{1,0:T(8,128)S(1)} %get-tuple-element.63.refs_1_, f32[2,128]{1,0:T(2,128)S(1)} %get-tuple-element.64.refs_2_, f32[2,128]{1,0:T(2,128)S(1)} %collective-permute-done.9.refs_3_, f32[2,128]{1,0:T(2,128)S(1)} %collective-permute-done.10.refs_4_, ...), custom_call_target="tpu_custom_call" | custom-call | tf_op jit(solution)/shard_map/pallas_call | solution.py:375
  (2 shorter events, 0.0 us)
Async XLA Ops:
  1.4 1.3 %collective-permute-start = (f32[2,64]{1,0:T(2,128)S(1)}, f32[2,64]{1,0:T(2,128)S(1)}, u32[]{:S(2)}, u32[]{:S(2)}) collective-permute-start(f32[2,64]{1,0:T(2,128)S(1)} %get-tuple-element.36), channel_id=1, source_target_pairs={{0,1},{1,0},{2,3},{3,2},{4,5},{5,4},{6,7},{7,6},{8,9},{9,8},{10,11... | collective-permute-start | bytes 1544 | tf_op jit(solution)/shard_map/ppermute | solution.py:241
  2.7 4.4 %collective-permute-start.1 = (f32[2,64]{1,0:T(2,128)S(1)}, f32[2,64]{1,0:T(2,128)S(1)}, u32[]{:S(2)}, u32[]{:S(2)}) collective-permute-start(f32[2,64]{1,0:T(2,128)S(1)} %add.6), channel_id=1, source_target_pairs={{0,2},{2,0},{1,3},{3,1},{4,6},{6,4},{5,7},{7,5},{8,10},{10,8},{9,1... | collective-permute-start | bytes 1544 | tf_op jit(solution)/shard_map/ppermute | solution.py:241
  7.2 10.2 %collective-permute-start.2 = (bf16[64,2048]{1,0:T(8,128)(2,1)S(1)}, bf16[64,2048]{1,0:T(8,128)(2,1)S(1)}, u32[]{:S(2)}, u32[]{:S(2)}) collective-permute-start(bf16[64,2048]{1,0:T(8,128)(2,1)S(1)} %shard_map.47.refs_3_), channel_id=1, source_target_pairs={{0,4},{4,8},{8,12},{12,0},{1,5},{5,9},{9,13},{13,1},{2,6},{6,10},{... | collective-permute-start | bytes 786440 | tf_op jit(solution)/shard_map/ppermute | solution.py:241
  12.9 4.6 %copy-start = (s32[176]{0:T(256)S(1)}, s32[176]{0:T(256)}, u32[]{:S(2)}) copy-start(s32[176]{0:T(256)} %param.5) | copy-start | bytes 2116
  12.9 13.6 %collective-permute-start.3 = (bf16[64,2048]{1,0:T(8,128)(2,1)S(1)}, bf16[64,2048]{1,0:T(8,128)(2,1)S(1)}, u32[]{:S(2)}, u32[]{:S(2)}) collective-permute-start(bf16[64,2048]{1,0:T(8,128)(2,1)S(1)} %shard_map.47.refs_3_), channel_id=1, source_target_pairs={{0,12},{4,0},{8,4},{12,8},{1,13},{5,1},{9,5},{13,9},{2,14},{6,2},{... | collective-permute-start | bytes 786440 | tf_op jit(solution)/shard_map/ppermute | solution.py:241
  17.5 10.7 %collective-permute-start.4 = (bf16[64,2048]{1,0:T(8,128)(2,1)S(1)}, bf16[64,2048]{1,0:T(8,128)(2,1)S(1)}, u32[]{:S(2)}, u32[]{:S(2)}) collective-permute-start(bf16[64,2048]{1,0:T(8,128)(2,1)S(1)} %collective-permute-done.2.refs_4_), channel_id=1, source_target_pairs={{0,4},{4,8},{8,12},{12,0},{1,5},{5,9},{9,13},{13,1},{2,6},{6,10},{... | collective-permute-start | bytes 786440 | tf_op jit(solution)/shard_map/ppermute | solution.py:241
  30.6 2.6 %collective-permute-start.5 = (f32[96,2560]{1,0:T(8,128)S(1)}, f32[96,2560]{1,0:T(8,128)S(1)}, u32[]{:S(2)}, u32[]{:S(2)}) collective-permute-start(f32[96,2560]{1,0:T(8,128)S(1)} %get-tuple-element.51), channel_id=1, source_target_pairs={{0,1},{1,0},{2,3},{3,2},{4,5},{5,4},{6,7},{7,6},{8,9},{9,8},{10,11... | collective-permute-start | bytes 2949128 | tf_op jit(solution)/shard_map/ppermute | solution.py:241
  32.7 2.6 %collective-permute-start.7 = (f32[96,2304]{1,0:T(8,128)S(1)}, f32[96,2304]{1,0:T(8,128)S(1)}, u32[]{:S(2)}, u32[]{:S(2)}) collective-permute-start(f32[96,2304]{1,0:T(8,128)S(1)} %get-tuple-element.60), channel_id=1, source_target_pairs={{0,1},{1,0},{2,3},{3,2},{4,5},{5,4},{6,7},{7,6},{8,9},{9,8},{10,11... | collective-permute-start | bytes 2654216 | tf_op jit(solution)/shard_map/ppermute | solution.py:241
  33.5 8.4 %collective-permute-start.6 = (s16[8,14080]{1,0:T(8,128)(2,1)S(1)}, s16[8,14080]{1,0:T(8,128)(2,1)S(1)}, u32[]{:S(2)}, u32[]{:S(2)}) collective-permute-start(s16[8,14080]{1,0:T(8,128)(2,1)S(1)} %get-tuple-element.53), channel_id=1, source_target_pairs={{0,2},{2,0},{1,3},{3,1},{4,6},{6,4},{5,7},{7,5},{8,10},{10,8},{9,1... | collective-permute-start | bytes 675848 | tf_op jit(solution)/shard_map/ppermute | solution.py:241
  35.5 9.9 %collective-permute-start.8 = (s16[8,12672]{1,0:T(8,128)(2,1)S(1)}, s16[8,12672]{1,0:T(8,128)(2,1)S(1)}, u32[]{:S(2)}, u32[]{:S(2)}) collective-permute-start(s16[8,12672]{1,0:T(8,128)(2,1)S(1)} %get-tuple-element.62), channel_id=1, source_target_pairs={{0,2},{2,0},{1,3},{3,1},{4,6},{6,4},{5,7},{7,5},{8,10},{10,8},{9,1... | collective-permute-start | bytes 608264 | tf_op jit(solution)/shard_map/ppermute | solution.py:241
  45.8 5.4 %collective-permute-start.11 = (f32[2,128]{1,0:T(2,128)S(1)}, f32[2,128]{1,0:T(2,128)S(1)}, u32[]{:S(2)}, u32[]{:S(2)}) collective-permute-start(f32[2,128]{1,0:T(2,128)S(1)} %get-tuple-element.64.refs_2_), channel_id=1, source_target_pairs={{0,12},{4,8},{8,4},{12,0},{1,13},{5,9},{9,5},{13,1},{2,14},{6,10},... | collective-permute-start | bytes 3080 | tf_op jit(solution)/shard_map/ppermute | solution.py:371
  49.3 4.5 %collective-permute-start.10 = (f32[2,128]{1,0:T(2,128)S(1)}, f32[2,128]{1,0:T(2,128)S(1)}, u32[]{:S(2)}, u32[]{:S(2)}) collective-permute-start(f32[2,128]{1,0:T(2,128)S(1)} %get-tuple-element.64.refs_2_), channel_id=1, source_target_pairs={{0,8},{4,12},{8,0},{12,4},{1,9},{5,13},{9,1},{13,5},{2,10},{6,14},... | collective-permute-start | bytes 3080 | tf_op jit(solution)/shard_map/ppermute | solution.py:371
  50.2 3.6 %collective-permute-start.9 = (f32[2,128]{1,0:T(2,128)S(1)}, f32[2,128]{1,0:T(2,128)S(1)}, u32[]{:S(2)}, u32[]{:S(2)}) collective-permute-start(f32[2,128]{1,0:T(2,128)S(1)} %get-tuple-element.64.refs_2_), channel_id=1, source_target_pairs={{0,4},{4,0},{8,12},{12,8},{1,5},{5,1},{9,13},{13,9},{2,6},{6,2},{1... | collective-permute-start | bytes 3080 | tf_op jit(solution)/shard_map/ppermute | solution.py:371

commit v5 on v4

--- a/solution.py
+++ b/solution.py
@@ -12,11 +12,10 @@
 TILE = 256
 LANES = 128
 MIB = 1 << 20
-LOADS = (1280, 512, 704, 1280)
-LOADS_BEHIND = 1
-LOADS_AHEAD = 1
+LOADS = ((1280,), (1216,))
 CHUNKS = (2496,)
 ROWS = 8
+USUAL = 7 / 8
 
 
 def in_vmem(count):
@@ -51,11 +50,12 @@
     return jnp.sum(jnp.where(diagonal(column.shape[0]), column, 0.0), axis=0, keepdims=True)
 
 
-def squares_kernel(hidden_far, gain_far, normed_ref, out_ref, hidden_ref, gain_ref, sems):
+def squares_kernel(hidden_far, gain_far, places_far, normed_ref, out_ref, places_ref, hidden_ref, gain_ref, sems):
     copies = [
         pltpu.make_async_copy(hidden_far.at[0], hidden_ref.at[0], sems.at[0]),
         pltpu.make_async_copy(hidden_far.at[1], hidden_ref.at[1], sems.at[1]),
         pltpu.make_async_copy(gain_far, gain_ref, sems.at[2]),
+        pltpu.make_async_copy(places_far, places_ref, sems.at[3]),
     ]
     for copy in copies:
         copy.start()
@@ -67,58 +67,89 @@
     gain = gain_ref[...]
     for b in range(2):
         normed_ref[b] = (hidden_ref[b].astype(jnp.float32) * gain).astype(jnp.bfloat16)
-
-
-def combine_kernel(width, normed_ref, totals_ref, *out_refs):
+    copies[3].wait()
+
+
+def combine_kernel(width, normed_ref, totals_ref, compact_ref, usual_ref, rest_ref):
     inv_rms = lax.rsqrt(totals_ref[...] / width + epsilon)
     factor = [as_column((1.0 + guidance) * inv_rms[0:1]), as_column(guidance * inv_rms[1:2])]
-    piece = out_refs[0].shape[0]
-    for i, out_ref in enumerate(out_refs):
-        rows = slice(i * piece, (i + 1) * piece)
-        terms = [factor[b][rows] * normed_ref[b, rows, :].astype(jnp.float32) for b in range(2)]
-        out_ref[...] = (terms[0] - terms[1]).astype(jnp.bfloat16)
+    terms = [factor[b] * normed_ref[b].astype(jnp.float32) for b in range(2)]
+    rows = (terms[0] - terms[1]).astype(jnp.bfloat16)
+    rows = jnp.dot(compact_ref[...], rows, preferred_element_type=jnp.float32)
+    usual = usual_ref.shape[0]
+    usual_ref[...] = rows[:usual].astype(jnp.bfloat16)
+    rest_ref[...] = rows[usual:].astype(jnp.bfloat16)
 
 
 def load_kernel(start, weights_far, *refs):
-    *_, out_ref, tiles_ref, sems = refs
-    size, slots = out_ref.shape[1], tiles_ref.shape[0]
-    tiles = [(at, min(TILE, size - at)) for at in range(0, size, TILE)]
+    *out_refs, tiles_ref, sems = refs
+    slots = tiles_ref.shape[0]
+    tiles = []
+    for ref in out_refs:
+        size = ref.shape[1]
+        tiles += [(ref, at, min(TILE, size - at), start + at) for at in range(0, size, TILE)]
+        start += size
     copies = [
         pltpu.make_async_copy(
-            weights_far.at[pl.ds(start + at, rows)],
+            weights_far.at[pl.ds(column, rows)],
             tiles_ref.at[i % slots, pl.ds(0, rows)],
             sems.at[i % slots],
         )
-        for i, (at, rows) in enumerate(tiles)
+        for i, (_, _, rows, column) in enumerate(tiles)
     ]
     for copy in copies[:slots]:
         copy.start()
-    for i, (at, rows) in enumerate(tiles):
+    for i, (ref, at, rows, _) in enumerate(tiles):
         copies[i].wait()
-        out_ref[:, at : at + rows] = tiles_ref[i % slots, :rows].T
+        ref[:, at : at + rows] = tiles_ref[i % slots, :rows].T
         if i + slots < len(tiles):
             copies[i + slots].start()
 
 
-def chooser_kernel(own, offsets, n_z, n_x, n_c, block, positions_ref, out_ref):
+def first_rank(positions_ref, at):
+    return jnp.sum((positions_ref[...] < at).astype(jnp.float32), axis=1, keepdims=True).astype(jnp.int32)
+
+
+def compact_kernel(usual, n_z, positions_ref, out_ref, crowded_ref):
+    block, masked = out_ref.shape[0], positions_ref.shape[1]
+    ranks = [first_rank(positions_ref, b * block) for b in range(n_z + 1)]
+    most = functools.reduce(jnp.maximum, [end - first for first, end in zip(ranks, ranks[1:])])
+    crowded_ref[0, 0] = (jnp.max(most) > usual).astype(jnp.int32)
+    at = lax.axis_index("vocab") * block
+    first = first_rank(positions_ref, at)
+    rank = lax.broadcasted_iota(jnp.int32, (block, masked), 1)
+    match = rank == first + lax.broadcasted_iota(jnp.int32, (block, masked), 0)
+    places = (positions_ref[...] + 1).astype(jnp.float32)
+    wanted = jnp.sum(jnp.where(match, places, 0.0), axis=1, keepdims=True).astype(jnp.int32) - 1
+    held = at + lax.broadcasted_iota(jnp.int32, (block, block), 1)
+    out_ref[...] = (wanted == held).astype(jnp.float32).astype(jnp.bfloat16)
+
+
+def chooser_kernel(own, block, offsets, n_z, n_x, n_c, positions_ref, usual_ref, rest_ref):
     z, x, c = (lax.axis_index(axis) for axis in ("vocab", "rows", "cfg"))
-    masked = positions_ref.shape[1]
-    segment = out_ref.shape[0] // (n_x * n_c)
-    places = (positions_ref[...] + 1).astype(jnp.float32)
-    i = lax.broadcasted_iota(jnp.int32, (segment, masked), 0)
-    rank = lax.broadcasted_iota(jnp.int32, (segment, masked), 1)
-    lane = lax.broadcasted_iota(jnp.int32, (segment, out_ref.shape[1]), 1)
-    held = lane
-    for k, offset in enumerate(offsets):
-        moved = lane + (lax.rem(z - offset + n_z, n_z) - k) * block
-        held = jnp.where(lane >= k * block, moved, held)
+    rows, usual = usual_ref.shape[1:]
+    extra = block - usual
+    segment = rows // (n_x * n_c)
+    row = lax.broadcasted_iota(jnp.int32, (rows, 1), 0)
+    wanted = jnp.full((rows, 1), -1, jnp.int32)
     for t in range(n_c):
         for s in range(n_x):
             owner = lax.rem(x + s, n_x) * n_c + lax.rem(c + t, n_c)
-            match = (rank == owner * own + i) & (i < own)
-            wanted = jnp.sum(jnp.where(match, places, 0.0), axis=1, keepdims=True).astype(jnp.int32) - 1
-            at = (t * n_x + s) * segment
-            out_ref[at : at + segment] = (wanted == held).astype(jnp.float32).astype(jnp.bfloat16)
+            i = row - (t * n_x + s) * segment
+            wanted = jnp.where((i >= 0) & (i < own), owner * own + i, wanted)
+    lane = lax.broadcasted_iota(jnp.int32, (1, usual), 1)
+    rest_lane = lax.broadcasted_iota(jnp.int32, (1, rest_ref.shape[1]), 1)
+    rest_rank = jnp.full(rest_lane.shape, -2, jnp.int32)
+    for k, offset in enumerate(offsets):
+        at = lax.rem(z - offset + n_z, n_z) * block
+        first, end = first_rank(positions_ref, at), first_rank(positions_ref, at + block)
+        rank = first + lane
+        held = jnp.where(rank < end, rank, -2)
+        usual_ref[k] = (wanted == held).astype(jnp.float32).astype(jnp.bfloat16)
+        i = rest_lane - k * extra
+        rank = first + usual + i
+        rest_rank = jnp.where((i >= 0) & (i < extra) & (rank < end), rank, rest_rank)
+    rest_ref[...] = (wanted == rest_rank).astype(jnp.float32).astype(jnp.bfloat16)
 
 
 def multiply(start, size, rows_ref, weights_refs, keep_ref, send_ref):
@@ -137,10 +168,18 @@
         ref[:, size:] = jnp.zeros((half, width - size), jnp.float32)
 
 
-def first_kernel(start, size, loads, chooser_ref, *refs):
-    weights_refs, block_refs, (rows_ref, keep_ref, send_ref) = refs[:loads], refs[loads:-3], refs[-3:]
-    blocks = jnp.concatenate([ref[...] for ref in block_refs], axis=0)
-    rows_ref[...] = jnp.dot(chooser_ref[...], blocks, preferred_element_type=jnp.float32).astype(jnp.bfloat16)
+def early_kernel(chooser_ref, rest_chooser_ref, *refs):
+    *block_refs, rest_ref, rows_ref = refs
+    rows = jnp.dot(rest_chooser_ref[...], rest_ref[...], preferred_element_type=jnp.float32)
+    for k, ref in enumerate(block_refs):
+        rows = rows + jnp.dot(chooser_ref[k], ref[...], preferred_element_type=jnp.float32)
+    rows_ref[...] = rows.astype(jnp.bfloat16)
+
+
+def first_kernel(start, size, chooser_ref, early_ref, block_ref, *refs):
+    *weights_refs, rows_ref, keep_ref, send_ref = refs
+    last = jnp.dot(chooser_ref[chooser_ref.shape[0] - 1], block_ref[...], preferred_element_type=jnp.float32)
+    rows_ref[...] = (early_ref[...].astype(jnp.float32) + last).astype(jnp.bfloat16)
     multiply(start, size, rows_ref, weights_refs, keep_ref, send_ref)
 
 
@@ -269,66 +308,98 @@
     own = masked // (n_x * n_c)
     segment = -(-(own + 1) // 16) * 16
 
-    normed, squares = call(
+    normed, squares, places = call(
         squares_kernel,
-        [((2, block, width_local), bf16), ((2, block), f32)],
+        [((2, block, width_local), bf16), ((2, block), f32), ((1, masked), jnp.int32)],
         [],
-        far=[final_hidden, norm_gain[None, :]],
+        far=[final_hidden, norm_gain[None, :], positions[None, :]],
         scratch_shapes=[
             pltpu.VMEM((2, block, width_local), bf16),
             pltpu.VMEM((1, width_local), f32),
-            pltpu.SemaphoreType.DMA((3,)),
+            pltpu.SemaphoreType.DMA((4,)),
         ],
     )
     for axis in ("cfg", "rows"):
         squares = sum([shifted(squares, axis, s) for s in range(1, lax.axis_size(axis))], squares)
-    (block_rows,) = call(
+    usual = int(block * USUAL) // ROWS * ROWS
+    compact, crowded = pl.pallas_call(
+        functools.partial(compact_kernel, usual, n_z),
+        out_shape=[pltpu.VMEM((block, block), bf16), jax.ShapeDtypeStruct((1, 1), jnp.int32)],
+        in_specs=in_vmem(1),
+        out_specs=[*in_vmem(1), pl.BlockSpec(memory_space=pltpu.SMEM)],
+        compiler_params=pltpu.CompilerParams(vmem_limit_bytes=8 * MIB),
+    )(*keep_in_vmem(places))
+    block_rows, rest_rows = call(
         functools.partial(combine_kernel, width_local * n_x * n_c),
-        [((block, width_local), bf16)],
-        [normed, squares],
+        [((usual, width_local), bf16), ((block - usual, width_local), bf16)],
+        [normed, squares, compact],
     )
 
     weights = unembedding.T
-    loads, loaded = cut(vocab, LOADS), []
+    loads, loaded = cut(vocab, [width for group in LOADS for width in group]), []
 
     def load(count, after):
         nonlocal weights
-        for start, size in loads[len(loaded) : len(loaded) + count]:
-            weights, after = lax.optimization_barrier((weights, after))
-            (piece,) = call(
-                functools.partial(load_kernel, start),
-                [((width_local, size), bf16)],
-                [],
-                far=[weights],
-                cost=(0, 2 * size * width_local),
-                scratch_shapes=[pltpu.VMEM((3, TILE, width_local), bf16), pltpu.SemaphoreType.DMA((3,))],
-            )
-            piece, after = lax.optimization_barrier((piece, after))
-            loaded.append(piece)
+        pieces = loads[len(loaded) : len(loaded) + count]
+        if not pieces:
+            return after
+        weights, after = lax.optimization_barrier((weights, after))
+        arrays = call(
+            functools.partial(load_kernel, pieces[0][0]),
+            [((width_local, size), bf16) for _, size in pieces],
+            [],
+            far=[weights],
+            cost=(0, 2 * sum(size for _, size in pieces) * width_local),
+            scratch_shapes=[pltpu.VMEM((3, TILE, width_local), bf16), pltpu.SemaphoreType.DMA((3,))],
+        )
+        *arrays, after = lax.optimization_barrier((*arrays, after))
+        loaded.extend(arrays)
         return after
 
+    def both_ways(own_block):
+        ahead = behind = own_block
+        gathered = [own_block]
+        for step in range(1, n_z // 2 + 1):
+            ahead = shifted(ahead, "vocab", 1)
+            gathered.append(ahead)
+            if 2 * step < n_z:
+                behind = shifted(behind, "vocab", -1)
+                gathered.append(behind)
+        return gathered
+
+    offsets = [0] + [sign * step for step in range(1, n_z // 2 + 1) for sign in (1, -1) if sign > 0 or 2 * step < n_z]
+    rest = lax.cond(
+        crowded[0, 0] > 0,
+        lambda rest: jnp.concatenate(both_ways(rest), axis=0),
+        lambda rest: jnp.zeros((n_z * rest.shape[0], rest.shape[1]), rest.dtype),
+        rest_rows,
+    )
+    weights, places, rest = lax.optimization_barrier((weights, places, rest))
     ahead = shifted(block_rows, "vocab", 1)
-    arrivals, offsets = [block_rows, ahead], [0, 1]
-    behind = load(LOADS_BEHIND, block_rows)
+    behind = load(len(LOADS[0]), block_rows)
+    aheads, behinds = [ahead], []
     for step in range(1, (n_z - 1) // 2 + 1):
         behind = shifted(behind, "vocab", -1)
-        arrivals.append(behind)
-        offsets.append(-step)
-    if LOADS_AHEAD:
-        load(LOADS_AHEAD, loaded[-1] if loaded else block_rows)
-        ahead, loaded[-1] = lax.optimization_barrier((ahead, loaded[-1]))
-    load_after = ahead
+        behinds.append(behind)
     for step in range(2, n_z // 2 + 1):
         ahead = shifted(ahead, "vocab", 1)
-        arrivals.append(ahead)
-        offsets.append(step)
-    load(len(loads), load_after)
-    (chooser,) = call(
-        functools.partial(chooser_kernel, own, offsets, n_z, n_x, n_c, block),
-        [((n_x * n_c * segment, n_z * block), bf16)],
-        [lax.optimization_barrier((positions[None, :], loaded[0]))[0]],
-    )
-    chooser, *loaded = lax.optimization_barrier((chooser, *loaded))
+        aheads.append(ahead)
+    arrivals = [block_rows]
+    for step in range(n_z // 2):
+        arrivals += aheads[step : step + 1] + behinds[step : step + 1]
+
+    chooser, rest_chooser = call(
+        functools.partial(chooser_kernel, own, block, offsets, n_z, n_x, n_c),
+        [((n_z, n_x * n_c * segment, usual), bf16), ((n_x * n_c * segment, n_z * (block - usual)), bf16)],
+        [places],
+    )
+    load(len(loads), aheads[0])
+    chooser, rest_chooser, *loaded = lax.optimization_barrier((chooser, rest_chooser, *loaded))
+    (early,) = call(
+        early_kernel,
+        [((n_x * n_c * segment, width_local), bf16)],
+        [chooser, rest_chooser, *arrivals[:-1], rest],
+    )
 
     half = n_x * segment
     chunks = cut(vocab, CHUNKS)
@@ -342,9 +413,9 @@
         pieces = [loaded[i] for i in needed]
         if j == 0:
             rows, keep, send = call(
-                functools.partial(first_kernel, skip, size, len(pieces)),
+                functools.partial(first_kernel, skip, size),
                 [((n_x * n_c * segment, width_local), bf16)] + outs,
-                [chooser, *pieces, *arrivals],
+                [chooser, early, arrivals[-1], *pieces],
                 cost=cost,
             )
         else:

time: 55.2 us -> 53.4 us (0.967)
  waiting for transfers between devices: 16.2 us -> 14.5 us
  Pallas kernels: 22.7 us -> 21.9 us
  between operations: 0.13 us -> 0.93 us
    pallas_call x14 -> x12, Pallas kernels: 21.5 us -> 20.1 us  [call(): pl.pallas_call(body, out_shape=[pltpu.VMEM(shape, dtype) for shape, dtype...]
    ppermute x9, waiting for transfers between devices: 12.8 us -> 11.8 us  [shifted(): lax.ppermute(value, axis, [(i, (i + by) % size) for i in range(size)])]
    pallas_call x0 -> x1, Pallas kernels: none -> 0.65 us  [per_device(): pl.pallas_call(functools.partial(compact_kernel, usual, n_z), out_shape=[...]
    ppermute x3, waiting for transfers between devices: 3.36 us -> 2.74 us  [per_device(): lax.ppermute(stats, 'vocab', [(i, i ^ far) for i in range(n_z)])]
where the time goes in v5:
time: 53.4 us; the launch traced here: 53.2 us
  Pallas kernels  21.9 us (41%)
  starting transfers between devices  15.8 us (30%)
  waiting for transfers between devices  14.5 us (27%)
  between operations  0.93 us (2%)
    pallas_call x12, Pallas kernels, call(): pl.pallas_call(body, out_shape=[pltpu.VMEM(shape, dtype) for shape, dtype...  20.1 us
    ppermute x9, waiting for transfers between devices, shifted(): lax.ppermute(value, axis, [(i, (i + by) % size) for i in range(size)])  11.8 us
    ppermute x9, starting transfers between devices, shifted(): lax.ppermute(value, axis, [(i, (i + by) % size) for i in range(size)])  11.3 us
    ppermute x3, starting transfers between devices, per_device(): lax.ppermute(stats, 'vocab', [(i, i ^ far) for i in range(n_z)])  4.45 us
    ppermute x3, waiting for transfers between devices, per_device(): lax.ppermute(stats, 'vocab', [(i, i ^ far) for i in range(n_z)])  2.74 us
    pallas_call x1, Pallas kernels, per_device(): pl.pallas_call(functools.partial(final_kernel, [size for _, size in chunk...  1.16 us
  transfers between devices with their start and end apart: 12, of which 9 were waited for; matrix products, arithmetic and copies ran while one was open for 0% of the time, Pallas kernels for 31%

profile of v5, /device:TPU:0, one launch (start us, length us, event | category | flops | bytes accessed | tf_op | source)
XLA Modules:
  0.0 53.2 jit_solution(7763619538731592076)
XLA Ops:
  0.0 1.4 %shard_map.46 = (bf16[2,64,2048]{2,1,0:T(8,128)(2,1)S(1)}, f32[2,64]{1,0:T(2,128)S(1)}, s32[1,176]{1,0:T(1,128)S(1)}) custom-call(bf16[2,64,2048]{2,1,0:T(8,128)(2,1)} %hidden_far.1, f32[1,2048]{1,0:T(1,128)} %bitcast.6, s32[1,176]{1,0:T(1,128)} %bitcast.7), custom_call_target="tpu_custom_call" | custom-call | tf_op jit(solution)/shard_map/pallas_call | solution.py:30
  1.4 0.5 collective-permute-start.3
  1.9 0.8 %collective-permute-done.3 = f32[2,64]{1,0:T(2,128)S(1)} collective-permute-done((f32[2,64]{1,0:T(2,128)S(1)}, f32[2,64]{1,0:T(2,128)S(1)}, u32[]{:S(2)}, u32[]{:S(2)}) %collective-permute-start.3) | collective-permute-done | bytes 544 | tf_op jit(solution)/shard_map/ppermute | solution.py:280
  2.7 2.8 %collective-permute-start.4 = (f32[2,64]{1,0:T(2,128)S(1)}, f32[2,64]{1,0:T(2,128)S(1)}, u32[]{:S(2)}, u32[]{:S(2)}) collective-permute-start(f32[2,64]{1,0:T(2,128)S(1)} %add.6), channel_id=1, source_target_pairs={{0,2},{2,0},{1,3},{3,1},{4,6},{6,4},{5,7},{7,5},{8,10},{10,8},{9,1... | collective-permute-start | bytes 1544 | tf_op jit(solution)/shard_map/ppermute | solution.py:280
  5.5 0.7 %shard_map.47 = (bf16[64,64]{1,0:T(8,128)(2,1)S(1)}, s32[1,1]{1,0:T(1,128)}) custom-call(s32[1,176]{1,0:T(1,128)S(1)} %get-tuple-element.52.positions_ref), custom_call_target="tpu_custom_call" | custom-call | tf_op jit(solution)/shard_map/pallas_call | solution.py:325
  6.2 0.9 %collective-permute-done.4 = f32[2,64]{1,0:T(2,128)S(1)} collective-permute-done((f32[2,64]{1,0:T(2,128)S(1)}, f32[2,64]{1,0:T(2,128)S(1)}, u32[]{:S(2)}, u32[]{:S(2)}) %collective-permute-start.4) | collective-permute-done | bytes 544 | tf_op jit(solution)/shard_map/ppermute | solution.py:280
  7.1 0.3 shard_map.48
  7.4 2.2 %collective-permute-start.5 = (bf16[56,2048]{1,0:T(8,128)(2,1)S(1)}, bf16[56,2048]{1,0:T(8,128)(2,1)S(1)}, u32[]{:S(2)}, u32[]{:S(2)}) collective-permute-start(bf16[56,2048]{1,0:T(8,128)(2,1)S(1)} %get-tuple-element.65.refs_0_), channel_id=1, source_target_pairs={{0,4},{4,8},{8,12},{12,0},{1,5},{5,9},{9,13},{13,1},{2,6},{6,10},{... | collective-permute-start | bytes 688136 | tf_op jit(solution)/shard_map/ppermute | solution.py:280
  10.3 3.5 %shard_map.50.refs_0_ = bf16[2048,1280]{1,0:T(8,128)(2,1)S(1)} custom-call(bf16[4752,2048]{1,0:T(8,128)(2,1)} %bitcast.4), custom_call_target="tpu_custom_call" | custom-call | bytes 5242880 | tf_op jit(solution)/shard_map/pallas_call | solution.py:30
  13.7 2.1 %collective-permute-start.6 = (bf16[56,2048]{1,0:T(8,128)(2,1)S(1)}, bf16[56,2048]{1,0:T(8,128)(2,1)S(1)}, u32[]{:S(2)}, u32[]{:S(2)}) collective-permute-start(bf16[56,2048]{1,0:T(8,128)(2,1)S(1)} %get-tuple-element.65.refs_0_), channel_id=1, source_target_pairs={{0,12},{4,0},{8,4},{12,8},{1,13},{5,1},{9,5},{13,9},{2,14},{6,2},{... | collective-permute-start | bytes 688136 | tf_op jit(solution)/shard_map/ppermute | solution.py:280
  15.8 0.7 %collective-permute-done.5.refs_1_ = bf16[56,2048]{1,0:T(8,128)(2,1)S(1)} collective-permute-done((bf16[56,2048]{1,0:T(8,128)(2,1)S(1)}, bf16[56,2048]{1,0:T(8,128)(2,1)S(1)}, u32[]{:S(2)}, u32[]{:S(2)}) %collective-permute-start.5) | collective-permute-done | bytes 229408 | tf_op jit(solution)/shard_map/ppermute | solution.py:280
  16.5 0.0 collective-permute-start.7
  16.5 0.2 shard_map.49
  16.7 8.2 %shard_map.51 = (bf16[2048,1216]{1,0:T(8,128)(2,1)S(1)}, bf16[2048,2256]{1,0:T(8,128)(2,1)S(1)}) custom-call(bf16[4752,2048]{1,0:T(8,128)(2,1)} %bitcast.5), custom_call_target="tpu_custom_call" | custom-call | bytes 14221312 | tf_op jit(solution)/shard_map/pallas_call | solution.py:30
  24.9 0.0 collective-permute-done.6.refs_2_
  24.9 0.9 %shard_map.52.early_ref = bf16[192,2048]{1,0:T(8,128)(2,1)S(1)} custom-call(bf16[4,192,56]{2,1,0:T(8,128)(2,1)S(1)} %get-tuple-element.63.chooser_ref, bf16[192,32]{1,0:T(8,128)(2,1)S(1)} %get-tuple-element.64.rest_chooser_ref, bf16[56,2048]{1,0:T(8,128)(2,1)S(1)} %get-tuple-element.65.refs_0_, bf16[56,2048]{1,0:T(8,128)(2,1)S(1)} %collective-permute-done.5.refs_1_, ...), custom_call_target="tpu_custom_call" | custom-call | tf_op jit(solution)/shard_map/pallas_call | solution.py:30
  25.8 1.2 %collective-permute-done.7.block_ref = bf16[56,2048]{1,0:T(8,128)(2,1)S(1)} collective-permute-done((bf16[56,2048]{1,0:T(8,128)(2,1)S(1)}, bf16[56,2048]{1,0:T(8,128)(2,1)S(1)}, u32[]{:S(2)}, u32[]{:S(2)}) %collective-permute-start.7) | collective-permute-done | bytes 229408 | tf_op jit(solution)/shard_map/ppermute | solution.py:280
  27.0 2.4 %shard_map.53 = (bf16[192,2048]{1,0:T(8,128)(2,1)S(1)}, f32[96,2560]{1,0:T(8,128)S(1)}, f32[96,2560]{1,0:T(8,128)S(1)}) custom-call(bf16[4,192,56]{2,1,0:T(8,128)(2,1)S(1)} %get-tuple-element.63.chooser_ref, bf16[192,2048]{1,0:T(8,128)(2,1)S(1)} %shard_map.52.early_ref, bf16[56,2048]{1,0:T(8,128)(2,1)S(1)} %collective-permute-done.7.block_ref, ...), custom_call_target="tpu_custom_call" | custom-call | flops 1962934272 | bytes 10223616 | tf_op jit(solution)/shard_map/pallas_call | solution.py:30
  29.4 0.1 collective-permute-start.8
  29.5 2.0 %shard_map.56 = (f32[96,2304]{1,0:T(8,128)S(1)}, f32[96,2304]{1,0:T(8,128)S(1)}) custom-call(bf16[192,2048]{1,0:T(8,128)(2,1)S(1)} %get-tuple-element.75.rows_ref, bf16[2048,2256]{1,0:T(8,128)(2,1)S(1)} %get-tuple-element.76.refs_0_), custom_call_target="tpu_custom_call" | custom-call | flops 1774190592 | bytes 9240576 | tf_op jit(solution)/shard_map/pallas_call | solution.py:30
  31.5 0.6 %collective-permute-start.10 = (f32[96,2304]{1,0:T(8,128)S(1)}, f32[96,2304]{1,0:T(8,128)S(1)}, u32[]{:S(2)}, u32[]{:S(2)}) collective-permute-start(f32[96,2304]{1,0:T(8,128)S(1)} %get-tuple-element.78), channel_id=1, source_target_pairs={{0,1},{1,0},{2,3},{3,2},{4,5},{5,4},{6,7},{7,6},{8,9},{9,8},{10,11... | collective-permute-start | bytes 2654216 | tf_op jit(solution)/shard_map/ppermute | solution.py:280
  32.0 0.0 collective-permute-done.8.got_ref
  32.0 0.2 shard_map.54
  32.3 1.6 %collective-permute-start.9 = (s16[8,14080]{1,0:T(8,128)(2,1)S(1)}, s16[8,14080]{1,0:T(8,128)(2,1)S(1)}, u32[]{:S(2)}, u32[]{:S(2)}) collective-permute-start(s16[8,14080]{1,0:T(8,128)(2,1)S(1)} %get-tuple-element.72), channel_id=1, source_target_pairs={{0,2},{2,0},{1,3},{3,1},{4,6},{6,4},{5,7},{7,5},{8,10},{10,8},{9,1... | collective-permute-start | bytes 675848 | tf_op jit(solution)/shard_map/ppermute | solution.py:280
  33.8 0.3 collective-permute-done.10.got_ref
  34.1 0.2 shard_map.57
  34.3 1.6 %collective-permute-start.11 = (s16[8,12672]{1,0:T(8,128)(2,1)S(1)}, s16[8,12672]{1,0:T(8,128)(2,1)S(1)}, u32[]{:S(2)}, u32[]{:S(2)}) collective-permute-start(s16[8,12672]{1,0:T(8,128)(2,1)S(1)} %get-tuple-element.80), channel_id=1, source_target_pairs={{0,2},{2,0},{1,3},{3,1},{4,6},{6,4},{5,7},{7,5},{8,10},{10,8},{9,1... | collective-permute-start | bytes 608264 | tf_op jit(solution)/shard_map/ppermute | solution.py:280
  35.9 4.8 %collective-permute-done.9.refs_1_ = s16[8,14080]{1,0:T(8,128)(2,1)S(1)} collective-permute-done((s16[8,14080]{1,0:T(8,128)(2,1)S(1)}, s16[8,14080]{1,0:T(8,128)(2,1)S(1)}, u32[]{:S(2)}, u32[]{:S(2)}) %collective-permute-start.9) | collective-permute-done | bytes 225312 | tf_op jit(solution)/shard_map/ppermute | solution.py:280
  40.7 0.4 shard_map.55
  41.1 3.1 %collective-permute-done.11.refs_2_ = s16[8,12672]{1,0:T(8,128)(2,1)S(1)} collective-permute-done((s16[8,12672]{1,0:T(8,128)(2,1)S(1)}, s16[8,12672]{1,0:T(8,128)(2,1)S(1)}, u32[]{:S(2)}, u32[]{:S(2)}) %collective-permute-start.11) | collective-permute-done | bytes 202784 | tf_op jit(solution)/shard_map/ppermute | solution.py:280
  44.2 0.4 shard_map.58
  44.6 2.7 %collective-permute-start.14 = (f32[2,128]{1,0:T(2,128)S(1)}, f32[2,128]{1,0:T(2,128)S(1)}, u32[]{:S(2)}, u32[]{:S(2)}) collective-permute-start(f32[2,128]{1,0:T(2,128)S(1)} %get-tuple-element.82.refs_2_), channel_id=1, source_target_pairs={{0,12},{4,8},{8,4},{12,0},{1,13},{5,9},{9,5},{13,1},{2,14},{6,10},... | collective-permute-start | bytes 3080 | tf_op jit(solution)/shard_map/ppermute | solution.py:442
  47.4 0.0 collective-permute-start.13
  47.4 1.7 %collective-permute-start.12 = (f32[2,128]{1,0:T(2,128)S(1)}, f32[2,128]{1,0:T(2,128)S(1)}, u32[]{:S(2)}, u32[]{:S(2)}) collective-permute-start(f32[2,128]{1,0:T(2,128)S(1)} %get-tuple-element.82.refs_2_), channel_id=1, source_target_pairs={{0,4},{4,0},{8,12},{12,8},{1,5},{5,1},{9,13},{13,9},{2,6},{6,2},{1... | collective-permute-start | bytes 3080 | tf_op jit(solution)/shard_map/ppermute | solution.py:442
  49.1 1.0 %collective-permute-done.14.refs_5_ = f32[2,128]{1,0:T(2,128)S(1)} collective-permute-done((f32[2,128]{1,0:T(2,128)S(1)}, f32[2,128]{1,0:T(2,128)S(1)}, u32[]{:S(2)}, u32[]{:S(2)}) %collective-permute-start.14) | collective-permute-done | bytes 1056 | tf_op jit(solution)/shard_map/ppermute | solution.py:442
  50.1 1.8 %collective-permute-done.13.refs_4_ = f32[2,128]{1,0:T(2,128)S(1)} collective-permute-done((f32[2,128]{1,0:T(2,128)S(1)}, f32[2,128]{1,0:T(2,128)S(1)}, u32[]{:S(2)}, u32[]{:S(2)}) %collective-permute-start.13) | collective-permute-done | bytes 1056 | tf_op jit(solution)/shard_map/ppermute | solution.py:442
  51.8 0.0 collective-permute-done.12.refs_3_
  51.8 1.2 %shard_map.59 = f32[44,4752]{1,0:T(8,128)} custom-call(f32[48,2560]{1,0:T(8,128)S(1)} %get-tuple-element.73.refs_0_, f32[48,2304]{1,0:T(8,128)S(1)} %get-tuple-element.81.refs_1_, f32[2,128]{1,0:T(2,128)S(1)} %get-tuple-element.82.refs_2_, f32[2,128]{1,0:T(2,128)S(1)} %collective-permute-done.12.refs_3_, f32[2,128]{1,0:T(2,128)S(1)} %collective-permute-done.13.refs_4_, ...), custom_call_target="tpu_custom_call" | custom-call | tf_op jit(solution)/shard_map/pallas_call | solution.py:446
  (4 shorter events, 0.1 us)
Async XLA Ops:
  1.4 1.3 %collective-permute-start.3 = (f32[2,64]{1,0:T(2,128)S(1)}, f32[2,64]{1,0:T(2,128)S(1)}, u32[]{:S(2)}, u32[]{:S(2)}) collective-permute-start(f32[2,64]{1,0:T(2,128)S(1)} %get-tuple-element.49), channel_id=1, source_target_pairs={{0,1},{1,0},{2,3},{3,2},{4,5},{5,4},{6,7},{7,6},{8,9},{9,8},{10,11... | collective-permute-start | bytes 1544 | tf_op jit(solution)/shard_map/ppermute | solution.py:280
  2.7 4.4 %collective-permute-start.4 = (f32[2,64]{1,0:T(2,128)S(1)}, f32[2,64]{1,0:T(2,128)S(1)}, u32[]{:S(2)}, u32[]{:S(2)}) collective-permute-start(f32[2,64]{1,0:T(2,128)S(1)} %add.6), channel_id=1, source_target_pairs={{0,2},{2,0},{1,3},{3,1},{4,6},{6,4},{5,7},{7,5},{8,10},{10,8},{9,1... | collective-permute-start | bytes 1544 | tf_op jit(solution)/shard_map/ppermute | solution.py:280
  7.4 9.1 %collective-permute-start.5 = (bf16[56,2048]{1,0:T(8,128)(2,1)S(1)}, bf16[56,2048]{1,0:T(8,128)(2,1)S(1)}, u32[]{:S(2)}, u32[]{:S(2)}) collective-permute-start(bf16[56,2048]{1,0:T(8,128)(2,1)S(1)} %get-tuple-element.65.refs_0_), channel_id=1, source_target_pairs={{0,4},{4,8},{8,12},{12,0},{1,5},{5,9},{9,13},{13,1},{2,6},{6,10},{... | collective-permute-start | bytes 688136 | tf_op jit(solution)/shard_map/ppermute | solution.py:280
  13.7 11.1 %collective-permute-start.6 = (bf16[56,2048]{1,0:T(8,128)(2,1)S(1)}, bf16[56,2048]{1,0:T(8,128)(2,1)S(1)}, u32[]{:S(2)}, u32[]{:S(2)}) collective-permute-start(bf16[56,2048]{1,0:T(8,128)(2,1)S(1)} %get-tuple-element.65.refs_0_), channel_id=1, source_target_pairs={{0,12},{4,0},{8,4},{12,8},{1,13},{5,1},{9,5},{13,9},{2,14},{6,2},{... | collective-permute-start | bytes 688136 | tf_op jit(solution)/shard_map/ppermute | solution.py:280
  16.5 10.5 %collective-permute-start.7 = (bf16[56,2048]{1,0:T(8,128)(2,1)S(1)}, bf16[56,2048]{1,0:T(8,128)(2,1)S(1)}, u32[]{:S(2)}, u32[]{:S(2)}) collective-permute-start(bf16[56,2048]{1,0:T(8,128)(2,1)S(1)} %collective-permute-done.5.refs_1_), channel_id=1, source_target_pairs={{0,4},{4,8},{8,12},{12,0},{1,5},{5,9},{9,13},{13,1},{2,6},{6,10},{... | collective-permute-start | bytes 688136 | tf_op jit(solution)/shard_map/ppermute | solution.py:280
  29.4 2.6 %collective-permute-start.8 = (f32[96,2560]{1,0:T(8,128)S(1)}, f32[96,2560]{1,0:T(8,128)S(1)}, u32[]{:S(2)}, u32[]{:S(2)}) collective-permute-start(f32[96,2560]{1,0:T(8,128)S(1)} %get-tuple-element.70), channel_id=1, source_target_pairs={{0,1},{1,0},{2,3},{3,2},{4,5},{5,4},{6,7},{7,6},{8,9},{9,8},{10,11... | collective-permute-start | bytes 2949128 | tf_op jit(solution)/shard_map/ppermute | solution.py:280
  31.5 2.6 %collective-permute-start.10 = (f32[96,2304]{1,0:T(8,128)S(1)}, f32[96,2304]{1,0:T(8,128)S(1)}, u32[]{:S(2)}, u32[]{:S(2)}) collective-permute-start(f32[96,2304]{1,0:T(8,128)S(1)} %get-tuple-element.78), channel_id=1, source_target_pairs={{0,1},{1,0},{2,3},{3,2},{4,5},{5,4},{6,7},{7,6},{8,9},{9,8},{10,11... | collective-permute-start | bytes 2654216 | tf_op jit(solution)/shard_map/ppermute | solution.py:280
  32.3 8.4 %collective-permute-start.9 = (s16[8,14080]{1,0:T(8,128)(2,1)S(1)}, s16[8,14080]{1,0:T(8,128)(2,1)S(1)}, u32[]{:S(2)}, u32[]{:S(2)}) collective-permute-start(s16[8,14080]{1,0:T(8,128)(2,1)S(1)} %get-tuple-element.72), channel_id=1, source_target_pairs={{0,2},{2,0},{1,3},{3,1},{4,6},{6,4},{5,7},{7,5},{8,10},{10,8},{9,1... | collective-permute-start | bytes 675848 | tf_op jit(solution)/shard_map/ppermute | solution.py:280
  34.3 9.9 %collective-permute-start.11 = (s16[8,12672]{1,0:T(8,128)(2,1)S(1)}, s16[8,12672]{1,0:T(8,128)(2,1)S(1)}, u32[]{:S(2)}, u32[]{:S(2)}) collective-permute-start(s16[8,12672]{1,0:T(8,128)(2,1)S(1)} %get-tuple-element.80), channel_id=1, source_target_pairs={{0,2},{2,0},{1,3},{3,1},{4,6},{6,4},{5,7},{7,5},{8,10},{10,8},{9,1... | collective-permute-start | bytes 608264 | tf_op jit(solution)/shard_map/ppermute | solution.py:280
  44.6 5.4 %collective-permute-start.14 = (f32[2,128]{1,0:T(2,128)S(1)}, f32[2,128]{1,0:T(2,128)S(1)}, u32[]{:S(2)}, u32[]{:S(2)}) collective-permute-start(f32[2,128]{1,0:T(2,128)S(1)} %get-tuple-element.82.refs_2_), channel_id=1, source_target_pairs={{0,12},{4,8},{8,4},{12,0},{1,13},{5,9},{9,5},{13,1},{2,14},{6,10},... | collective-permute-start | bytes 3080 | tf_op jit(solution)/shard_map/ppermute | solution.py:442
  47.4 4.5 %collective-permute-start.13 = (f32[2,128]{1,0:T(2,128)S(1)}, f32[2,128]{1,0:T(2,128)S(1)}, u32[]{:S(2)}, u32[]{:S(2)}) collective-permute-start(f32[2,128]{1,0:T(2,128)S(1)} %get-tuple-element.82.refs_2_), channel_id=1, source_target_pairs={{0,8},{4,12},{8,0},{12,4},{1,9},{5,13},{9,1},{13,5},{2,10},{6,14},... | collective-permute-start | bytes 3080 | tf_op jit(solution)/shard_map/ppermute | solution.py:442
  47.4 4.5 %collective-permute-start.12 = (f32[2,128]{1,0:T(2,128)S(1)}, f32[2,128]{1,0:T(2,128)S(1)}, u32[]{:S(2)}, u32[]{:S(2)}) collective-permute-start(f32[2,128]{1,0:T(2,128)S(1)} %get-tuple-element.82.refs_2_), channel_id=1, source_target_pairs={{0,4},{4,0},{8,12},{12,8},{1,5},{5,1},{9,13},{13,9},{2,6},{6,2},{1... | collective-permute-start | bytes 3080 | tf_op jit(solution)/shard_map/ppermute | solution.py:442

commit v6 on v5

--- a/solution.py
+++ b/solution.py
@@ -13,9 +13,11 @@
 LANES = 128
 MIB = 1 << 20
 LOADS = ((1280,), (1216,))
+SLOTS = 5
 CHUNKS = (2496,)
 ROWS = 8
-USUAL = 7 / 8
+USUAL = 13 / 16
+DEEP = 16
 
 
 def in_vmem(count):
@@ -70,15 +72,33 @@
     copies[3].wait()
 
 
-def combine_kernel(width, normed_ref, totals_ref, compact_ref, usual_ref, rest_ref):
+def combine_kernel(width, usual, normed_ref, totals_ref, compact_ref, usual_ref, rest_ref):
     inv_rms = lax.rsqrt(totals_ref[...] / width + epsilon)
     factor = [as_column((1.0 + guidance) * inv_rms[0:1]), as_column(guidance * inv_rms[1:2])]
     terms = [factor[b] * normed_ref[b].astype(jnp.float32) for b in range(2)]
     rows = (terms[0] - terms[1]).astype(jnp.bfloat16)
     rows = jnp.dot(compact_ref[...], rows, preferred_element_type=jnp.float32)
-    usual = usual_ref.shape[0]
-    usual_ref[...] = rows[:usual].astype(jnp.bfloat16)
-    rest_ref[...] = rows[usual:].astype(jnp.bfloat16)
+    whole, last = divmod(usual, DEEP)
+    columns = rows.shape[1]
+    for t in range(whole):
+        usual_ref[:, t * columns : (t + 1) * columns] = rows[t * DEEP : (t + 1) * DEEP].astype(jnp.bfloat16)
+    if last:
+        share = columns * last // DEEP
+        ending = rows[whole * DEEP : usual]
+        ending = jnp.concatenate([ending[:, at : at + share] for at in range(0, columns, share)], axis=0)
+        usual_ref[:, whole * columns :] = ending.astype(jnp.bfloat16)
+    rest_ref[...] = rows[whole * DEEP :].astype(jnp.bfloat16)
+
+
+def unpacked(ref, usual, columns):
+    whole, last = divmod(usual, DEEP)
+    blocks = [ref[:, t * columns : (t + 1) * columns] for t in range(whole)]
+    if last:
+        ending = ref[:, whole * columns :].astype(jnp.float32)
+        ending = jnp.concatenate([ending[at : at + last] for at in range(0, DEEP, last)], axis=1)
+        ending = jnp.concatenate([ending, jnp.zeros((DEEP - last, columns), jnp.float32)], axis=0)
+        blocks.append(ending.astype(jnp.bfloat16))
+    return blocks
 
 
 def load_kernel(start, weights_far, *refs):
@@ -125,10 +145,9 @@
     out_ref[...] = (wanted == held).astype(jnp.float32).astype(jnp.bfloat16)
 
 
-def chooser_kernel(own, block, offsets, n_z, n_x, n_c, positions_ref, usual_ref, rest_ref):
+def chooser_kernel(own, block, usual, offsets, n_z, n_x, n_c, positions_ref, early_ref, last_ref):
     z, x, c = (lax.axis_index(axis) for axis in ("vocab", "rows", "cfg"))
-    rows, usual = usual_ref.shape[1:]
-    extra = block - usual
+    rows, deep = last_ref.shape
     segment = rows // (n_x * n_c)
     row = lax.broadcasted_iota(jnp.int32, (rows, 1), 0)
     wanted = jnp.full((rows, 1), -1, jnp.int32)
@@ -137,19 +156,22 @@
             owner = lax.rem(x + s, n_x) * n_c + lax.rem(c + t, n_c)
             i = row - (t * n_x + s) * segment
             wanted = jnp.where((i >= 0) & (i < own), owner * own + i, wanted)
-    lane = lax.broadcasted_iota(jnp.int32, (1, usual), 1)
-    rest_lane = lax.broadcasted_iota(jnp.int32, (1, rest_ref.shape[1]), 1)
-    rest_rank = jnp.full(rest_lane.shape, -2, jnp.int32)
+    lane = lax.broadcasted_iota(jnp.int32, (1, early_ref.shape[1]), 1)
+    held = jnp.full(lane.shape, -2, jnp.int32)
+    skipped = usual // DEEP * DEEP
     for k, offset in enumerate(offsets):
         at = lax.rem(z - offset + n_z, n_z) * block
         first, end = first_rank(positions_ref, at), first_rank(positions_ref, at + block)
-        rank = first + lane
-        held = jnp.where(rank < end, rank, -2)
-        usual_ref[k] = (wanted == held).astype(jnp.float32).astype(jnp.bfloat16)
-        i = rest_lane - k * extra
-        rank = first + usual + i
-        rest_rank = jnp.where((i >= 0) & (i < extra) & (rank < end), rank, rest_rank)
-    rest_ref[...] = (wanted == rest_rank).astype(jnp.float32).astype(jnp.bfloat16)
+        if k < n_z - 1:
+            i = lane - k * deep
+            held = jnp.where((i >= 0) & (i < usual) & (first + i < end), first + i, held)
+        else:
+            i = lax.broadcasted_iota(jnp.int32, (1, deep), 1)
+            last = jnp.where((i < usual) & (first + i < end), first + i, -2)
+        i = lane - (n_z - 1) * deep - k * (block - skipped) + skipped
+        held = jnp.where((i >= usual) & (i < block) & (first + i < end), first + i, held)
+    early_ref[...] = (wanted == held).astype(jnp.float32).astype(jnp.bfloat16)
+    last_ref[...] = (wanted == last).astype(jnp.float32).astype(jnp.bfloat16)
 
 
 def multiply(start, size, rows_ref, weights_refs, keep_ref, send_ref):
@@ -168,17 +190,17 @@
         ref[:, size:] = jnp.zeros((half, width - size), jnp.float32)
 
 
-def early_kernel(chooser_ref, rest_chooser_ref, *refs):
+def early_kernel(usual, chooser_ref, *refs):
     *block_refs, rest_ref, rows_ref = refs
-    rows = jnp.dot(rest_chooser_ref[...], rest_ref[...], preferred_element_type=jnp.float32)
-    for k, ref in enumerate(block_refs):
-        rows = rows + jnp.dot(chooser_ref[k], ref[...], preferred_element_type=jnp.float32)
-    rows_ref[...] = rows.astype(jnp.bfloat16)
-
-
-def first_kernel(start, size, chooser_ref, early_ref, block_ref, *refs):
+    blocks = [part for ref in block_refs for part in unpacked(ref, usual, rows_ref.shape[1])]
+    blocks = jnp.concatenate([*blocks, rest_ref[...]], axis=0)
+    rows_ref[...] = jnp.dot(chooser_ref[...], blocks, preferred_element_type=jnp.float32).astype(jnp.bfloat16)
+
+
+def first_kernel(start, size, usual, chooser_ref, early_ref, block_ref, *refs):
     *weights_refs, rows_ref, keep_ref, send_ref = refs
-    last = jnp.dot(chooser_ref[chooser_ref.shape[0] - 1], block_ref[...], preferred_element_type=jnp.float32)
+    block = jnp.concatenate(unpacked(block_ref, usual, rows_ref.shape[1]), axis=0)
+    last = jnp.dot(chooser_ref[...], block, preferred_element_type=jnp.float32)
     rows_ref[...] = (early_ref[...].astype(jnp.float32) + last).astype(jnp.bfloat16)
     multiply(start, size, rows_ref, weights_refs, keep_ref, send_ref)
 
@@ -321,7 +343,8 @@
     )
     for axis in ("cfg", "rows"):
         squares = sum([shifted(squares, axis, s) for s in range(1, lax.axis_size(axis))], squares)
-    usual = int(block * USUAL) // ROWS * ROWS
+    usual = int(block * USUAL)
+    skipped = usual // DEEP * DEEP
     compact, crowded = pl.pallas_call(
         functools.partial(compact_kernel, usual, n_z),
         out_shape=[pltpu.VMEM((block, block), bf16), jax.ShapeDtypeStruct((1, 1), jnp.int32)],
@@ -330,8 +353,8 @@
         compiler_params=pltpu.CompilerParams(vmem_limit_bytes=8 * MIB),
     )(*keep_in_vmem(places))
     block_rows, rest_rows = call(
-        functools.partial(combine_kernel, width_local * n_x * n_c),
-        [((usual, width_local), bf16), ((block - usual, width_local), bf16)],
+        functools.partial(combine_kernel, width_local * n_x * n_c, usual),
+        [((DEEP, usual * width_local // DEEP), bf16), ((block - skipped, width_local), bf16)],
         [normed, squares, compact],
     )
 
@@ -350,7 +373,7 @@
             [],
             far=[weights],
             cost=(0, 2 * sum(size for _, size in pieces) * width_local),
-            scratch_shapes=[pltpu.VMEM((3, TILE, width_local), bf16), pltpu.SemaphoreType.DMA((3,))],
+            scratch_shapes=[pltpu.VMEM((SLOTS, TILE, width_local), bf16), pltpu.SemaphoreType.DMA((SLOTS,))],
         )
         *arrays, after = lax.optimization_barrier((*arrays, after))
         loaded.extend(arrays)
@@ -388,17 +411,18 @@
     for step in range(n_z // 2):
         arrivals += aheads[step : step + 1] + behinds[step : step + 1]
 
-    chooser, rest_chooser = call(
-        functools.partial(chooser_kernel, own, block, offsets, n_z, n_x, n_c),
-        [((n_z, n_x * n_c * segment, usual), bf16), ((n_x * n_c * segment, n_z * (block - usual)), bf16)],
+    selected, deep = n_x * n_c * segment, -(-usual // DEEP) * DEEP
+    early_chooser, last_chooser = call(
+        functools.partial(chooser_kernel, own, block, usual, offsets, n_z, n_x, n_c),
+        [((selected, (n_z - 1) * deep + n_z * (block - skipped)), bf16), ((selected, deep), bf16)],
         [places],
     )
     load(len(loads), aheads[0])
-    chooser, rest_chooser, *loaded = lax.optimization_barrier((chooser, rest_chooser, *loaded))
+    early_chooser, last_chooser, *loaded = lax.optimization_barrier((early_chooser, last_chooser, *loaded))
     (early,) = call(
-        early_kernel,
-        [((n_x * n_c * segment, width_local), bf16)],
-        [chooser, rest_chooser, *arrivals[:-1], rest],
+        functools.partial(early_kernel, usual),
+        [((selected, width_local), bf16)],
+        [early_chooser, *arrivals[:-1], rest],
     )
 
     half = n_x * segment
@@ -413,9 +437,9 @@
         pieces = [loaded[i] for i in needed]
         if j == 0:
             rows, keep, send = call(
-                functools.partial(first_kernel, skip, size),
-                [((n_x * n_c * segment, width_local), bf16)] + outs,
-                [chooser, early, arrivals[-1], *pieces],
+                functools.partial(first_kernel, skip, size, usual),
+                [((selected, width_local), bf16)] + outs,
+                [last_chooser, early, arrivals[-1], *pieces],
                 cost=cost,
             )
         else:

time: 53.4 us -> 51.3 us (0.961)
  Pallas kernels: 21.9 us -> 18.6 us
  waiting for transfers between devices: 14.5 us -> 15.8 us
    pallas_call x12, Pallas kernels: 20.1 us -> 16.7 us  [call(): pl.pallas_call(body, out_shape=[pltpu.VMEM(shape, dtype) for shape, dtype...]
    ppermute x9, waiting for transfers between devices: 11.8 us -> 13.8 us  [shifted(): lax.ppermute(value, axis, [(i, (i + by) % size) for i in range(size)])]
    ppermute x3, waiting for transfers between devices: 2.74 us -> 1.98 us  [per_device(): lax.ppermute(stats, 'vocab', [(i, i ^ far) for i in range(n_z)])]
  transfers between devices with their start and end apart: 12 -> 12, of which waited for: 9 -> 9; matrix products, arithmetic and copies ran while one was open for 0% -> 0% of each run, Pallas kernels for 31% -> 25%
where the time goes in v6:
time: 51.3 us; the launch traced here: 51.1 us
  Pallas kernels  18.6 us (36%)
  starting transfers between devices  15.8 us (31%)
  waiting for transfers between devices  15.8 us (31%)
  between operations  0.93 us (2%)
    pallas_call x12, Pallas kernels, call(): pl.pallas_call(body, out_shape=[pltpu.VMEM(shape, dtype) for shape, dtype...  16.7 us
    ppermute x9, waiting for transfers between devices, shifted(): lax.ppermute(value, axis, [(i, (i + by) % size) for i in range(size)])  13.8 us
    ppermute x9, starting transfers between devices, shifted(): lax.ppermute(value, axis, [(i, (i + by) % size) for i in range(size)])  11.3 us
    ppermute x3, starting transfers between devices, per_device(): lax.ppermute(stats, 'vocab', [(i, i ^ far) for i in range(n_z)])  4.45 us
    ppermute x3, waiting for transfers between devices, per_device(): lax.ppermute(stats, 'vocab', [(i, i ^ far) for i in range(n_z)])  1.98 us
    pallas_call x1, Pallas kernels, per_device(): pl.pallas_call(functools.partial(final_kernel, [size for _, size in chunk...  1.16 us
  transfers between devices with their start and end apart: 12, of which 9 were waited for; matrix products, arithmetic and copies ran while one was open for 0% of the time, Pallas kernels for 25%

profile of v6, /device:TPU:0, one launch (start us, length us, event | category | flops | bytes accessed | tf_op | source)
XLA Modules:
  0.0 51.1 jit_solution(11963809762352183055)
XLA Ops:
  0.0 1.4 %shard_map.46 = (bf16[2,64,2048]{2,1,0:T(8,128)(2,1)S(1)}, f32[2,64]{1,0:T(2,128)S(1)}, s32[1,176]{1,0:T(1,128)S(1)}) custom-call(bf16[2,64,2048]{2,1,0:T(8,128)(2,1)} %hidden_far.1, f32[1,2048]{1,0:T(1,128)} %bitcast.6, s32[1,176]{1,0:T(1,128)} %bitcast.7), custom_call_target="tpu_custom_call" | custom-call | tf_op jit(solution)/shard_map/pallas_call | solution.py:32
  1.4 0.5 %collective-permute-start.3 = (f32[2,64]{1,0:T(2,128)S(1)}, f32[2,64]{1,0:T(2,128)S(1)}, u32[]{:S(2)}, u32[]{:S(2)}) collective-permute-start(f32[2,64]{1,0:T(2,128)S(1)} %get-tuple-element.49), channel_id=1, source_target_pairs={{0,1},{1,0},{2,3},{3,2},{4,5},{5,4},{6,7},{7,6},{8,9},{9,8},{10,11... | collective-permute-start | bytes 1544 | tf_op jit(solution)/shard_map/ppermute | solution.py:302
  1.9 0.8 %collective-permute-done.3 = f32[2,64]{1,0:T(2,128)S(1)} collective-permute-done((f32[2,64]{1,0:T(2,128)S(1)}, f32[2,64]{1,0:T(2,128)S(1)}, u32[]{:S(2)}, u32[]{:S(2)}) %collective-permute-start.3) | collective-permute-done | bytes 544 | tf_op jit(solution)/shard_map/ppermute | solution.py:302
  2.7 2.8 %collective-permute-start.4 = (f32[2,64]{1,0:T(2,128)S(1)}, f32[2,64]{1,0:T(2,128)S(1)}, u32[]{:S(2)}, u32[]{:S(2)}) collective-permute-start(f32[2,64]{1,0:T(2,128)S(1)} %add.6), channel_id=1, source_target_pairs={{0,2},{2,0},{1,3},{3,1},{4,6},{6,4},{5,7},{7,5},{8,10},{10,8},{9,1... | collective-permute-start | bytes 1544 | tf_op jit(solution)/shard_map/ppermute | solution.py:302
  5.5 0.7 %shard_map.47 = (bf16[64,64]{1,0:T(8,128)(2,1)S(1)}, s32[1,1]{1,0:T(1,128)}) custom-call(s32[1,176]{1,0:T(1,128)S(1)} %get-tuple-element.52.positions_ref), custom_call_target="tpu_custom_call" | custom-call | tf_op jit(solution)/shard_map/pallas_call | solution.py:348
  6.2 0.9 %collective-permute-done.4 = f32[2,64]{1,0:T(2,128)S(1)} collective-permute-done((f32[2,64]{1,0:T(2,128)S(1)}, f32[2,64]{1,0:T(2,128)S(1)}, u32[]{:S(2)}, u32[]{:S(2)}) %collective-permute-start.4) | collective-permute-done | bytes 544 | tf_op jit(solution)/shard_map/ppermute | solution.py:302
  7.1 0.3 shard_map.48
  7.4 2.2 %collective-permute-start.5 = (bf16[16,6656]{1,0:T(8,128)(2,1)S(1)}, bf16[16,6656]{1,0:T(8,128)(2,1)S(1)}, u32[]{:S(2)}, u32[]{:S(2)}) collective-permute-start(bf16[16,6656]{1,0:T(8,128)(2,1)S(1)} %get-tuple-element.65.refs_0_), channel_id=1, source_target_pairs={{0,4},{4,8},{8,12},{12,0},{1,5},{5,9},{9,13},{13,1},{2,6},{6,10},{... | collective-permute-start | bytes 638984 | tf_op jit(solution)/shard_map/ppermute | solution.py:302
  10.3 2.9 %shard_map.50.refs_0_ = bf16[2048,1280]{1,0:T(8,128)(2,1)S(1)} custom-call(bf16[4752,2048]{1,0:T(8,128)(2,1)} %bitcast.4), custom_call_target="tpu_custom_call" | custom-call | bytes 5242880 | tf_op jit(solution)/shard_map/pallas_call | solution.py:32
  13.2 2.1 %collective-permute-start.6 = (bf16[16,6656]{1,0:T(8,128)(2,1)S(1)}, bf16[16,6656]{1,0:T(8,128)(2,1)S(1)}, u32[]{:S(2)}, u32[]{:S(2)}) collective-permute-start(bf16[16,6656]{1,0:T(8,128)(2,1)S(1)} %get-tuple-element.65.refs_0_), channel_id=1, source_target_pairs={{0,12},{4,0},{8,4},{12,8},{1,13},{5,1},{9,5},{13,9},{2,14},{6,2},{... | collective-permute-start | bytes 638984 | tf_op jit(solution)/shard_map/ppermute | solution.py:302
  15.3 0.9 %collective-permute-done.5.refs_1_ = bf16[16,6656]{1,0:T(8,128)(2,1)S(1)} collective-permute-done((bf16[16,6656]{1,0:T(8,128)(2,1)S(1)}, bf16[16,6656]{1,0:T(8,128)(2,1)S(1)}, u32[]{:S(2)}, u32[]{:S(2)}) %collective-permute-start.5) | collective-permute-done | bytes 213024 | tf_op jit(solution)/shard_map/ppermute | solution.py:302
  16.2 0.0 collective-permute-start.7
  16.2 0.1 shard_map.49
  16.3 6.0 %shard_map.51 = (bf16[2048,1216]{1,0:T(8,128)(2,1)S(1)}, bf16[2048,2256]{1,0:T(8,128)(2,1)S(1)}) custom-call(bf16[4752,2048]{1,0:T(8,128)(2,1)} %bitcast.5), custom_call_target="tpu_custom_call" | custom-call | bytes 14221312 | tf_op jit(solution)/shard_map/pallas_call | solution.py:32
  22.3 0.0 collective-permute-done.6.refs_2_
  22.3 0.4 shard_map.52.early_ref
  22.7 3.0 %collective-permute-done.7.block_ref = bf16[16,6656]{1,0:T(8,128)(2,1)S(1)} collective-permute-done((bf16[16,6656]{1,0:T(8,128)(2,1)S(1)}, bf16[16,6656]{1,0:T(8,128)(2,1)S(1)}, u32[]{:S(2)}, u32[]{:S(2)}) %collective-permute-start.7) | collective-permute-done | bytes 213024 | tf_op jit(solution)/shard_map/ppermute | solution.py:302
  25.7 2.4 %shard_map.53 = (bf16[192,2048]{1,0:T(8,128)(2,1)S(1)}, f32[96,2560]{1,0:T(8,128)S(1)}, f32[96,2560]{1,0:T(8,128)S(1)}) custom-call(bf16[192,64]{1,0:T(8,128)(2,1)S(1)} %get-tuple-element.63.chooser_ref, bf16[192,2048]{1,0:T(8,128)(2,1)S(1)} %shard_map.52.early_ref, bf16[16,6656]{1,0:T(8,128)(2,1)S(1)} %collective-permute-done.7.block_ref, ...), custom_call_target="tpu_custom_call" | custom-call | flops 1962934272 | bytes 10223616 | tf_op jit(solution)/shard_map/pallas_call | solution.py:32
  28.1 0.1 collective-permute-start.8
  28.2 2.0 %shard_map.56 = (f32[96,2304]{1,0:T(8,128)S(1)}, f32[96,2304]{1,0:T(8,128)S(1)}) custom-call(bf16[192,2048]{1,0:T(8,128)(2,1)S(1)} %get-tuple-element.75.rows_ref, bf16[2048,2256]{1,0:T(8,128)(2,1)S(1)} %get-tuple-element.76.refs_0_), custom_call_target="tpu_custom_call" | custom-call | flops 1774190592 | bytes 9240576 | tf_op jit(solution)/shard_map/pallas_call | solution.py:32
  30.2 0.6 %collective-permute-start.10 = (f32[96,2304]{1,0:T(8,128)S(1)}, f32[96,2304]{1,0:T(8,128)S(1)}, u32[]{:S(2)}, u32[]{:S(2)}) collective-permute-start(f32[96,2304]{1,0:T(8,128)S(1)} %get-tuple-element.78), channel_id=1, source_target_pairs={{0,1},{1,0},{2,3},{3,2},{4,5},{5,4},{6,7},{7,6},{8,9},{9,8},{10,11... | collective-permute-start | bytes 2654216 | tf_op jit(solution)/shard_map/ppermute | solution.py:302
  30.8 0.0 collective-permute-done.8.got_ref
  30.8 0.2 shard_map.54
  31.0 1.6 %collective-permute-start.9 = (s16[8,14080]{1,0:T(8,128)(2,1)S(1)}, s16[8,14080]{1,0:T(8,128)(2,1)S(1)}, u32[]{:S(2)}, u32[]{:S(2)}) collective-permute-start(s16[8,14080]{1,0:T(8,128)(2,1)S(1)} %get-tuple-element.72), channel_id=1, source_target_pairs={{0,2},{2,0},{1,3},{3,1},{4,6},{6,4},{5,7},{7,5},{8,10},{10,8},{9,1... | collective-permute-start | bytes 675848 | tf_op jit(solution)/shard_map/ppermute | solution.py:302
  32.6 0.2 collective-permute-done.10.got_ref
  32.8 0.2 shard_map.57
  33.0 1.6 %collective-permute-start.11 = (s16[8,12672]{1,0:T(8,128)(2,1)S(1)}, s16[8,12672]{1,0:T(8,128)(2,1)S(1)}, u32[]{:S(2)}, u32[]{:S(2)}) collective-permute-start(s16[8,12672]{1,0:T(8,128)(2,1)S(1)} %get-tuple-element.80), channel_id=1, source_target_pairs={{0,2},{2,0},{1,3},{3,1},{4,6},{6,4},{5,7},{7,5},{8,10},{10,8},{9,1... | collective-permute-start | bytes 608264 | tf_op jit(solution)/shard_map/ppermute | solution.py:302
  34.6 4.8 %collective-permute-done.9.refs_1_ = s16[8,14080]{1,0:T(8,128)(2,1)S(1)} collective-permute-done((s16[8,14080]{1,0:T(8,128)(2,1)S(1)}, s16[8,14080]{1,0:T(8,128)(2,1)S(1)}, u32[]{:S(2)}, u32[]{:S(2)}) %collective-permute-start.9) | collective-permute-done | bytes 225312 | tf_op jit(solution)/shard_map/ppermute | solution.py:302
  39.4 0.4 shard_map.55
  39.9 3.1 %collective-permute-done.11.refs_2_ = s16[8,12672]{1,0:T(8,128)(2,1)S(1)} collective-permute-done((s16[8,12672]{1,0:T(8,128)(2,1)S(1)}, s16[8,12672]{1,0:T(8,128)(2,1)S(1)}, u32[]{:S(2)}, u32[]{:S(2)}) %collective-permute-start.11) | collective-permute-done | bytes 202784 | tf_op jit(solution)/shard_map/ppermute | solution.py:302
  43.0 0.4 shard_map.58
  43.4 2.0 %collective-permute-start.14 = (f32[2,128]{1,0:T(2,128)S(1)}, f32[2,128]{1,0:T(2,128)S(1)}, u32[]{:S(2)}, u32[]{:S(2)}) collective-permute-start(f32[2,128]{1,0:T(2,128)S(1)} %get-tuple-element.82.refs_2_), channel_id=1, source_target_pairs={{0,12},{4,8},{8,4},{12,0},{1,13},{5,9},{9,5},{13,1},{2,14},{6,10},... | collective-permute-start | bytes 3080 | tf_op jit(solution)/shard_map/ppermute | solution.py:466
  45.3 0.0 collective-permute-start.13
  45.3 2.5 %collective-permute-start.12 = (f32[2,128]{1,0:T(2,128)S(1)}, f32[2,128]{1,0:T(2,128)S(1)}, u32[]{:S(2)}, u32[]{:S(2)}) collective-permute-start(f32[2,128]{1,0:T(2,128)S(1)} %get-tuple-element.82.refs_2_), channel_id=1, source_target_pairs={{0,4},{4,0},{8,12},{12,8},{1,5},{5,1},{9,13},{13,9},{2,6},{6,2},{1... | collective-permute-start | bytes 3080 | tf_op jit(solution)/shard_map/ppermute | solution.py:466
  47.8 1.0 %collective-permute-done.14.refs_5_ = f32[2,128]{1,0:T(2,128)S(1)} collective-permute-done((f32[2,128]{1,0:T(2,128)S(1)}, f32[2,128]{1,0:T(2,128)S(1)}, u32[]{:S(2)}, u32[]{:S(2)}) %collective-permute-start.14) | collective-permute-done | bytes 1056 | tf_op jit(solution)/shard_map/ppermute | solution.py:466
  48.8 1.0 %collective-permute-done.13.refs_4_ = f32[2,128]{1,0:T(2,128)S(1)} collective-permute-done((f32[2,128]{1,0:T(2,128)S(1)}, f32[2,128]{1,0:T(2,128)S(1)}, u32[]{:S(2)}, u32[]{:S(2)}) %collective-permute-start.13) | collective-permute-done | bytes 1056 | tf_op jit(solution)/shard_map/ppermute | solution.py:466
  49.8 0.0 collective-permute-done.12.refs_3_
  49.8 1.2 %shard_map.59 = f32[44,4752]{1,0:T(8,128)} custom-call(f32[48,2560]{1,0:T(8,128)S(1)} %get-tuple-element.73.refs_0_, f32[48,2304]{1,0:T(8,128)S(1)} %get-tuple-element.81.refs_1_, f32[2,128]{1,0:T(2,128)S(1)} %get-tuple-element.82.refs_2_, f32[2,128]{1,0:T(2,128)S(1)} %collective-permute-done.12.refs_3_, f32[2,128]{1,0:T(2,128)S(1)} %collective-permute-done.13.refs_4_, ...), custom_call_target="tpu_custom_call" | custom-call | tf_op jit(solution)/shard_map/pallas_call | solution.py:470
  (4 shorter events, 0.1 us)
Async XLA Ops:
  1.4 1.3 %collective-permute-start.3 = (f32[2,64]{1,0:T(2,128)S(1)}, f32[2,64]{1,0:T(2,128)S(1)}, u32[]{:S(2)}, u32[]{:S(2)}) collective-permute-start(f32[2,64]{1,0:T(2,128)S(1)} %get-tuple-element.49), channel_id=1, source_target_pairs={{0,1},{1,0},{2,3},{3,2},{4,5},{5,4},{6,7},{7,6},{8,9},{9,8},{10,11... | collective-permute-start | bytes 1544 | tf_op jit(solution)/shard_map/ppermute | solution.py:302
  2.7 4.4 %collective-permute-start.4 = (f32[2,64]{1,0:T(2,128)S(1)}, f32[2,64]{1,0:T(2,128)S(1)}, u32[]{:S(2)}, u32[]{:S(2)}) collective-permute-start(f32[2,64]{1,0:T(2,128)S(1)} %add.6), channel_id=1, source_target_pairs={{0,2},{2,0},{1,3},{3,1},{4,6},{6,4},{5,7},{7,5},{8,10},{10,8},{9,1... | collective-permute-start | bytes 1544 | tf_op jit(solution)/shard_map/ppermute | solution.py:302
  7.4 8.7 %collective-permute-start.5 = (bf16[16,6656]{1,0:T(8,128)(2,1)S(1)}, bf16[16,6656]{1,0:T(8,128)(2,1)S(1)}, u32[]{:S(2)}, u32[]{:S(2)}) collective-permute-start(bf16[16,6656]{1,0:T(8,128)(2,1)S(1)} %get-tuple-element.65.refs_0_), channel_id=1, source_target_pairs={{0,4},{4,8},{8,12},{12,0},{1,5},{5,9},{9,13},{13,1},{2,6},{6,10},{... | collective-permute-start | bytes 638984 | tf_op jit(solution)/shard_map/ppermute | solution.py:302
  13.2 9.1 %collective-permute-start.6 = (bf16[16,6656]{1,0:T(8,128)(2,1)S(1)}, bf16[16,6656]{1,0:T(8,128)(2,1)S(1)}, u32[]{:S(2)}, u32[]{:S(2)}) collective-permute-start(bf16[16,6656]{1,0:T(8,128)(2,1)S(1)} %get-tuple-element.65.refs_0_), channel_id=1, source_target_pairs={{0,12},{4,0},{8,4},{12,8},{1,13},{5,1},{9,5},{13,9},{2,14},{6,2},{... | collective-permute-start | bytes 638984 | tf_op jit(solution)/shard_map/ppermute | solution.py:302
  16.2 9.6 %collective-permute-start.7 = (bf16[16,6656]{1,0:T(8,128)(2,1)S(1)}, bf16[16,6656]{1,0:T(8,128)(2,1)S(1)}, u32[]{:S(2)}, u32[]{:S(2)}) collective-permute-start(bf16[16,6656]{1,0:T(8,128)(2,1)S(1)} %collective-permute-done.5.refs_1_), channel_id=1, source_target_pairs={{0,4},{4,8},{8,12},{12,0},{1,5},{5,9},{9,13},{13,1},{2,6},{6,10},{... | collective-permute-start | bytes 638984 | tf_op jit(solution)/shard_map/ppermute | solution.py:302
  28.1 2.6 %collective-permute-start.8 = (f32[96,2560]{1,0:T(8,128)S(1)}, f32[96,2560]{1,0:T(8,128)S(1)}, u32[]{:S(2)}, u32[]{:S(2)}) collective-permute-start(f32[96,2560]{1,0:T(8,128)S(1)} %get-tuple-element.70), channel_id=1, source_target_pairs={{0,1},{1,0},{2,3},{3,2},{4,5},{5,4},{6,7},{7,6},{8,9},{9,8},{10,11... | collective-permute-start | bytes 2949128 | tf_op jit(solution)/shard_map/ppermute | solution.py:302
  30.2 2.6 %collective-permute-start.10 = (f32[96,2304]{1,0:T(8,128)S(1)}, f32[96,2304]{1,0:T(8,128)S(1)}, u32[]{:S(2)}, u32[]{:S(2)}) collective-permute-start(f32[96,2304]{1,0:T(8,128)S(1)} %get-tuple-element.78), channel_id=1, source_target_pairs={{0,1},{1,0},{2,3},{3,2},{4,5},{5,4},{6,7},{7,6},{8,9},{9,8},{10,11... | collective-permute-start | bytes 2654216 | tf_op jit(solution)/shard_map/ppermute | solution.py:302
  31.0 8.4 %collective-permute-start.9 = (s16[8,14080]{1,0:T(8,128)(2,1)S(1)}, s16[8,14080]{1,0:T(8,128)(2,1)S(1)}, u32[]{:S(2)}, u32[]{:S(2)}) collective-permute-start(s16[8,14080]{1,0:T(8,128)(2,1)S(1)} %get-tuple-element.72), channel_id=1, source_target_pairs={{0,2},{2,0},{1,3},{3,1},{4,6},{6,4},{5,7},{7,5},{8,10},{10,8},{9,1... | collective-permute-start | bytes 675848 | tf_op jit(solution)/shard_map/ppermute | solution.py:302
  33.0 9.9 %collective-permute-start.11 = (s16[8,12672]{1,0:T(8,128)(2,1)S(1)}, s16[8,12672]{1,0:T(8,128)(2,1)S(1)}, u32[]{:S(2)}, u32[]{:S(2)}) collective-permute-start(s16[8,12672]{1,0:T(8,128)(2,1)S(1)} %get-tuple-element.80), channel_id=1, source_target_pairs={{0,2},{2,0},{1,3},{3,1},{4,6},{6,4},{5,7},{7,5},{8,10},{10,8},{9,1... | collective-permute-start | bytes 608264 | tf_op jit(solution)/shard_map/ppermute | solution.py:302
  43.4 5.4 %collective-permute-start.14 = (f32[2,128]{1,0:T(2,128)S(1)}, f32[2,128]{1,0:T(2,128)S(1)}, u32[]{:S(2)}, u32[]{:S(2)}) collective-permute-start(f32[2,128]{1,0:T(2,128)S(1)} %get-tuple-element.82.refs_2_), channel_id=1, source_target_pairs={{0,12},{4,8},{8,4},{12,0},{1,13},{5,9},{9,5},{13,1},{2,14},{6,10},... | collective-permute-start | bytes 3080 | tf_op jit(solution)/shard_map/ppermute | solution.py:466
  45.3 4.5 %collective-permute-start.13 = (f32[2,128]{1,0:T(2,128)S(1)}, f32[2,128]{1,0:T(2,128)S(1)}, u32[]{:S(2)}, u32[]{:S(2)}) collective-permute-start(f32[2,128]{1,0:T(2,128)S(1)} %get-tuple-element.82.refs_2_), channel_id=1, source_target_pairs={{0,8},{4,12},{8,0},{12,4},{1,9},{5,13},{9,1},{13,5},{2,10},{6,14},... | collective-permute-start | bytes 3080 | tf_op jit(solution)/shard_map/ppermute | solution.py:466
  45.3 4.5 %collective-permute-start.12 = (f32[2,128]{1,0:T(2,128)S(1)}, f32[2,128]{1,0:T(2,128)S(1)}, u32[]{:S(2)}, u32[]{:S(2)}) collective-permute-start(f32[2,128]{1,0:T(2,128)S(1)} %get-tuple-element.82.refs_2_), channel_id=1, source_target_pairs={{0,4},{4,0},{8,12},{12,8},{1,5},{5,1},{9,13},{13,9},{2,6},{6,2},{1... | collective-permute-start | bytes 3080 | tf_op jit(solution)/shard_map/ppermute | solution.py:466

commit v7 on v6

--- a/solution.py
+++ b/solution.py
@@ -12,7 +12,7 @@
 TILE = 256
 LANES = 128
 MIB = 1 << 20
-LOADS = ((1280,), (1216,))
+LOADS = ((768,), (1728,))
 SLOTS = 5
 CHUNKS = (2496,)
 ROWS = 8
@@ -463,7 +463,7 @@
         guided.append(chunk)
     if n_z & (n_z - 1) == 0:
         all_stats = [stats] + [
-            lax.ppermute(stats, "vocab", [(i, i ^ far) for i in range(n_z)]) for far in range(1, n_z)
+            lax.ppermute(stats, "vocab", [(i, i ^ far) for i in range(n_z)]) for far in sorted(range(1, n_z), key=lambda far: [0,1,3,2][far % 4])
         ]
     else:
         all_stats = [stats] + [shifted(stats, "vocab", s) for s in range(1, n_z)]

time: 51.3 us -> 50.8 us (level)
  starting transfers between devices: 15.8 us -> 14.9 us
    ppermute x3, waiting for transfers between devices: 1.98 us -> 2.97 us  [per_device(): lax.ppermute(stats, 'vocab', [(i, i ^ far) for i in range(n_z)])]
    ppermute x3, starting transfers between devices: 4.45 us -> 3.55 us  [per_device(): lax.ppermute(stats, 'vocab', [(i, i ^ far) for i in range(n_z)])]
    ppermute x9, waiting for transfers between devices: 13.8 us -> 13.1 us  [shifted(): lax.ppermute(value, axis, [(i, (i + by) % size) for i in range(size)])]
  transfers between devices with their start and end apart: 12 -> 12, of which waited for: 9 -> 9; matrix products, arithmetic and copies ran while one was open for 0% -> 0% of each run, Pallas kernels for 25% -> 26%
where the time goes in v7:
time: 50.8 us; the launch traced here: 50.7 us
  Pallas kernels  18.7 us (37%)
  waiting for transfers between devices  16.1 us (32%)
  starting transfers between devices  14.9 us (29%)
  between operations  0.93 us (2%)
    pallas_call x12, Pallas kernels, call(): pl.pallas_call(body, out_shape=[pltpu.VMEM(shape, dtype) for shape, dtype...  16.9 us
    ppermute x9, waiting for transfers between devices, shifted(): lax.ppermute(value, axis, [(i, (i + by) % size) for i in range(size)])  13.1 us
    ppermute x9, starting transfers between devices, shifted(): lax.ppermute(value, axis, [(i, (i + by) % size) for i in range(size)])  11.3 us
    ppermute x3, starting transfers between devices, per_device(): lax.ppermute(stats, 'vocab', [(i, i ^ far) for i in range(n_z)])  3.55 us
    ppermute x3, waiting for transfers between devices, per_device(): lax.ppermute(stats, 'vocab', [(i, i ^ far) for i in range(n_z)])  2.97 us
    pallas_call x1, Pallas kernels, per_device(): pl.pallas_call(functools.partial(final_kernel, [size for _, size in chunk...  1.16 us
  transfers between devices with their start and end apart: 12, of which 9 were waited for; matrix products, arithmetic and copies ran while one was open for 0% of the time, Pallas kernels for 26%

profile of v7, /device:TPU:0, one launch (start us, length us, event | category | flops | bytes accessed | tf_op | source)
XLA Modules:
  0.0 50.7 jit_solution(10273181087059786175)
XLA Ops:
  0.0 1.4 %shard_map.46 = (bf16[2,64,2048]{2,1,0:T(8,128)(2,1)S(1)}, f32[2,64]{1,0:T(2,128)S(1)}, s32[1,176]{1,0:T(1,128)S(1)}) custom-call(bf16[2,64,2048]{2,1,0:T(8,128)(2,1)} %hidden_far.1, f32[1,2048]{1,0:T(1,128)} %bitcast.6, s32[1,176]{1,0:T(1,128)} %bitcast.7), custom_call_target="tpu_custom_call" | custom-call | tf_op jit(solution)/shard_map/pallas_call | solution.py:32
  1.4 0.5 %collective-permute-start.3 = (f32[2,64]{1,0:T(2,128)S(1)}, f32[2,64]{1,0:T(2,128)S(1)}, u32[]{:S(2)}, u32[]{:S(2)}) collective-permute-start(f32[2,64]{1,0:T(2,128)S(1)} %get-tuple-element.49), channel_id=1, source_target_pairs={{0,1},{1,0},{2,3},{3,2},{4,5},{5,4},{6,7},{7,6},{8,9},{9,8},{10,11... | collective-permute-start | bytes 1544 | tf_op jit(solution)/shard_map/ppermute | solution.py:302
  1.9 0.8 %collective-permute-done.3 = f32[2,64]{1,0:T(2,128)S(1)} collective-permute-done((f32[2,64]{1,0:T(2,128)S(1)}, f32[2,64]{1,0:T(2,128)S(1)}, u32[]{:S(2)}, u32[]{:S(2)}) %collective-permute-start.3) | collective-permute-done | bytes 544 | tf_op jit(solution)/shard_map/ppermute | solution.py:302
  2.7 2.8 %collective-permute-start.4 = (f32[2,64]{1,0:T(2,128)S(1)}, f32[2,64]{1,0:T(2,128)S(1)}, u32[]{:S(2)}, u32[]{:S(2)}) collective-permute-start(f32[2,64]{1,0:T(2,128)S(1)} %add.6), channel_id=1, source_target_pairs={{0,2},{2,0},{1,3},{3,1},{4,6},{6,4},{5,7},{7,5},{8,10},{10,8},{9,1... | collective-permute-start | bytes 1544 | tf_op jit(solution)/shard_map/ppermute | solution.py:302
  5.5 0.7 %shard_map.47 = (bf16[64,64]{1,0:T(8,128)(2,1)S(1)}, s32[1,1]{1,0:T(1,128)}) custom-call(s32[1,176]{1,0:T(1,128)S(1)} %get-tuple-element.52.positions_ref), custom_call_target="tpu_custom_call" | custom-call | tf_op jit(solution)/shard_map/pallas_call | solution.py:348
  6.2 0.9 %collective-permute-done.4 = f32[2,64]{1,0:T(2,128)S(1)} collective-permute-done((f32[2,64]{1,0:T(2,128)S(1)}, f32[2,64]{1,0:T(2,128)S(1)}, u32[]{:S(2)}, u32[]{:S(2)}) %collective-permute-start.4) | collective-permute-done | bytes 544 | tf_op jit(solution)/shard_map/ppermute | solution.py:302
  7.1 0.3 shard_map.48
  7.4 2.2 %collective-permute-start.5 = (bf16[16,6656]{1,0:T(8,128)(2,1)S(1)}, bf16[16,6656]{1,0:T(8,128)(2,1)S(1)}, u32[]{:S(2)}, u32[]{:S(2)}) collective-permute-start(bf16[16,6656]{1,0:T(8,128)(2,1)S(1)} %get-tuple-element.65.refs_0_), channel_id=1, source_target_pairs={{0,4},{4,8},{8,12},{12,0},{1,5},{5,9},{9,13},{13,1},{2,6},{6,10},{... | collective-permute-start | bytes 638984 | tf_op jit(solution)/shard_map/ppermute | solution.py:302
  10.3 2.3 %shard_map.50.refs_0_ = bf16[2048,768]{1,0:T(8,128)(2,1)S(1)} custom-call(bf16[4752,2048]{1,0:T(8,128)(2,1)} %bitcast.4), custom_call_target="tpu_custom_call" | custom-call | bytes 3145728 | tf_op jit(solution)/shard_map/pallas_call | solution.py:32
  12.5 2.1 %collective-permute-start.6 = (bf16[16,6656]{1,0:T(8,128)(2,1)S(1)}, bf16[16,6656]{1,0:T(8,128)(2,1)S(1)}, u32[]{:S(2)}, u32[]{:S(2)}) collective-permute-start(bf16[16,6656]{1,0:T(8,128)(2,1)S(1)} %get-tuple-element.65.refs_0_), channel_id=1, source_target_pairs={{0,12},{4,0},{8,4},{12,8},{1,13},{5,1},{9,5},{13,9},{2,14},{6,2},{... | collective-permute-start | bytes 638984 | tf_op jit(solution)/shard_map/ppermute | solution.py:302
  14.6 1.6 %collective-permute-done.5.refs_1_ = bf16[16,6656]{1,0:T(8,128)(2,1)S(1)} collective-permute-done((bf16[16,6656]{1,0:T(8,128)(2,1)S(1)}, bf16[16,6656]{1,0:T(8,128)(2,1)S(1)}, u32[]{:S(2)}, u32[]{:S(2)}) %collective-permute-start.5) | collective-permute-done | bytes 213024 | tf_op jit(solution)/shard_map/ppermute | solution.py:302
  16.2 0.0 collective-permute-start.7
  16.2 0.1 shard_map.49
  16.4 6.7 %shard_map.51 = (bf16[2048,1728]{1,0:T(8,128)(2,1)S(1)}, bf16[2048,2256]{1,0:T(8,128)(2,1)S(1)}) custom-call(bf16[4752,2048]{1,0:T(8,128)(2,1)} %bitcast.5), custom_call_target="tpu_custom_call" | custom-call | bytes 16318464 | tf_op jit(solution)/shard_map/pallas_call | solution.py:32
  23.1 0.0 collective-permute-done.6.refs_2_
  23.1 0.4 shard_map.52.early_ref
  23.5 1.7 %collective-permute-done.7.block_ref = bf16[16,6656]{1,0:T(8,128)(2,1)S(1)} collective-permute-done((bf16[16,6656]{1,0:T(8,128)(2,1)S(1)}, bf16[16,6656]{1,0:T(8,128)(2,1)S(1)}, u32[]{:S(2)}, u32[]{:S(2)}) %collective-permute-start.7) | collective-permute-done | bytes 213024 | tf_op jit(solution)/shard_map/ppermute | solution.py:302
  25.2 2.4 %shard_map.53 = (bf16[192,2048]{1,0:T(8,128)(2,1)S(1)}, f32[96,2560]{1,0:T(8,128)S(1)}, f32[96,2560]{1,0:T(8,128)S(1)}) custom-call(bf16[192,64]{1,0:T(8,128)(2,1)S(1)} %get-tuple-element.63.chooser_ref, bf16[192,2048]{1,0:T(8,128)(2,1)S(1)} %shard_map.52.early_ref, bf16[16,6656]{1,0:T(8,128)(2,1)S(1)} %collective-permute-done.7.block_ref, ...), custom_call_target="tpu_custom_call" | custom-call | flops 1962934272 | bytes 10223616 | tf_op jit(solution)/shard_map/pallas_call | solution.py:32
  27.6 0.1 collective-permute-start.8
  27.6 2.0 %shard_map.56 = (f32[96,2304]{1,0:T(8,128)S(1)}, f32[96,2304]{1,0:T(8,128)S(1)}) custom-call(bf16[192,2048]{1,0:T(8,128)(2,1)S(1)} %get-tuple-element.75.rows_ref, bf16[2048,2256]{1,0:T(8,128)(2,1)S(1)} %get-tuple-element.76.refs_0_), custom_call_target="tpu_custom_call" | custom-call | flops 1774190592 | bytes 9240576 | tf_op jit(solution)/shard_map/pallas_call | solution.py:32
  29.6 0.6 %collective-permute-start.10 = (f32[96,2304]{1,0:T(8,128)S(1)}, f32[96,2304]{1,0:T(8,128)S(1)}, u32[]{:S(2)}, u32[]{:S(2)}) collective-permute-start(f32[96,2304]{1,0:T(8,128)S(1)} %get-tuple-element.78), channel_id=1, source_target_pairs={{0,1},{1,0},{2,3},{3,2},{4,5},{5,4},{6,7},{7,6},{8,9},{9,8},{10,11... | collective-permute-start | bytes 2654216 | tf_op jit(solution)/shard_map/ppermute | solution.py:302
  30.2 0.0 collective-permute-done.8.got_ref
  30.2 0.2 shard_map.54
  30.4 1.6 %collective-permute-start.9 = (s16[8,14080]{1,0:T(8,128)(2,1)S(1)}, s16[8,14080]{1,0:T(8,128)(2,1)S(1)}, u32[]{:S(2)}, u32[]{:S(2)}) collective-permute-start(s16[8,14080]{1,0:T(8,128)(2,1)S(1)} %get-tuple-element.72), channel_id=1, source_target_pairs={{0,2},{2,0},{1,3},{3,1},{4,6},{6,4},{5,7},{7,5},{8,10},{10,8},{9,1... | collective-permute-start | bytes 675848 | tf_op jit(solution)/shard_map/ppermute | solution.py:302
  32.0 0.2 collective-permute-done.10.got_ref
  32.3 0.2 shard_map.57
  32.5 1.6 %collective-permute-start.11 = (s16[8,12672]{1,0:T(8,128)(2,1)S(1)}, s16[8,12672]{1,0:T(8,128)(2,1)S(1)}, u32[]{:S(2)}, u32[]{:S(2)}) collective-permute-start(s16[8,12672]{1,0:T(8,128)(2,1)S(1)} %get-tuple-element.80), channel_id=1, source_target_pairs={{0,2},{2,0},{1,3},{3,1},{4,6},{6,4},{5,7},{7,5},{8,10},{10,8},{9,1... | collective-permute-start | bytes 608264 | tf_op jit(solution)/shard_map/ppermute | solution.py:302
  34.1 4.8 %collective-permute-done.9.refs_1_ = s16[8,14080]{1,0:T(8,128)(2,1)S(1)} collective-permute-done((s16[8,14080]{1,0:T(8,128)(2,1)S(1)}, s16[8,14080]{1,0:T(8,128)(2,1)S(1)}, u32[]{:S(2)}, u32[]{:S(2)}) %collective-permute-start.9) | collective-permute-done | bytes 225312 | tf_op jit(solution)/shard_map/ppermute | solution.py:302
  38.9 0.4 shard_map.55
  39.3 3.1 %collective-permute-done.11.refs_2_ = s16[8,12672]{1,0:T(8,128)(2,1)S(1)} collective-permute-done((s16[8,12672]{1,0:T(8,128)(2,1)S(1)}, s16[8,12672]{1,0:T(8,128)(2,1)S(1)}, u32[]{:S(2)}, u32[]{:S(2)}) %collective-permute-start.11) | collective-permute-done | bytes 202784 | tf_op jit(solution)/shard_map/ppermute | solution.py:302
  42.4 0.4 shard_map.58
  42.8 1.2 %collective-permute-start.14 = (f32[2,128]{1,0:T(2,128)S(1)}, f32[2,128]{1,0:T(2,128)S(1)}, u32[]{:S(2)}, u32[]{:S(2)}) collective-permute-start(f32[2,128]{1,0:T(2,128)S(1)} %get-tuple-element.82.refs_2_), channel_id=1, source_target_pairs={{0,8},{4,12},{8,0},{12,4},{1,9},{5,13},{9,1},{13,5},{2,10},{6,14},... | collective-permute-start | bytes 3080 | tf_op jit(solution)/shard_map/ppermute | solution.py:466
  44.0 1.5 %collective-permute-start.13 = (f32[2,128]{1,0:T(2,128)S(1)}, f32[2,128]{1,0:T(2,128)S(1)}, u32[]{:S(2)}, u32[]{:S(2)}) collective-permute-start(f32[2,128]{1,0:T(2,128)S(1)} %get-tuple-element.82.refs_2_), channel_id=1, source_target_pairs={{0,12},{4,8},{8,4},{12,0},{1,13},{5,9},{9,5},{13,1},{2,14},{6,10},... | collective-permute-start | bytes 3080 | tf_op jit(solution)/shard_map/ppermute | solution.py:466
  45.5 0.9 %collective-permute-start.12 = (f32[2,128]{1,0:T(2,128)S(1)}, f32[2,128]{1,0:T(2,128)S(1)}, u32[]{:S(2)}, u32[]{:S(2)}) collective-permute-start(f32[2,128]{1,0:T(2,128)S(1)} %get-tuple-element.82.refs_2_), channel_id=1, source_target_pairs={{0,4},{4,0},{8,12},{12,8},{1,5},{5,1},{9,13},{13,9},{2,6},{6,2},{1... | collective-permute-start | bytes 3080 | tf_op jit(solution)/shard_map/ppermute | solution.py:466
  46.4 1.0 %collective-permute-done.14.refs_5_ = f32[2,128]{1,0:T(2,128)S(1)} collective-permute-done((f32[2,128]{1,0:T(2,128)S(1)}, f32[2,128]{1,0:T(2,128)S(1)}, u32[]{:S(2)}, u32[]{:S(2)}) %collective-permute-start.14) | collective-permute-done | bytes 1056 | tf_op jit(solution)/shard_map/ppermute | solution.py:466
  47.3 2.0 %collective-permute-done.13.refs_4_ = f32[2,128]{1,0:T(2,128)S(1)} collective-permute-done((f32[2,128]{1,0:T(2,128)S(1)}, f32[2,128]{1,0:T(2,128)S(1)}, u32[]{:S(2)}, u32[]{:S(2)}) %collective-permute-start.13) | collective-permute-done | bytes 1056 | tf_op jit(solution)/shard_map/ppermute | solution.py:466
  49.3 0.0 collective-permute-done.12.refs_3_
  49.3 1.2 %shard_map.59 = f32[44,4752]{1,0:T(8,128)} custom-call(f32[48,2560]{1,0:T(8,128)S(1)} %get-tuple-element.73.refs_0_, f32[48,2304]{1,0:T(8,128)S(1)} %get-tuple-element.81.refs_1_, f32[2,128]{1,0:T(2,128)S(1)} %get-tuple-element.82.refs_2_, f32[2,128]{1,0:T(2,128)S(1)} %collective-permute-done.12.refs_3_, f32[2,128]{1,0:T(2,128)S(1)} %collective-permute-done.13.refs_4_, ...), custom_call_target="tpu_custom_call" | custom-call | tf_op jit(solution)/shard_map/pallas_call | solution.py:470
  (4 shorter events, 0.1 us)
Async XLA Ops:
  1.4 1.3 %collective-permute-start.3 = (f32[2,64]{1,0:T(2,128)S(1)}, f32[2,64]{1,0:T(2,128)S(1)}, u32[]{:S(2)}, u32[]{:S(2)}) collective-permute-start(f32[2,64]{1,0:T(2,128)S(1)} %get-tuple-element.49), channel_id=1, source_target_pairs={{0,1},{1,0},{2,3},{3,2},{4,5},{5,4},{6,7},{7,6},{8,9},{9,8},{10,11... | collective-permute-start | bytes 1544 | tf_op jit(solution)/shard_map/ppermute | solution.py:302
  2.7 4.4 %collective-permute-start.4 = (f32[2,64]{1,0:T(2,128)S(1)}, f32[2,64]{1,0:T(2,128)S(1)}, u32[]{:S(2)}, u32[]{:S(2)}) collective-permute-start(f32[2,64]{1,0:T(2,128)S(1)} %add.6), channel_id=1, source_target_pairs={{0,2},{2,0},{1,3},{3,1},{4,6},{6,4},{5,7},{7,5},{8,10},{10,8},{9,1... | collective-permute-start | bytes 1544 | tf_op jit(solution)/shard_map/ppermute | solution.py:302
  7.4 8.8 %collective-permute-start.5 = (bf16[16,6656]{1,0:T(8,128)(2,1)S(1)}, bf16[16,6656]{1,0:T(8,128)(2,1)S(1)}, u32[]{:S(2)}, u32[]{:S(2)}) collective-permute-start(bf16[16,6656]{1,0:T(8,128)(2,1)S(1)} %get-tuple-element.65.refs_0_), channel_id=1, source_target_pairs={{0,4},{4,8},{8,12},{12,0},{1,5},{5,9},{9,13},{13,1},{2,6},{6,10},{... | collective-permute-start | bytes 638984 | tf_op jit(solution)/shard_map/ppermute | solution.py:302
  12.5 10.6 %collective-permute-start.6 = (bf16[16,6656]{1,0:T(8,128)(2,1)S(1)}, bf16[16,6656]{1,0:T(8,128)(2,1)S(1)}, u32[]{:S(2)}, u32[]{:S(2)}) collective-permute-start(bf16[16,6656]{1,0:T(8,128)(2,1)S(1)} %get-tuple-element.65.refs_0_), channel_id=1, source_target_pairs={{0,12},{4,0},{8,4},{12,8},{1,13},{5,1},{9,5},{13,9},{2,14},{6,2},{... | collective-permute-start | bytes 638984 | tf_op jit(solution)/shard_map/ppermute | solution.py:302
  16.2 9.0 %collective-permute-start.7 = (bf16[16,6656]{1,0:T(8,128)(2,1)S(1)}, bf16[16,6656]{1,0:T(8,128)(2,1)S(1)}, u32[]{:S(2)}, u32[]{:S(2)}) collective-permute-start(bf16[16,6656]{1,0:T(8,128)(2,1)S(1)} %collective-permute-done.5.refs_1_), channel_id=1, source_target_pairs={{0,4},{4,8},{8,12},{12,0},{1,5},{5,9},{9,13},{13,1},{2,6},{6,10},{... | collective-permute-start | bytes 638984 | tf_op jit(solution)/shard_map/ppermute | solution.py:302
  27.6 2.6 %collective-permute-start.8 = (f32[96,2560]{1,0:T(8,128)S(1)}, f32[96,2560]{1,0:T(8,128)S(1)}, u32[]{:S(2)}, u32[]{:S(2)}) collective-permute-start(f32[96,2560]{1,0:T(8,128)S(1)} %get-tuple-element.70), channel_id=1, source_target_pairs={{0,1},{1,0},{2,3},{3,2},{4,5},{5,4},{6,7},{7,6},{8,9},{9,8},{10,11... | collective-permute-start | bytes 2949128 | tf_op jit(solution)/shard_map/ppermute | solution.py:302
  29.6 2.6 %collective-permute-start.10 = (f32[96,2304]{1,0:T(8,128)S(1)}, f32[96,2304]{1,0:T(8,128)S(1)}, u32[]{:S(2)}, u32[]{:S(2)}) collective-permute-start(f32[96,2304]{1,0:T(8,128)S(1)} %get-tuple-element.78), channel_id=1, source_target_pairs={{0,1},{1,0},{2,3},{3,2},{4,5},{5,4},{6,7},{7,6},{8,9},{9,8},{10,11... | collective-permute-start | bytes 2654216 | tf_op jit(solution)/shard_map/ppermute | solution.py:302
  30.4 8.4 %collective-permute-start.9 = (s16[8,14080]{1,0:T(8,128)(2,1)S(1)}, s16[8,14080]{1,0:T(8,128)(2,1)S(1)}, u32[]{:S(2)}, u32[]{:S(2)}) collective-permute-start(s16[8,14080]{1,0:T(8,128)(2,1)S(1)} %get-tuple-element.72), channel_id=1, source_target_pairs={{0,2},{2,0},{1,3},{3,1},{4,6},{6,4},{5,7},{7,5},{8,10},{10,8},{9,1... | collective-permute-start | bytes 675848 | tf_op jit(solution)/shard_map/ppermute | solution.py:302
  32.5 9.9 %collective-permute-start.11 = (s16[8,12672]{1,0:T(8,128)(2,1)S(1)}, s16[8,12672]{1,0:T(8,128)(2,1)S(1)}, u32[]{:S(2)}, u32[]{:S(2)}) collective-permute-start(s16[8,12672]{1,0:T(8,128)(2,1)S(1)} %get-tuple-element.80), channel_id=1, source_target_pairs={{0,2},{2,0},{1,3},{3,1},{4,6},{6,4},{5,7},{7,5},{8,10},{10,8},{9,1... | collective-permute-start | bytes 608264 | tf_op jit(solution)/shard_map/ppermute | solution.py:302
  42.8 4.5 %collective-permute-start.14 = (f32[2,128]{1,0:T(2,128)S(1)}, f32[2,128]{1,0:T(2,128)S(1)}, u32[]{:S(2)}, u32[]{:S(2)}) collective-permute-start(f32[2,128]{1,0:T(2,128)S(1)} %get-tuple-element.82.refs_2_), channel_id=1, source_target_pairs={{0,8},{4,12},{8,0},{12,4},{1,9},{5,13},{9,1},{13,5},{2,10},{6,14},... | collective-permute-start | bytes 3080 | tf_op jit(solution)/shard_map/ppermute | solution.py:466
  44.0 5.4 %collective-permute-start.13 = (f32[2,128]{1,0:T(2,128)S(1)}, f32[2,128]{1,0:T(2,128)S(1)}, u32[]{:S(2)}, u32[]{:S(2)}) collective-permute-start(f32[2,128]{1,0:T(2,128)S(1)} %get-tuple-element.82.refs_2_), channel_id=1, source_target_pairs={{0,12},{4,8},{8,4},{12,0},{1,13},{5,9},{9,5},{13,1},{2,14},{6,10},... | collective-permute-start | bytes 3080 | tf_op jit(solution)/shard_map/ppermute | solution.py:466
  45.5 3.9 %collective-permute-start.12 = (f32[2,128]{1,0:T(2,128)S(1)}, f32[2,128]{1,0:T(2,128)S(1)}, u32[]{:S(2)}, u32[]{:S(2)}) collective-permute-start(f32[2,128]{1,0:T(2,128)S(1)} %get-tuple-element.82.refs_2_), channel_id=1, source_target_pairs={{0,4},{4,0},{8,12},{12,8},{1,5},{5,1},{9,13},{13,9},{2,6},{6,2},{1... | collective-permute-start | bytes 3080 | tf_op jit(solution)/shard_map/ppermute | solution.py:466

commit v8 on v7

--- a/solution.py
+++ b/solution.py
@@ -148,14 +148,16 @@
 def chooser_kernel(own, block, usual, offsets, n_z, n_x, n_c, positions_ref, early_ref, last_ref):
     z, x, c = (lax.axis_index(axis) for axis in ("vocab", "rows", "cfg"))
     rows, deep = last_ref.shape
-    segment = rows // (n_x * n_c)
+    half = rows // n_c
+    segment = -(-own // ROWS) * ROWS if tight(own, n_x) else half // n_x
     row = lax.broadcasted_iota(jnp.int32, (rows, 1), 0)
     wanted = jnp.full((rows, 1), -1, jnp.int32)
     for t in range(n_c):
         for s in range(n_x):
             owner = lax.rem(x + s, n_x) * n_c + lax.rem(c + t, n_c)
-            i = row - (t * n_x + s) * segment
-            wanted = jnp.where((i >= 0) & (i < own), owner * own + i, wanted)
+            for at, first, end in row_ranges(own, segment, n_x, s):
+                i = row - (t * half + at) + first
+                wanted = jnp.where((i >= first) & (i < end), owner * own + i, wanted)
     lane = lax.broadcasted_iota(jnp.int32, (1, early_ref.shape[1]), 1)
     held = jnp.full(lane.shape, -2, jnp.int32)
     skipped = usual // DEEP * DEEP
@@ -210,6 +212,21 @@
     multiply(start, size, rows_ref, weights_refs, keep_ref, send_ref)
 
 
+def tight(own, n_x):
+    return n_x == 2 and own % ROWS == ROWS // 2
+
+
+def half_rows(own, segment, n_x):
+    return 2 * own if tight(own, n_x) else n_x * segment
+
+
+def row_ranges(own, segment, n_x, s):
+    if not tight(own, n_x):
+        return [(s * segment, 0, own)]
+    whole = own // ROWS * ROWS
+    return [(0, 0, own)] if s == 0 else [(own, whole, own), (whole + ROWS, 0, whole)]
+
+
 def add_kernel(own, size, keep_ref, got_ref, own_ref, *out_refs):
     segment, width = own_ref.shape
     own_ref[...] = keep_ref[:segment] + got_ref[:segment]
@@ -217,16 +234,18 @@
     spare = lax.broadcasted_iota(jnp.int32, (ROWS, TILE), 1) >= size - last
     for s, out_ref in enumerate(out_refs, 1):
         for t in range(-(-own // ROWS)):
-            rows = slice(s * segment + t * ROWS, s * segment + (t + 1) * ROWS)
-            value = keep_ref[rows] + got_ref[rows]
+            half = own - t * ROWS <= ROWS // 2
+            shared = half and keep_ref.shape[0] == 2 * own
+            at = t * ROWS if shared else s * segment + t * ROWS
+            value = keep_ref[at : at + ROWS] + got_ref[at : at + ROWS]
             peak = jnp.max(jnp.abs(value), axis=1, keepdims=True)
             exponent = jnp.clip(jnp.ceil(jnp.log2(jnp.maximum(peak, 1e-30))), -90.0, 127.0)
             scaled = jnp.clip(jnp.round(value * jnp.exp2(15.0 - exponent)), -32767.0, 32767.0)
             ending = jnp.where(spare, exponent, scaled[:, last:])
             scaled = jnp.concatenate([scaled[:, :last], ending], axis=1) if last else ending
-            if own - t * ROWS <= ROWS // 2:
-                half = ROWS // 2
-                scaled = jnp.concatenate([scaled[:half, : width // 2], scaled[:half, width // 2 :]], axis=0)
+            if half:
+                kept = slice(ROWS // 2, ROWS) if shared else slice(0, ROWS // 2)
+                scaled = jnp.concatenate([scaled[kept, : width // 2], scaled[kept, width // 2 :]], axis=0)
             out_ref[:, t * width : t * width + scaled.shape[1]] = scaled.astype(jnp.int32).astype(jnp.int16)
 
 
@@ -411,7 +430,8 @@
     for step in range(n_z // 2):
         arrivals += aheads[step : step + 1] + behinds[step : step + 1]
 
-    selected, deep = n_x * n_c * segment, -(-usual // DEEP) * DEEP
+    half = half_rows(own, segment, n_x)
+    selected, deep = n_c * half, -(-usual // DEEP) * DEEP
     early_chooser, last_chooser = call(
         functools.partial(chooser_kernel, own, block, usual, offsets, n_z, n_x, n_c),
         [((selected, (n_z - 1) * deep + n_z * (block - skipped)), bf16), ((selected, deep), bf16)],
@@ -425,7 +445,6 @@
         [early_chooser, *arrivals[:-1], rest],
     )
 
-    half = n_x * segment
     chunks = cut(vocab, CHUNKS)
     parts, leaving = [], []
     for j, (start, size) in enumerate(chunks):

time: 50.8 us -> 50.7 us (level)
  no operation moved by 1% of the time
where the time goes in v8:
time: 50.7 us; the launch traced here: 50.5 us
  Pallas kernels  18.6 us (37%)
  waiting for transfers between devices  16 us (32%)
  starting transfers between devices  14.9 us (29%)
  between operations  0.93 us (2%)
    pallas_call x12, Pallas kernels, call(): pl.pallas_call(body, out_shape=[pltpu.VMEM(shape, dtype) for shape, dtype...  16.8 us
    ppermute x9, waiting for transfers between devices, shifted(): lax.ppermute(value, axis, [(i, (i + by) % size) for i in range(size)])  13.1 us
    ppermute x9, starting transfers between devices, shifted(): lax.ppermute(value, axis, [(i, (i + by) % size) for i in range(size)])  11.3 us
    ppermute x3, starting transfers between devices, per_device(): lax.ppermute(stats, 'vocab', [(i, i ^ far) for i in range(n_z)])  3.55 us
    ppermute x3, waiting for transfers between devices, per_device(): lax.ppermute(stats, 'vocab', [(i, i ^ far) for i in range(n_z)])  2.96 us
    pallas_call x1, Pallas kernels, per_device(): pl.pallas_call(functools.partial(final_kernel, [size for _, size in chunk...  1.17 us
  transfers between devices with their start and end apart: 12, of which 9 were waited for; matrix products, arithmetic and copies ran while one was open for 0% of the time, Pallas kernels for 26%

profile of v8, /device:TPU:0, one launch (start us, length us, event | category | flops | bytes accessed | tf_op | source)
XLA Modules:
  0.0 50.5 jit_solution(6585355554265015668)
XLA Ops:
  0.0 1.4 %shard_map.46 = (bf16[2,64,2048]{2,1,0:T(8,128)(2,1)S(1)}, f32[2,64]{1,0:T(2,128)S(1)}, s32[1,176]{1,0:T(1,128)S(1)}) custom-call(bf16[2,64,2048]{2,1,0:T(8,128)(2,1)} %hidden_far.1, f32[1,2048]{1,0:T(1,128)} %bitcast.6, s32[1,176]{1,0:T(1,128)} %bitcast.7), custom_call_target="tpu_custom_call" | custom-call | tf_op jit(solution)/shard_map/pallas_call | solution.py:32
  1.4 0.5 %collective-permute-start.3 = (f32[2,64]{1,0:T(2,128)S(1)}, f32[2,64]{1,0:T(2,128)S(1)}, u32[]{:S(2)}, u32[]{:S(2)}) collective-permute-start(f32[2,64]{1,0:T(2,128)S(1)} %get-tuple-element.49), channel_id=1, source_target_pairs={{0,1},{1,0},{2,3},{3,2},{4,5},{5,4},{6,7},{7,6},{8,9},{9,8},{10,11... | collective-permute-start | bytes 1544 | tf_op jit(solution)/shard_map/ppermute | solution.py:321
  1.9 0.8 %collective-permute-done.3 = f32[2,64]{1,0:T(2,128)S(1)} collective-permute-done((f32[2,64]{1,0:T(2,128)S(1)}, f32[2,64]{1,0:T(2,128)S(1)}, u32[]{:S(2)}, u32[]{:S(2)}) %collective-permute-start.3) | collective-permute-done | bytes 544 | tf_op jit(solution)/shard_map/ppermute | solution.py:321
  2.7 2.8 %collective-permute-start.4 = (f32[2,64]{1,0:T(2,128)S(1)}, f32[2,64]{1,0:T(2,128)S(1)}, u32[]{:S(2)}, u32[]{:S(2)}) collective-permute-start(f32[2,64]{1,0:T(2,128)S(1)} %add.6), channel_id=1, source_target_pairs={{0,2},{2,0},{1,3},{3,1},{4,6},{6,4},{5,7},{7,5},{8,10},{10,8},{9,1... | collective-permute-start | bytes 1544 | tf_op jit(solution)/shard_map/ppermute | solution.py:321
  5.5 0.7 %shard_map.47 = (bf16[64,64]{1,0:T(8,128)(2,1)S(1)}, s32[1,1]{1,0:T(1,128)}) custom-call(s32[1,176]{1,0:T(1,128)S(1)} %get-tuple-element.52.positions_ref), custom_call_target="tpu_custom_call" | custom-call | tf_op jit(solution)/shard_map/pallas_call | solution.py:367
  6.2 0.9 %collective-permute-done.4 = f32[2,64]{1,0:T(2,128)S(1)} collective-permute-done((f32[2,64]{1,0:T(2,128)S(1)}, f32[2,64]{1,0:T(2,128)S(1)}, u32[]{:S(2)}, u32[]{:S(2)}) %collective-permute-start.4) | collective-permute-done | bytes 544 | tf_op jit(solution)/shard_map/ppermute | solution.py:321
  7.1 0.3 shard_map.48
  7.4 2.2 %collective-permute-start.5 = (bf16[16,6656]{1,0:T(8,128)(2,1)S(1)}, bf16[16,6656]{1,0:T(8,128)(2,1)S(1)}, u32[]{:S(2)}, u32[]{:S(2)}) collective-permute-start(bf16[16,6656]{1,0:T(8,128)(2,1)S(1)} %get-tuple-element.65.refs_0_), channel_id=1, source_target_pairs={{0,4},{4,8},{8,12},{12,0},{1,5},{5,9},{9,13},{13,1},{2,6},{6,10},{... | collective-permute-start | bytes 638984 | tf_op jit(solution)/shard_map/ppermute | solution.py:321
  10.3 2.3 %shard_map.50.refs_0_ = bf16[2048,768]{1,0:T(8,128)(2,1)S(1)} custom-call(bf16[4752,2048]{1,0:T(8,128)(2,1)} %bitcast.4), custom_call_target="tpu_custom_call" | custom-call | bytes 3145728 | tf_op jit(solution)/shard_map/pallas_call | solution.py:32
  12.5 2.1 %collective-permute-start.6 = (bf16[16,6656]{1,0:T(8,128)(2,1)S(1)}, bf16[16,6656]{1,0:T(8,128)(2,1)S(1)}, u32[]{:S(2)}, u32[]{:S(2)}) collective-permute-start(bf16[16,6656]{1,0:T(8,128)(2,1)S(1)} %get-tuple-element.65.refs_0_), channel_id=1, source_target_pairs={{0,12},{4,0},{8,4},{12,8},{1,13},{5,1},{9,5},{13,9},{2,14},{6,2},{... | collective-permute-start | bytes 638984 | tf_op jit(solution)/shard_map/ppermute | solution.py:321
  14.6 1.6 %collective-permute-done.5.refs_1_ = bf16[16,6656]{1,0:T(8,128)(2,1)S(1)} collective-permute-done((bf16[16,6656]{1,0:T(8,128)(2,1)S(1)}, bf16[16,6656]{1,0:T(8,128)(2,1)S(1)}, u32[]{:S(2)}, u32[]{:S(2)}) %collective-permute-start.5) | collective-permute-done | bytes 213024 | tf_op jit(solution)/shard_map/ppermute | solution.py:321
  16.2 0.0 collective-permute-start.7
  16.2 0.1 shard_map.49
  16.4 6.7 %shard_map.51 = (bf16[2048,1728]{1,0:T(8,128)(2,1)S(1)}, bf16[2048,2256]{1,0:T(8,128)(2,1)S(1)}) custom-call(bf16[4752,2048]{1,0:T(8,128)(2,1)} %bitcast.5), custom_call_target="tpu_custom_call" | custom-call | bytes 16318464 | tf_op jit(solution)/shard_map/pallas_call | solution.py:32
  23.1 0.0 collective-permute-done.6.refs_2_
  23.1 0.4 shard_map.52.early_ref
  23.5 1.7 %collective-permute-done.7.block_ref = bf16[16,6656]{1,0:T(8,128)(2,1)S(1)} collective-permute-done((bf16[16,6656]{1,0:T(8,128)(2,1)S(1)}, bf16[16,6656]{1,0:T(8,128)(2,1)S(1)}, u32[]{:S(2)}, u32[]{:S(2)}) %collective-permute-start.7) | collective-permute-done | bytes 213024 | tf_op jit(solution)/shard_map/ppermute | solution.py:321
  25.2 2.3 %shard_map.53 = (bf16[176,2048]{1,0:T(8,128)(2,1)S(1)}, f32[88,2560]{1,0:T(8,128)S(1)}, f32[88,2560]{1,0:T(8,128)S(1)}) custom-call(bf16[176,64]{1,0:T(8,128)(2,1)S(1)} %get-tuple-element.63.chooser_ref, bf16[176,2048]{1,0:T(8,128)(2,1)S(1)} %shard_map.52.early_ref, bf16[16,6656]{1,0:T(8,128)(2,1)S(1)} %collective-permute-done.7.block_ref, ...), custom_call_target="tpu_custom_call" | custom-call | flops 1799356416 | bytes 10223616 | tf_op jit(solution)/shard_map/pallas_call | solution.py:32
  27.5 0.1 collective-permute-start.8
  27.6 2.0 %shard_map.56 = (f32[88,2304]{1,0:T(8,128)S(1)}, f32[88,2304]{1,0:T(8,128)S(1)}) custom-call(bf16[176,2048]{1,0:T(8,128)(2,1)S(1)} %get-tuple-element.75.rows_ref, bf16[2048,2256]{1,0:T(8,128)(2,1)S(1)} %get-tuple-element.76.refs_0_), custom_call_target="tpu_custom_call" | custom-call | flops 1626341376 | bytes 9240576 | tf_op jit(solution)/shard_map/pallas_call | solution.py:32
  29.6 0.6 %collective-permute-start.10 = (f32[88,2304]{1,0:T(8,128)S(1)}, f32[88,2304]{1,0:T(8,128)S(1)}, u32[]{:S(2)}, u32[]{:S(2)}) collective-permute-start(f32[88,2304]{1,0:T(8,128)S(1)} %get-tuple-element.78), channel_id=1, source_target_pairs={{0,1},{1,0},{2,3},{3,2},{4,5},{5,4},{6,7},{7,6},{8,9},{9,8},{10,11... | collective-permute-start | bytes 2433032 | tf_op jit(solution)/shard_map/ppermute | solution.py:321
  30.1 0.0 collective-permute-done.8.got_ref
  30.1 0.3 shard_map.54
  30.4 1.6 %collective-permute-start.9 = (s16[8,14080]{1,0:T(8,128)(2,1)S(1)}, s16[8,14080]{1,0:T(8,128)(2,1)S(1)}, u32[]{:S(2)}, u32[]{:S(2)}) collective-permute-start(s16[8,14080]{1,0:T(8,128)(2,1)S(1)} %get-tuple-element.72), channel_id=1, source_target_pairs={{0,2},{2,0},{1,3},{3,1},{4,6},{6,4},{5,7},{7,5},{8,10},{10,8},{9,1... | collective-permute-start | bytes 675848 | tf_op jit(solution)/shard_map/ppermute | solution.py:321
  32.0 0.1 collective-permute-done.10.got_ref
  32.1 0.2 shard_map.57
  32.3 1.6 %collective-permute-start.11 = (s16[8,12672]{1,0:T(8,128)(2,1)S(1)}, s16[8,12672]{1,0:T(8,128)(2,1)S(1)}, u32[]{:S(2)}, u32[]{:S(2)}) collective-permute-start(s16[8,12672]{1,0:T(8,128)(2,1)S(1)} %get-tuple-element.80), channel_id=1, source_target_pairs={{0,2},{2,0},{1,3},{3,1},{4,6},{6,4},{5,7},{7,5},{8,10},{10,8},{9,1... | collective-permute-start | bytes 608264 | tf_op jit(solution)/shard_map/ppermute | solution.py:321
  33.9 5.0 %collective-permute-done.9.refs_1_ = s16[8,14080]{1,0:T(8,128)(2,1)S(1)} collective-permute-done((s16[8,14080]{1,0:T(8,128)(2,1)S(1)}, s16[8,14080]{1,0:T(8,128)(2,1)S(1)}, u32[]{:S(2)}, u32[]{:S(2)}) %collective-permute-start.9) | collective-permute-done | bytes 225312 | tf_op jit(solution)/shard_map/ppermute | solution.py:321
  38.8 0.4 shard_map.55
  39.3 3.0 %collective-permute-done.11.refs_2_ = s16[8,12672]{1,0:T(8,128)(2,1)S(1)} collective-permute-done((s16[8,12672]{1,0:T(8,128)(2,1)S(1)}, s16[8,12672]{1,0:T(8,128)(2,1)S(1)}, u32[]{:S(2)}, u32[]{:S(2)}) %collective-permute-start.11) | collective-permute-done | bytes 202784 | tf_op jit(solution)/shard_map/ppermute | solution.py:321
  42.3 0.4 shard_map.58
  42.7 1.1 %collective-permute-start.14 = (f32[2,128]{1,0:T(2,128)S(1)}, f32[2,128]{1,0:T(2,128)S(1)}, u32[]{:S(2)}, u32[]{:S(2)}) collective-permute-start(f32[2,128]{1,0:T(2,128)S(1)} %get-tuple-element.82.refs_2_), channel_id=1, source_target_pairs={{0,8},{4,12},{8,0},{12,4},{1,9},{5,13},{9,1},{13,5},{2,10},{6,14},... | collective-permute-start | bytes 3080 | tf_op jit(solution)/shard_map/ppermute | solution.py:485
  43.8 1.5 %collective-permute-start.13 = (f32[2,128]{1,0:T(2,128)S(1)}, f32[2,128]{1,0:T(2,128)S(1)}, u32[]{:S(2)}, u32[]{:S(2)}) collective-permute-start(f32[2,128]{1,0:T(2,128)S(1)} %get-tuple-element.82.refs_2_), channel_id=1, source_target_pairs={{0,12},{4,8},{8,4},{12,0},{1,13},{5,9},{9,5},{13,1},{2,14},{6,10},... | collective-permute-start | bytes 3080 | tf_op jit(solution)/shard_map/ppermute | solution.py:485
  45.3 0.9 %collective-permute-start.12 = (f32[2,128]{1,0:T(2,128)S(1)}, f32[2,128]{1,0:T(2,128)S(1)}, u32[]{:S(2)}, u32[]{:S(2)}) collective-permute-start(f32[2,128]{1,0:T(2,128)S(1)} %get-tuple-element.82.refs_2_), channel_id=1, source_target_pairs={{0,4},{4,0},{8,12},{12,8},{1,5},{5,1},{9,13},{13,9},{2,6},{6,2},{1... | collective-permute-start | bytes 3080 | tf_op jit(solution)/shard_map/ppermute | solution.py:485
  46.2 1.0 %collective-permute-done.14.refs_5_ = f32[2,128]{1,0:T(2,128)S(1)} collective-permute-done((f32[2,128]{1,0:T(2,128)S(1)}, f32[2,128]{1,0:T(2,128)S(1)}, u32[]{:S(2)}, u32[]{:S(2)}) %collective-permute-start.14) | collective-permute-done | bytes 1056 | tf_op jit(solution)/shard_map/ppermute | solution.py:485
  47.2 2.0 %collective-permute-done.13.refs_4_ = f32[2,128]{1,0:T(2,128)S(1)} collective-permute-done((f32[2,128]{1,0:T(2,128)S(1)}, f32[2,128]{1,0:T(2,128)S(1)}, u32[]{:S(2)}, u32[]{:S(2)}) %collective-permute-start.13) | collective-permute-done | bytes 1056 | tf_op jit(solution)/shard_map/ppermute | solution.py:485
  49.2 0.0 collective-permute-done.12.refs_3_
  49.2 1.2 %shard_map.59 = f32[44,4752]{1,0:T(8,128)} custom-call(f32[48,2560]{1,0:T(8,128)S(1)} %get-tuple-element.73.refs_0_, f32[48,2304]{1,0:T(8,128)S(1)} %get-tuple-element.81.refs_1_, f32[2,128]{1,0:T(2,128)S(1)} %get-tuple-element.82.refs_2_, f32[2,128]{1,0:T(2,128)S(1)} %collective-permute-done.12.refs_3_, f32[2,128]{1,0:T(2,128)S(1)} %collective-permute-done.13.refs_4_, ...), custom_call_target="tpu_custom_call" | custom-call | tf_op jit(solution)/shard_map/pallas_call | solution.py:489
  (4 shorter events, 0.1 us)
Async XLA Ops:
  1.4 1.3 %collective-permute-start.3 = (f32[2,64]{1,0:T(2,128)S(1)}, f32[2,64]{1,0:T(2,128)S(1)}, u32[]{:S(2)}, u32[]{:S(2)}) collective-permute-start(f32[2,64]{1,0:T(2,128)S(1)} %get-tuple-element.49), channel_id=1, source_target_pairs={{0,1},{1,0},{2,3},{3,2},{4,5},{5,4},{6,7},{7,6},{8,9},{9,8},{10,11... | collective-permute-start | bytes 1544 | tf_op jit(solution)/shard_map/ppermute | solution.py:321
  2.7 4.4 %collective-permute-start.4 = (f32[2,64]{1,0:T(2,128)S(1)}, f32[2,64]{1,0:T(2,128)S(1)}, u32[]{:S(2)}, u32[]{:S(2)}) collective-permute-start(f32[2,64]{1,0:T(2,128)S(1)} %add.6), channel_id=1, source_target_pairs={{0,2},{2,0},{1,3},{3,1},{4,6},{6,4},{5,7},{7,5},{8,10},{10,8},{9,1... | collective-permute-start | bytes 1544 | tf_op jit(solution)/shard_map/ppermute | solution.py:321
  7.4 8.8 %collective-permute-start.5 = (bf16[16,6656]{1,0:T(8,128)(2,1)S(1)}, bf16[16,6656]{1,0:T(8,128)(2,1)S(1)}, u32[]{:S(2)}, u32[]{:S(2)}) collective-permute-start(bf16[16,6656]{1,0:T(8,128)(2,1)S(1)} %get-tuple-element.65.refs_0_), channel_id=1, source_target_pairs={{0,4},{4,8},{8,12},{12,0},{1,5},{5,9},{9,13},{13,1},{2,6},{6,10},{... | collective-permute-start | bytes 638984 | tf_op jit(solution)/shard_map/ppermute | solution.py:321
  12.5 10.6 %collective-permute-start.6 = (bf16[16,6656]{1,0:T(8,128)(2,1)S(1)}, bf16[16,6656]{1,0:T(8,128)(2,1)S(1)}, u32[]{:S(2)}, u32[]{:S(2)}) collective-permute-start(bf16[16,6656]{1,0:T(8,128)(2,1)S(1)} %get-tuple-element.65.refs_0_), channel_id=1, source_target_pairs={{0,12},{4,0},{8,4},{12,8},{1,13},{5,1},{9,5},{13,9},{2,14},{6,2},{... | collective-permute-start | bytes 638984 | tf_op jit(solution)/shard_map/ppermute | solution.py:321
  16.2 9.0 %collective-permute-start.7 = (bf16[16,6656]{1,0:T(8,128)(2,1)S(1)}, bf16[16,6656]{1,0:T(8,128)(2,1)S(1)}, u32[]{:S(2)}, u32[]{:S(2)}) collective-permute-start(bf16[16,6656]{1,0:T(8,128)(2,1)S(1)} %collective-permute-done.5.refs_1_), channel_id=1, source_target_pairs={{0,4},{4,8},{8,12},{12,0},{1,5},{5,9},{9,13},{13,1},{2,6},{6,10},{... | collective-permute-start | bytes 638984 | tf_op jit(solution)/shard_map/ppermute | solution.py:321
  27.5 2.6 %collective-permute-start.8 = (f32[88,2560]{1,0:T(8,128)S(1)}, f32[88,2560]{1,0:T(8,128)S(1)}, u32[]{:S(2)}, u32[]{:S(2)}) collective-permute-start(f32[88,2560]{1,0:T(8,128)S(1)} %get-tuple-element.70), channel_id=1, source_target_pairs={{0,1},{1,0},{2,3},{3,2},{4,5},{5,4},{6,7},{7,6},{8,9},{9,8},{10,11... | collective-permute-start | bytes 2703368 | tf_op jit(solution)/shard_map/ppermute | solution.py:321
  29.6 2.5 %collective-permute-start.10 = (f32[88,2304]{1,0:T(8,128)S(1)}, f32[88,2304]{1,0:T(8,128)S(1)}, u32[]{:S(2)}, u32[]{:S(2)}) collective-permute-start(f32[88,2304]{1,0:T(8,128)S(1)} %get-tuple-element.78), channel_id=1, source_target_pairs={{0,1},{1,0},{2,3},{3,2},{4,5},{5,4},{6,7},{7,6},{8,9},{9,8},{10,11... | collective-permute-start | bytes 2433032 | tf_op jit(solution)/shard_map/ppermute | solution.py:321
  30.4 8.4 %collective-permute-start.9 = (s16[8,14080]{1,0:T(8,128)(2,1)S(1)}, s16[8,14080]{1,0:T(8,128)(2,1)S(1)}, u32[]{:S(2)}, u32[]{:S(2)}) collective-permute-start(s16[8,14080]{1,0:T(8,128)(2,1)S(1)} %get-tuple-element.72), channel_id=1, source_target_pairs={{0,2},{2,0},{1,3},{3,1},{4,6},{6,4},{5,7},{7,5},{8,10},{10,8},{9,1... | collective-permute-start | bytes 675848 | tf_op jit(solution)/shard_map/ppermute | solution.py:321
  32.3 9.9 %collective-permute-start.11 = (s16[8,12672]{1,0:T(8,128)(2,1)S(1)}, s16[8,12672]{1,0:T(8,128)(2,1)S(1)}, u32[]{:S(2)}, u32[]{:S(2)}) collective-permute-start(s16[8,12672]{1,0:T(8,128)(2,1)S(1)} %get-tuple-element.80), channel_id=1, source_target_pairs={{0,2},{2,0},{1,3},{3,1},{4,6},{6,4},{5,7},{7,5},{8,10},{10,8},{9,1... | collective-permute-start | bytes 608264 | tf_op jit(solution)/shard_map/ppermute | solution.py:321
  42.7 4.5 %collective-permute-start.14 = (f32[2,128]{1,0:T(2,128)S(1)}, f32[2,128]{1,0:T(2,128)S(1)}, u32[]{:S(2)}, u32[]{:S(2)}) collective-permute-start(f32[2,128]{1,0:T(2,128)S(1)} %get-tuple-element.82.refs_2_), channel_id=1, source_target_pairs={{0,8},{4,12},{8,0},{12,4},{1,9},{5,13},{9,1},{13,5},{2,10},{6,14},... | collective-permute-start | bytes 3080 | tf_op jit(solution)/shard_map/ppermute | solution.py:485
  43.8 5.4 %collective-permute-start.13 = (f32[2,128]{1,0:T(2,128)S(1)}, f32[2,128]{1,0:T(2,128)S(1)}, u32[]{:S(2)}, u32[]{:S(2)}) collective-permute-start(f32[2,128]{1,0:T(2,128)S(1)} %get-tuple-element.82.refs_2_), channel_id=1, source_target_pairs={{0,12},{4,8},{8,4},{12,0},{1,13},{5,9},{9,5},{13,1},{2,14},{6,10},... | collective-permute-start | bytes 3080 | tf_op jit(solution)/shard_map/ppermute | solution.py:485
  45.3 3.9 %collective-permute-start.12 = (f32[2,128]{1,0:T(2,128)S(1)}, f32[2,128]{1,0:T(2,128)S(1)}, u32[]{:S(2)}, u32[]{:S(2)}) collective-permute-start(f32[2,128]{1,0:T(2,128)S(1)} %get-tuple-element.82.refs_2_), channel_id=1, source_target_pairs={{0,4},{4,0},{8,12},{12,8},{1,5},{5,1},{9,13},{13,9},{2,6},{6,2},{1... | collective-permute-start | bytes 3080 | tf_op jit(solution)/shard_map/ppermute | solution.py:485

commit v9 on v8

--- a/solution.py
+++ b/solution.py
@@ -12,7 +12,7 @@
 TILE = 256
 LANES = 128
 MIB = 1 << 20
-LOADS = ((768,), (1728,))
+LOADS = ((512,), (1984,))
 SLOTS = 5
 CHUNKS = (2496,)
 ROWS = 8
@@ -52,10 +52,10 @@
     return jnp.sum(jnp.where(diagonal(column.shape[0]), column, 0.0), axis=0, keepdims=True)
 
 
-def squares_kernel(hidden_far, gain_far, places_far, normed_ref, out_ref, places_ref, hidden_ref, gain_ref, sems):
-    copies = [
-        pltpu.make_async_copy(hidden_far.at[0], hidden_ref.at[0], sems.at[0]),
-        pltpu.make_async_copy(hidden_far.at[1], hidden_ref.at[1], sems.at[1]),
+def squares_kernel(hidden_far, gain_far, places_far, hidden_ref, gain_ref, places_ref, out_ref, sems):
+    block = hidden_ref.shape[1]
+    copies = [pltpu.make_async_copy(hidden_far.at[b], hidden_ref.at[b], sems.at[b]) for b in range(2)]
+    copies += [
         pltpu.make_async_copy(gain_far, gain_ref, sems.at[2]),
         pltpu.make_async_copy(places_far, places_ref, sems.at[3]),
     ]
@@ -65,19 +65,41 @@
         copies[b].wait()
         widened = hidden_ref[b].astype(jnp.float32)
         out_ref[b : b + 1] = as_row(jnp.sum(widened * widened, axis=1, keepdims=True))
-    copies[2].wait()
-    gain = gain_ref[...]
+    for copy in copies[2:]:
+        copy.wait()
+
+
+def first_rank(positions_ref, at):
+    return jnp.sum((positions_ref[...] < at).astype(jnp.float32), axis=1, keepdims=True).astype(jnp.int32)
+
+
+def compact_kernel(usual, n_z, positions_ref, hidden_ref, gain_ref, compact_ref, normed_ref, crowded_ref):
+    block, masked = compact_ref.shape[0], positions_ref.shape[1]
+    ranks = [first_rank(positions_ref, b * block) for b in range(n_z + 1)]
+    most = functools.reduce(jnp.maximum, [end - first for first, end in zip(ranks, ranks[1:])])
+    crowded_ref[0, 0] = (jnp.max(most) > usual).astype(jnp.int32)
+    at = lax.axis_index("vocab") * block
+    first = first_rank(positions_ref, at)
+    rank = lax.broadcasted_iota(jnp.int32, (block, masked), 1)
+    match = rank == first + lax.broadcasted_iota(jnp.int32, (block, masked), 0)
+    places = (positions_ref[...] + 1).astype(jnp.float32)
+    wanted = jnp.sum(jnp.where(match, places, 0.0), axis=1, keepdims=True).astype(jnp.int32) - 1
+    held = at + lax.broadcasted_iota(jnp.int32, (block, block), 1)
+    compact = (wanted == held).astype(jnp.float32)
+    compact_ref[...] = compact
     for b in range(2):
-        normed_ref[b] = (hidden_ref[b].astype(jnp.float32) * gain).astype(jnp.bfloat16)
-    copies[3].wait()
+        normed = (hidden_ref[b].astype(jnp.float32) * gain_ref[...]).astype(jnp.bfloat16)
+        normed = jnp.dot(compact.astype(jnp.bfloat16), normed, preferred_element_type=jnp.float32)
+        normed_ref[b] = normed.astype(jnp.bfloat16)
 
 
 def combine_kernel(width, usual, normed_ref, totals_ref, compact_ref, usual_ref, rest_ref):
     inv_rms = lax.rsqrt(totals_ref[...] / width + epsilon)
-    factor = [as_column((1.0 + guidance) * inv_rms[0:1]), as_column(guidance * inv_rms[1:2])]
+    place = compact_ref[...] > 0.5
+    weight = [(1.0 + guidance) * inv_rms[0:1], guidance * inv_rms[1:2]]
+    factor = [jnp.sum(jnp.where(place, row, 0.0), axis=1, keepdims=True) for row in weight]
     terms = [factor[b] * normed_ref[b].astype(jnp.float32) for b in range(2)]
-    rows = (terms[0] - terms[1]).astype(jnp.bfloat16)
-    rows = jnp.dot(compact_ref[...], rows, preferred_element_type=jnp.float32)
+    rows = terms[0] - terms[1]
     whole, last = divmod(usual, DEEP)
     columns = rows.shape[1]
     for t in range(whole):
@@ -124,25 +146,6 @@
         ref[:, at : at + rows] = tiles_ref[i % slots, :rows].T
         if i + slots < len(tiles):
             copies[i + slots].start()
-
-
-def first_rank(positions_ref, at):
-    return jnp.sum((positions_ref[...] < at).astype(jnp.float32), axis=1, keepdims=True).astype(jnp.int32)
-
-
-def compact_kernel(usual, n_z, positions_ref, out_ref, crowded_ref):
-    block, masked = out_ref.shape[0], positions_ref.shape[1]
-    ranks = [first_rank(positions_ref, b * block) for b in range(n_z + 1)]
-    most = functools.reduce(jnp.maximum, [end - first for first, end in zip(ranks, ranks[1:])])
-    crowded_ref[0, 0] = (jnp.max(most) > usual).astype(jnp.int32)
-    at = lax.axis_index("vocab") * block
-    first = first_rank(positions_ref, at)
-    rank = lax.broadcasted_iota(jnp.int32, (block, masked), 1)
-    match = rank == first + lax.broadcasted_iota(jnp.int32, (block, masked), 0)
-    places = (positions_ref[...] + 1).astype(jnp.float32)
-    wanted = jnp.sum(jnp.where(match, places, 0.0), axis=1, keepdims=True).astype(jnp.int32) - 1
-    held = at + lax.broadcasted_iota(jnp.int32, (block, block), 1)
-    out_ref[...] = (wanted == held).astype(jnp.float32).astype(jnp.bfloat16)
 
 
 def chooser_kernel(own, block, usual, offsets, n_z, n_x, n_c, positions_ref, early_ref, last_ref):
@@ -349,28 +352,28 @@
     own = masked // (n_x * n_c)
     segment = -(-(own + 1) // 16) * 16
 
-    normed, squares, places = call(
+    hidden, gain, places, squares = call(
         squares_kernel,
-        [((2, block, width_local), bf16), ((2, block), f32), ((1, masked), jnp.int32)],
+        [((2, block, width_local), bf16), ((1, width_local), f32), ((1, masked), jnp.int32), ((2, block), f32)],
         [],
         far=[final_hidden, norm_gain[None, :], positions[None, :]],
-        scratch_shapes=[
-            pltpu.VMEM((2, block, width_local), bf16),
-            pltpu.VMEM((1, width_local), f32),
-            pltpu.SemaphoreType.DMA((4,)),
-        ],
+        scratch_shapes=[pltpu.SemaphoreType.DMA((4,))],
     )
     for axis in ("cfg", "rows"):
         squares = sum([shifted(squares, axis, s) for s in range(1, lax.axis_size(axis))], squares)
     usual = int(block * USUAL)
     skipped = usual // DEEP * DEEP
-    compact, crowded = pl.pallas_call(
+    compact, normed, crowded = pl.pallas_call(
         functools.partial(compact_kernel, usual, n_z),
-        out_shape=[pltpu.VMEM((block, block), bf16), jax.ShapeDtypeStruct((1, 1), jnp.int32)],
-        in_specs=in_vmem(1),
-        out_specs=[*in_vmem(1), pl.BlockSpec(memory_space=pltpu.SMEM)],
+        out_shape=[
+            pltpu.VMEM((block, block), f32),
+            pltpu.VMEM((2, block, width_local), bf16),
+            jax.ShapeDtypeStruct((1, 1), jnp.int32),
+        ],
+        in_specs=in_vmem(3),
+        out_specs=[*in_vmem(2), pl.BlockSpec(memory_space=pltpu.SMEM)],
         compiler_params=pltpu.CompilerParams(vmem_limit_bytes=8 * MIB),
-    )(*keep_in_vmem(places))
+    )(*keep_in_vmem(places, hidden, gain))
     block_rows, rest_rows = call(
         functools.partial(combine_kernel, width_local * n_x * n_c, usual),
         [((DEEP, usual * width_local // DEEP), bf16), ((block - skipped, width_local), bf16)],

time: 50.7 us -> 50.1 us (0.988)
  transfers between devices with their start and end apart: 12 -> 12, of which waited for: 9 -> 10; matrix products, arithmetic and copies ran while one was open for 0% -> 0% of each run, Pallas kernels for 26% -> 27%
where the time goes in v9:
time: 50.1 us; the launch traced here: 49.9 us
  Pallas kernels  18.6 us (37%)
  waiting for transfers between devices  15.7 us (31%)
  starting transfers between devices  14.9 us (30%)
  between operations  0.77 us (2%)
    pallas_call x12, Pallas kernels, call(): pl.pallas_call(body, out_shape=[pltpu.VMEM(shape, dtype) for shape, dtype...  16.5 us
    ppermute x9, waiting for transfers between devices, shifted(): lax.ppermute(value, axis, [(i, (i + by) % size) for i in range(size)])  12.8 us
    ppermute x9, starting transfers between devices, shifted(): lax.ppermute(value, axis, [(i, (i + by) % size) for i in range(size)])  11.3 us
    ppermute x3, starting transfers between devices, per_device(): lax.ppermute(stats, 'vocab', [(i, i ^ far) for i in range(n_z)])  3.55 us
    ppermute x3, waiting for transfers between devices, per_device(): lax.ppermute(stats, 'vocab', [(i, i ^ far) for i in range(n_z)])  2.86 us
    pallas_call x1, Pallas kernels, per_device(): pl.pallas_call(functools.partial(final_kernel, [size for _, size in chunk...  1.16 us
  transfers between devices with their start and end apart: 12, of which 10 were waited for; matrix products, arithmetic and copies ran while one was open for 0% of the time, Pallas kernels for 27%

profile of v9, /device:TPU:0, one launch (start us, length us, event | category | flops | bytes accessed | tf_op | source)
XLA Modules:
  0.0 49.9 jit_solution(16523815845894354807)
XLA Ops:
  0.0 1.3 %shard_map.46 = (bf16[2,64,2048]{2,1,0:T(8,128)(2,1)S(1)}, f32[1,2048]{1,0:T(1,128)S(1)}, s32[1,176]{1,0:T(1,128)S(1)}, f32[2,64]{1,0:T(2,128)S(1)}) custom-call(bf16[2,64,2048]{2,1,0:T(8,128)(2,1)} %hidden_far.1, f32[1,2048]{1,0:T(1,128)} %bitcast.6, s32[1,176]{1,0:T(1,128)} %bitcast.7), custom_call_target="tpu_custom_call" | custom-call | tf_op jit(solution)/shard_map/pallas_call | solution.py:32
  1.3 0.5 %collective-permute-start.3 = (f32[2,64]{1,0:T(2,128)S(1)}, f32[2,64]{1,0:T(2,128)S(1)}, u32[]{:S(2)}, u32[]{:S(2)}) collective-permute-start(f32[2,64]{1,0:T(2,128)S(1)} %get-tuple-element.53), channel_id=1, source_target_pairs={{0,1},{1,0},{2,3},{3,2},{4,5},{5,4},{6,7},{7,6},{8,9},{9,8},{10,11... | collective-permute-start | bytes 1544 | tf_op jit(solution)/shard_map/ppermute | solution.py:324
  1.8 0.8 %collective-permute-done.3 = f32[2,64]{1,0:T(2,128)S(1)} collective-permute-done((f32[2,64]{1,0:T(2,128)S(1)}, f32[2,64]{1,0:T(2,128)S(1)}, u32[]{:S(2)}, u32[]{:S(2)}) %collective-permute-start.3) | collective-permute-done | bytes 544 | tf_op jit(solution)/shard_map/ppermute | solution.py:324
  2.6 2.8 %collective-permute-start.4 = (f32[2,64]{1,0:T(2,128)S(1)}, f32[2,64]{1,0:T(2,128)S(1)}, u32[]{:S(2)}, u32[]{:S(2)}) collective-permute-start(f32[2,64]{1,0:T(2,128)S(1)} %add.6), channel_id=1, source_target_pairs={{0,2},{2,0},{1,3},{3,1},{4,6},{6,4},{5,7},{7,5},{8,10},{10,8},{9,1... | collective-permute-start | bytes 1544 | tf_op jit(solution)/shard_map/ppermute | solution.py:324
  5.4 0.9 %shard_map.47 = (f32[64,64]{1,0:T(8,128)S(1)}, bf16[2,64,2048]{2,1,0:T(8,128)(2,1)S(1)}, s32[1,1]{1,0:T(1,128)}) custom-call(s32[1,176]{1,0:T(1,128)S(1)} %get-tuple-element.56.positions_ref, bf16[2,64,2048]{2,1,0:T(8,128)(2,1)S(1)} %get-tuple-element.49.hidden_ref, f32[1,2048]{1,0:T(1,128)S(1)} %get-tuple-element.50.gain_ref), custom_call_target="tpu_custom_call" | custom-call | tf_op jit(solution)/shard_map/pallas_call | solution.py:366
  6.3 0.6 %collective-permute-done.4 = f32[2,64]{1,0:T(2,128)S(1)} collective-permute-done((f32[2,64]{1,0:T(2,128)S(1)}, f32[2,64]{1,0:T(2,128)S(1)}, u32[]{:S(2)}, u32[]{:S(2)}) %collective-permute-start.4) | collective-permute-done | bytes 544 | tf_op jit(solution)/shard_map/ppermute | solution.py:324
  7.0 0.2 shard_map.48
  7.2 2.2 %collective-permute-start.5 = (bf16[16,6656]{1,0:T(8,128)(2,1)S(1)}, bf16[16,6656]{1,0:T(8,128)(2,1)S(1)}, u32[]{:S(2)}, u32[]{:S(2)}) collective-permute-start(bf16[16,6656]{1,0:T(8,128)(2,1)S(1)} %get-tuple-element.69.refs_0_), channel_id=1, source_target_pairs={{0,4},{4,8},{8,12},{12,0},{1,5},{5,9},{9,13},{13,1},{2,6},{6,10},{... | collective-permute-start | bytes 638984 | tf_op jit(solution)/shard_map/ppermute | solution.py:324
  10.0 1.9 %shard_map.50.refs_0_ = bf16[2048,512]{1,0:T(8,128)(2,1)S(1)} custom-call(bf16[4752,2048]{1,0:T(8,128)(2,1)} %bitcast.4), custom_call_target="tpu_custom_call" | custom-call | bytes 2097152 | tf_op jit(solution)/shard_map/pallas_call | solution.py:32
  12.0 2.1 %collective-permute-start.6 = (bf16[16,6656]{1,0:T(8,128)(2,1)S(1)}, bf16[16,6656]{1,0:T(8,128)(2,1)S(1)}, u32[]{:S(2)}, u32[]{:S(2)}) collective-permute-start(bf16[16,6656]{1,0:T(8,128)(2,1)S(1)} %get-tuple-element.69.refs_0_), channel_id=1, source_target_pairs={{0,12},{4,0},{8,4},{12,8},{1,13},{5,1},{9,5},{13,9},{2,14},{6,2},{... | collective-permute-start | bytes 638984 | tf_op jit(solution)/shard_map/ppermute | solution.py:324
  14.1 2.1 %collective-permute-done.5.refs_1_ = bf16[16,6656]{1,0:T(8,128)(2,1)S(1)} collective-permute-done((bf16[16,6656]{1,0:T(8,128)(2,1)S(1)}, bf16[16,6656]{1,0:T(8,128)(2,1)S(1)}, u32[]{:S(2)}, u32[]{:S(2)}) %collective-permute-start.5) | collective-permute-done | bytes 213024 | tf_op jit(solution)/shard_map/ppermute | solution.py:324
  16.2 0.0 collective-permute-start.7
  16.2 0.1 shard_map.49
  16.3 7.1 %shard_map.51 = (bf16[2048,1984]{1,0:T(8,128)(2,1)S(1)}, bf16[2048,2256]{1,0:T(8,128)(2,1)S(1)}) custom-call(bf16[4752,2048]{1,0:T(8,128)(2,1)} %bitcast.5), custom_call_target="tpu_custom_call" | custom-call | bytes 17367040 | tf_op jit(solution)/shard_map/pallas_call | solution.py:32
  23.4 0.0 collective-permute-done.6.refs_2_
  23.4 0.4 shard_map.52.early_ref
  23.8 1.1 %collective-permute-done.7.block_ref = bf16[16,6656]{1,0:T(8,128)(2,1)S(1)} collective-permute-done((bf16[16,6656]{1,0:T(8,128)(2,1)S(1)}, bf16[16,6656]{1,0:T(8,128)(2,1)S(1)}, u32[]{:S(2)}, u32[]{:S(2)}) %collective-permute-start.7) | collective-permute-done | bytes 213024 | tf_op jit(solution)/shard_map/ppermute | solution.py:324
  24.9 2.3 %shard_map.53 = (bf16[176,2048]{1,0:T(8,128)(2,1)S(1)}, f32[88,2560]{1,0:T(8,128)S(1)}, f32[88,2560]{1,0:T(8,128)S(1)}) custom-call(bf16[176,64]{1,0:T(8,128)(2,1)S(1)} %get-tuple-element.67.chooser_ref, bf16[176,2048]{1,0:T(8,128)(2,1)S(1)} %shard_map.52.early_ref, bf16[16,6656]{1,0:T(8,128)(2,1)S(1)} %collective-permute-done.7.block_ref, ...), custom_call_target="tpu_custom_call" | custom-call | flops 1799356416 | bytes 10223616 | tf_op jit(solution)/shard_map/pallas_call | solution.py:32
  27.2 0.1 collective-permute-start.8
  27.3 1.9 %shard_map.56 = (f32[88,2304]{1,0:T(8,128)S(1)}, f32[88,2304]{1,0:T(8,128)S(1)}) custom-call(bf16[176,2048]{1,0:T(8,128)(2,1)S(1)} %get-tuple-element.79.rows_ref, bf16[2048,2256]{1,0:T(8,128)(2,1)S(1)} %get-tuple-element.80.refs_0_), custom_call_target="tpu_custom_call" | custom-call | flops 1626341376 | bytes 9240576 | tf_op jit(solution)/shard_map/pallas_call | solution.py:32
  29.2 0.6 %collective-permute-start.10 = (f32[88,2304]{1,0:T(8,128)S(1)}, f32[88,2304]{1,0:T(8,128)S(1)}, u32[]{:S(2)}, u32[]{:S(2)}) collective-permute-start(f32[88,2304]{1,0:T(8,128)S(1)} %get-tuple-element.82), channel_id=1, source_target_pairs={{0,1},{1,0},{2,3},{3,2},{4,5},{5,4},{6,7},{7,6},{8,9},{9,8},{10,11... | collective-permute-start | bytes 2433032 | tf_op jit(solution)/shard_map/ppermute | solution.py:324
  29.8 0.0 collective-permute-done.8.got_ref
  29.8 0.3 shard_map.54
  30.1 1.6 %collective-permute-start.9 = (s16[8,14080]{1,0:T(8,128)(2,1)S(1)}, s16[8,14080]{1,0:T(8,128)(2,1)S(1)}, u32[]{:S(2)}, u32[]{:S(2)}) collective-permute-start(s16[8,14080]{1,0:T(8,128)(2,1)S(1)} %get-tuple-element.76), channel_id=1, source_target_pairs={{0,2},{2,0},{1,3},{3,1},{4,6},{6,4},{5,7},{7,5},{8,10},{10,8},{9,1... | collective-permute-start | bytes 675848 | tf_op jit(solution)/shard_map/ppermute | solution.py:324
  31.6 0.1 collective-permute-done.10.got_ref
  31.7 0.2 shard_map.57
  32.0 1.6 %collective-permute-start.11 = (s16[8,12672]{1,0:T(8,128)(2,1)S(1)}, s16[8,12672]{1,0:T(8,128)(2,1)S(1)}, u32[]{:S(2)}, u32[]{:S(2)}) collective-permute-start(s16[8,12672]{1,0:T(8,128)(2,1)S(1)} %get-tuple-element.84), channel_id=1, source_target_pairs={{0,2},{2,0},{1,3},{3,1},{4,6},{6,4},{5,7},{7,5},{8,10},{10,8},{9,1... | collective-permute-start | bytes 608264 | tf_op jit(solution)/shard_map/ppermute | solution.py:324
  33.6 4.9 %collective-permute-done.9.refs_1_ = s16[8,14080]{1,0:T(8,128)(2,1)S(1)} collective-permute-done((s16[8,14080]{1,0:T(8,128)(2,1)S(1)}, s16[8,14080]{1,0:T(8,128)(2,1)S(1)}, u32[]{:S(2)}, u32[]{:S(2)}) %collective-permute-start.9) | collective-permute-done | bytes 225312 | tf_op jit(solution)/shard_map/ppermute | solution.py:324
  38.5 0.4 shard_map.55
  38.9 3.0 %collective-permute-done.11.refs_2_ = s16[8,12672]{1,0:T(8,128)(2,1)S(1)} collective-permute-done((s16[8,12672]{1,0:T(8,128)(2,1)S(1)}, s16[8,12672]{1,0:T(8,128)(2,1)S(1)}, u32[]{:S(2)}, u32[]{:S(2)}) %collective-permute-start.11) | collective-permute-done | bytes 202784 | tf_op jit(solution)/shard_map/ppermute | solution.py:324
  42.0 0.4 shard_map.58
  42.4 0.9 %collective-permute-start.14 = (f32[2,128]{1,0:T(2,128)S(1)}, f32[2,128]{1,0:T(2,128)S(1)}, u32[]{:S(2)}, u32[]{:S(2)}) collective-permute-start(f32[2,128]{1,0:T(2,128)S(1)} %get-tuple-element.86.refs_2_), channel_id=1, source_target_pairs={{0,8},{4,12},{8,0},{12,4},{1,9},{5,13},{9,1},{13,5},{2,10},{6,14},... | collective-permute-start | bytes 3080 | tf_op jit(solution)/shard_map/ppermute | solution.py:488
  43.3 1.9 %collective-permute-start.13 = (f32[2,128]{1,0:T(2,128)S(1)}, f32[2,128]{1,0:T(2,128)S(1)}, u32[]{:S(2)}, u32[]{:S(2)}) collective-permute-start(f32[2,128]{1,0:T(2,128)S(1)} %get-tuple-element.86.refs_2_), channel_id=1, source_target_pairs={{0,12},{4,8},{8,4},{12,0},{1,13},{5,9},{9,5},{13,1},{2,14},{6,10},... | collective-permute-start | bytes 3080 | tf_op jit(solution)/shard_map/ppermute | solution.py:488
  45.2 0.7 %collective-permute-start.12 = (f32[2,128]{1,0:T(2,128)S(1)}, f32[2,128]{1,0:T(2,128)S(1)}, u32[]{:S(2)}, u32[]{:S(2)}) collective-permute-start(f32[2,128]{1,0:T(2,128)S(1)} %get-tuple-element.86.refs_2_), channel_id=1, source_target_pairs={{0,4},{4,0},{8,12},{12,8},{1,5},{5,1},{9,13},{13,9},{2,6},{6,2},{1... | collective-permute-start | bytes 3080 | tf_op jit(solution)/shard_map/ppermute | solution.py:488
  45.9 1.0 %collective-permute-done.14.refs_5_ = f32[2,128]{1,0:T(2,128)S(1)} collective-permute-done((f32[2,128]{1,0:T(2,128)S(1)}, f32[2,128]{1,0:T(2,128)S(1)}, u32[]{:S(2)}, u32[]{:S(2)}) %collective-permute-start.14) | collective-permute-done | bytes 1056 | tf_op jit(solution)/shard_map/ppermute | solution.py:488
  46.9 1.7 %collective-permute-done.13.refs_4_ = f32[2,128]{1,0:T(2,128)S(1)} collective-permute-done((f32[2,128]{1,0:T(2,128)S(1)}, f32[2,128]{1,0:T(2,128)S(1)}, u32[]{:S(2)}, u32[]{:S(2)}) %collective-permute-start.13) | collective-permute-done | bytes 1056 | tf_op jit(solution)/shard_map/ppermute | solution.py:488
  48.6 0.1 collective-permute-done.12.refs_3_
  48.8 1.2 %shard_map.59 = f32[44,4752]{1,0:T(8,128)} custom-call(f32[48,2560]{1,0:T(8,128)S(1)} %get-tuple-element.77.refs_0_, f32[48,2304]{1,0:T(8,128)S(1)} %get-tuple-element.85.refs_1_, f32[2,128]{1,0:T(2,128)S(1)} %get-tuple-element.86.refs_2_, f32[2,128]{1,0:T(2,128)S(1)} %collective-permute-done.12.refs_3_, f32[2,128]{1,0:T(2,128)S(1)} %collective-permute-done.13.refs_4_, ...), custom_call_target="tpu_custom_call" | custom-call | tf_op jit(solution)/shard_map/pallas_call | solution.py:492
  (4 shorter events, 0.1 us)
Async XLA Ops:
  1.3 1.3 %collective-permute-start.3 = (f32[2,64]{1,0:T(2,128)S(1)}, f32[2,64]{1,0:T(2,128)S(1)}, u32[]{:S(2)}, u32[]{:S(2)}) collective-permute-start(f32[2,64]{1,0:T(2,128)S(1)} %get-tuple-element.53), channel_id=1, source_target_pairs={{0,1},{1,0},{2,3},{3,2},{4,5},{5,4},{6,7},{7,6},{8,9},{9,8},{10,11... | collective-permute-start | bytes 1544 | tf_op jit(solution)/shard_map/ppermute | solution.py:324
  2.6 4.4 %collective-permute-start.4 = (f32[2,64]{1,0:T(2,128)S(1)}, f32[2,64]{1,0:T(2,128)S(1)}, u32[]{:S(2)}, u32[]{:S(2)}) collective-permute-start(f32[2,64]{1,0:T(2,128)S(1)} %add.6), channel_id=1, source_target_pairs={{0,2},{2,0},{1,3},{3,1},{4,6},{6,4},{5,7},{7,5},{8,10},{10,8},{9,1... | collective-permute-start | bytes 1544 | tf_op jit(solution)/shard_map/ppermute | solution.py:324
  7.2 9.0 %collective-permute-start.5 = (bf16[16,6656]{1,0:T(8,128)(2,1)S(1)}, bf16[16,6656]{1,0:T(8,128)(2,1)S(1)}, u32[]{:S(2)}, u32[]{:S(2)}) collective-permute-start(bf16[16,6656]{1,0:T(8,128)(2,1)S(1)} %get-tuple-element.69.refs_0_), channel_id=1, source_target_pairs={{0,4},{4,8},{8,12},{12,0},{1,5},{5,9},{9,13},{13,1},{2,6},{6,10},{... | collective-permute-start | bytes 638984 | tf_op jit(solution)/shard_map/ppermute | solution.py:324
  12.0 11.5 %collective-permute-start.6 = (bf16[16,6656]{1,0:T(8,128)(2,1)S(1)}, bf16[16,6656]{1,0:T(8,128)(2,1)S(1)}, u32[]{:S(2)}, u32[]{:S(2)}) collective-permute-start(bf16[16,6656]{1,0:T(8,128)(2,1)S(1)} %get-tuple-element.69.refs_0_), channel_id=1, source_target_pairs={{0,12},{4,0},{8,4},{12,8},{1,13},{5,1},{9,5},{13,9},{2,14},{6,2},{... | collective-permute-start | bytes 638984 | tf_op jit(solution)/shard_map/ppermute | solution.py:324
  16.2 8.8 %collective-permute-start.7 = (bf16[16,6656]{1,0:T(8,128)(2,1)S(1)}, bf16[16,6656]{1,0:T(8,128)(2,1)S(1)}, u32[]{:S(2)}, u32[]{:S(2)}) collective-permute-start(bf16[16,6656]{1,0:T(8,128)(2,1)S(1)} %collective-permute-done.5.refs_1_), channel_id=1, source_target_pairs={{0,4},{4,8},{8,12},{12,0},{1,5},{5,9},{9,13},{13,1},{2,6},{6,10},{... | collective-permute-start | bytes 638984 | tf_op jit(solution)/shard_map/ppermute | solution.py:324
  27.2 2.6 %collective-permute-start.8 = (f32[88,2560]{1,0:T(8,128)S(1)}, f32[88,2560]{1,0:T(8,128)S(1)}, u32[]{:S(2)}, u32[]{:S(2)}) collective-permute-start(f32[88,2560]{1,0:T(8,128)S(1)} %get-tuple-element.74), channel_id=1, source_target_pairs={{0,1},{1,0},{2,3},{3,2},{4,5},{5,4},{6,7},{7,6},{8,9},{9,8},{10,11... | collective-permute-start | bytes 2703368 | tf_op jit(solution)/shard_map/ppermute | solution.py:324
  29.2 2.5 %collective-permute-start.10 = (f32[88,2304]{1,0:T(8,128)S(1)}, f32[88,2304]{1,0:T(8,128)S(1)}, u32[]{:S(2)}, u32[]{:S(2)}) collective-permute-start(f32[88,2304]{1,0:T(8,128)S(1)} %get-tuple-element.82), channel_id=1, source_target_pairs={{0,1},{1,0},{2,3},{3,2},{4,5},{5,4},{6,7},{7,6},{8,9},{9,8},{10,11... | collective-permute-start | bytes 2433032 | tf_op jit(solution)/shard_map/ppermute | solution.py:324
  30.1 8.4 %collective-permute-start.9 = (s16[8,14080]{1,0:T(8,128)(2,1)S(1)}, s16[8,14080]{1,0:T(8,128)(2,1)S(1)}, u32[]{:S(2)}, u32[]{:S(2)}) collective-permute-start(s16[8,14080]{1,0:T(8,128)(2,1)S(1)} %get-tuple-element.76), channel_id=1, source_target_pairs={{0,2},{2,0},{1,3},{3,1},{4,6},{6,4},{5,7},{7,5},{8,10},{10,8},{9,1... | collective-permute-start | bytes 675848 | tf_op jit(solution)/shard_map/ppermute | solution.py:324
  32.0 10.0 %collective-permute-start.11 = (s16[8,12672]{1,0:T(8,128)(2,1)S(1)}, s16[8,12672]{1,0:T(8,128)(2,1)S(1)}, u32[]{:S(2)}, u32[]{:S(2)}) collective-permute-start(s16[8,12672]{1,0:T(8,128)(2,1)S(1)} %get-tuple-element.84), channel_id=1, source_target_pairs={{0,2},{2,0},{1,3},{3,1},{4,6},{6,4},{5,7},{7,5},{8,10},{10,8},{9,1... | collective-permute-start | bytes 608264 | tf_op jit(solution)/shard_map/ppermute | solution.py:324
  42.4 4.5 %collective-permute-start.14 = (f32[2,128]{1,0:T(2,128)S(1)}, f32[2,128]{1,0:T(2,128)S(1)}, u32[]{:S(2)}, u32[]{:S(2)}) collective-permute-start(f32[2,128]{1,0:T(2,128)S(1)} %get-tuple-element.86.refs_2_), channel_id=1, source_target_pairs={{0,8},{4,12},{8,0},{12,4},{1,9},{5,13},{9,1},{13,5},{2,10},{6,14},... | collective-permute-start | bytes 3080 | tf_op jit(solution)/shard_map/ppermute | solution.py:488
  43.3 5.4 %collective-permute-start.13 = (f32[2,128]{1,0:T(2,128)S(1)}, f32[2,128]{1,0:T(2,128)S(1)}, u32[]{:S(2)}, u32[]{:S(2)}) collective-permute-start(f32[2,128]{1,0:T(2,128)S(1)} %get-tuple-element.86.refs_2_), channel_id=1, source_target_pairs={{0,12},{4,8},{8,4},{12,0},{1,13},{5,9},{9,5},{13,1},{2,14},{6,10},... | collective-permute-start | bytes 3080 | tf_op jit(solution)/shard_map/ppermute | solution.py:488
  45.2 3.6 %collective-permute-start.12 = (f32[2,128]{1,0:T(2,128)S(1)}, f32[2,128]{1,0:T(2,128)S(1)}, u32[]{:S(2)}, u32[]{:S(2)}) collective-permute-start(f32[2,128]{1,0:T(2,128)S(1)} %get-tuple-element.86.refs_2_), channel_id=1, source_target_pairs={{0,4},{4,0},{8,12},{12,8},{1,5},{5,1},{9,13},{13,9},{2,6},{6,2},{1... | collective-permute-start | bytes 3080 | tf_op jit(solution)/shard_map/ppermute | solution.py:488

commit v10 on v9

--- a/solution.py
+++ b/solution.py
@@ -13,7 +13,7 @@
 LANES = 128
 MIB = 1 << 20
 LOADS = ((512,), (1984,))
-SLOTS = 5
+SLOTS = 8
 CHUNKS = (2496,)
 ROWS = 8
 USUAL = 13 / 16
@@ -28,7 +28,7 @@
     return [pltpu.with_memory_space_constraint(a, pltpu.VMEM) for a in arrays]
 
 
-def call(body, outs, args, far=(), limit=8, cost=None, **kwargs):
+def call(body, outs, args, far=(), limit=12, cost=None, **kwargs):
     return pl.pallas_call(
         body,
         out_shape=[pltpu.VMEM(shape, dtype) for shape, dtype in outs],
@@ -53,19 +53,18 @@
 
 
 def squares_kernel(hidden_far, gain_far, places_far, hidden_ref, gain_ref, places_ref, out_ref, sems):
-    block = hidden_ref.shape[1]
-    copies = [pltpu.make_async_copy(hidden_far.at[b], hidden_ref.at[b], sems.at[b]) for b in range(2)]
-    copies += [
-        pltpu.make_async_copy(gain_far, gain_ref, sems.at[2]),
-        pltpu.make_async_copy(places_far, places_ref, sems.at[3]),
+    copies = [
+        pltpu.make_async_copy(hidden_far, hidden_ref, sems.at[0]),
+        pltpu.make_async_copy(gain_far, gain_ref, sems.at[1]),
+        pltpu.make_async_copy(places_far, places_ref, sems.at[2]),
     ]
     for copy in copies:
         copy.start()
+    copies[0].wait()
     for b in range(2):
-        copies[b].wait()
         widened = hidden_ref[b].astype(jnp.float32)
         out_ref[b : b + 1] = as_row(jnp.sum(widened * widened, axis=1, keepdims=True))
-    for copy in copies[2:]:
+    for copy in copies[1:]:
         copy.wait()
 
 
@@ -266,7 +265,8 @@
     *in_refs, guided_ref, out_ref = refs
     before = in_refs.pop(0) if in_refs[0].shape == out_ref.shape else None
     segment, width = guided_ref.shape
-    real = lax.broadcasted_iota(jnp.int32, (ROWS, width), 1) < size
+    last = width - TILE
+    real = lax.broadcasted_iota(jnp.int32, (ROWS, TILE), 1) < size - last
     tops, totals = [], []
     for t in range(segment // ROWS):
         rows = slice(t * ROWS, (t + 1) * ROWS)
@@ -275,9 +275,11 @@
             for got in in_refs[1:]:
                 guided = guided + restored(own, size, width, got, t)
         guided_ref[rows] = guided
-        top = jnp.max(jnp.where(real, guided, -jnp.inf), axis=1, keepdims=True)
+        ending = jnp.where(real, guided[:, last:], -jnp.inf)
+        guided = jnp.concatenate([guided[:, :last], ending], axis=1) if last else ending
+        top = jnp.max(guided, axis=1, keepdims=True)
         tops.append(top)
-        totals.append(jnp.sum(jnp.where(real, jnp.exp(guided - top), 0.0), axis=1, keepdims=True))
+        totals.append(jnp.sum(jnp.exp(guided - top), axis=1, keepdims=True))
     top, total = as_row(jnp.concatenate(tops, axis=0)), as_row(jnp.concatenate(totals, axis=0))
     if before is not None:
         top, total = merged((top, total), (before[0:1, :segment], before[1:2, :segment]))
@@ -357,7 +359,7 @@
         [((2, block, width_local), bf16), ((1, width_local), f32), ((1, masked), jnp.int32), ((2, block), f32)],
         [],
         far=[final_hidden, norm_gain[None, :], positions[None, :]],
-        scratch_shapes=[pltpu.SemaphoreType.DMA((4,))],
+        scratch_shapes=[pltpu.SemaphoreType.DMA((3,))],
     )
     for axis in ("cfg", "rows"):
         squares = sum([shifted(squares, axis, s) for s in range(1, lax.axis_size(axis))], squares)

time: 50.1 us -> 50 us (level)
  no operation moved by 1% of the time
where the time goes in v10:
time: 50 us; the launch traced here: 49.9 us
  Pallas kernels  18.5 us (37%)
  waiting for transfers between devices  15.6 us (31%)
  starting transfers between devices  14.9 us (30%)
  between operations  0.77 us (2%)
    pallas_call x12, Pallas kernels, call(): pl.pallas_call(body, out_shape=[pltpu.VMEM(shape, dtype) for shape, dtype...  16.5 us
    ppermute x9, waiting for transfers between devices, shifted(): lax.ppermute(value, axis, [(i, (i + by) % size) for i in range(size)])  12.8 us
    ppermute x9, starting transfers between devices, shifted(): lax.ppermute(value, axis, [(i, (i + by) % size) for i in range(size)])  11.4 us
    ppermute x3, starting transfers between devices, per_device(): lax.ppermute(stats, 'vocab', [(i, i ^ far) for i in range(n_z)])  3.55 us
    ppermute x3, waiting for transfers between devices, per_device(): lax.ppermute(stats, 'vocab', [(i, i ^ far) for i in range(n_z)])  2.79 us
    pallas_call x1, Pallas kernels, per_device(): pl.pallas_call(functools.partial(final_kernel, [size for _, size in chunk...  1.16 us
  transfers between devices with their start and end apart: 12, of which 10 were waited for; matrix products, arithmetic and copies ran while one was open for 0% of the time, Pallas kernels for 27%

profile of v10, /device:TPU:0, one launch (start us, length us, event | category | flops | bytes accessed | tf_op | source)
XLA Modules:
  0.0 49.9 jit_solution(12930096336959338721)
XLA Ops:
  0.0 1.3 %shard_map.46 = (bf16[2,64,2048]{2,1,0:T(8,128)(2,1)S(1)}, f32[1,2048]{1,0:T(1,128)S(1)}, s32[1,176]{1,0:T(1,128)S(1)}, f32[2,64]{1,0:T(2,128)S(1)}) custom-call(bf16[2,64,2048]{2,1,0:T(8,128)(2,1)} %hidden_far.1, f32[1,2048]{1,0:T(1,128)} %bitcast.6, s32[1,176]{1,0:T(1,128)} %bitcast.7), custom_call_target="tpu_custom_call" | custom-call | tf_op jit(solution)/shard_map/pallas_call | solution.py:32
  1.3 0.5 %collective-permute-start.3 = (f32[2,64]{1,0:T(2,128)S(1)}, f32[2,64]{1,0:T(2,128)S(1)}, u32[]{:S(2)}, u32[]{:S(2)}) collective-permute-start(f32[2,64]{1,0:T(2,128)S(1)} %get-tuple-element.53), channel_id=1, source_target_pairs={{0,1},{1,0},{2,3},{3,2},{4,5},{5,4},{6,7},{7,6},{8,9},{9,8},{10,11... | collective-permute-start | bytes 1544 | tf_op jit(solution)/shard_map/ppermute | solution.py:326
  1.8 0.8 %collective-permute-done.3 = f32[2,64]{1,0:T(2,128)S(1)} collective-permute-done((f32[2,64]{1,0:T(2,128)S(1)}, f32[2,64]{1,0:T(2,128)S(1)}, u32[]{:S(2)}, u32[]{:S(2)}) %collective-permute-start.3) | collective-permute-done | bytes 544 | tf_op jit(solution)/shard_map/ppermute | solution.py:326
  2.6 2.8 %collective-permute-start.4 = (f32[2,64]{1,0:T(2,128)S(1)}, f32[2,64]{1,0:T(2,128)S(1)}, u32[]{:S(2)}, u32[]{:S(2)}) collective-permute-start(f32[2,64]{1,0:T(2,128)S(1)} %add.6), channel_id=1, source_target_pairs={{0,2},{2,0},{1,3},{3,1},{4,6},{6,4},{5,7},{7,5},{8,10},{10,8},{9,1... | collective-permute-start | bytes 1544 | tf_op jit(solution)/shard_map/ppermute | solution.py:326
  5.4 0.9 %shard_map.47 = (f32[64,64]{1,0:T(8,128)S(1)}, bf16[2,64,2048]{2,1,0:T(8,128)(2,1)S(1)}, s32[1,1]{1,0:T(1,128)}) custom-call(s32[1,176]{1,0:T(1,128)S(1)} %get-tuple-element.56.positions_ref, bf16[2,64,2048]{2,1,0:T(8,128)(2,1)S(1)} %get-tuple-element.49.hidden_ref, f32[1,2048]{1,0:T(1,128)S(1)} %get-tuple-element.50.gain_ref), custom_call_target="tpu_custom_call" | custom-call | tf_op jit(solution)/shard_map/pallas_call | solution.py:368
  6.3 0.6 %collective-permute-done.4 = f32[2,64]{1,0:T(2,128)S(1)} collective-permute-done((f32[2,64]{1,0:T(2,128)S(1)}, f32[2,64]{1,0:T(2,128)S(1)}, u32[]{:S(2)}, u32[]{:S(2)}) %collective-permute-start.4) | collective-permute-done | bytes 544 | tf_op jit(solution)/shard_map/ppermute | solution.py:326
  7.0 0.2 shard_map.48
  7.2 2.2 %collective-permute-start.5 = (bf16[16,6656]{1,0:T(8,128)(2,1)S(1)}, bf16[16,6656]{1,0:T(8,128)(2,1)S(1)}, u32[]{:S(2)}, u32[]{:S(2)}) collective-permute-start(bf16[16,6656]{1,0:T(8,128)(2,1)S(1)} %get-tuple-element.69.refs_0_), channel_id=1, source_target_pairs={{0,4},{4,8},{8,12},{12,0},{1,5},{5,9},{9,13},{13,1},{2,6},{6,10},{... | collective-permute-start | bytes 638984 | tf_op jit(solution)/shard_map/ppermute | solution.py:326
  10.0 2.0 %shard_map.50.refs_0_ = bf16[2048,512]{1,0:T(8,128)(2,1)S(1)} custom-call(bf16[4752,2048]{1,0:T(8,128)(2,1)} %bitcast.4), custom_call_target="tpu_custom_call" | custom-call | bytes 2097152 | tf_op jit(solution)/shard_map/pallas_call | solution.py:32
  12.0 2.1 %collective-permute-start.6 = (bf16[16,6656]{1,0:T(8,128)(2,1)S(1)}, bf16[16,6656]{1,0:T(8,128)(2,1)S(1)}, u32[]{:S(2)}, u32[]{:S(2)}) collective-permute-start(bf16[16,6656]{1,0:T(8,128)(2,1)S(1)} %get-tuple-element.69.refs_0_), channel_id=1, source_target_pairs={{0,12},{4,0},{8,4},{12,8},{1,13},{5,1},{9,5},{13,9},{2,14},{6,2},{... | collective-permute-start | bytes 638984 | tf_op jit(solution)/shard_map/ppermute | solution.py:326
  14.1 2.1 %collective-permute-done.5.refs_1_ = bf16[16,6656]{1,0:T(8,128)(2,1)S(1)} collective-permute-done((bf16[16,6656]{1,0:T(8,128)(2,1)S(1)}, bf16[16,6656]{1,0:T(8,128)(2,1)S(1)}, u32[]{:S(2)}, u32[]{:S(2)}) %collective-permute-start.5) | collective-permute-done | bytes 213024 | tf_op jit(solution)/shard_map/ppermute | solution.py:326
  16.1 0.0 collective-permute-start.7
  16.1 0.1 shard_map.49
  16.3 7.1 %shard_map.51 = (bf16[2048,1984]{1,0:T(8,128)(2,1)S(1)}, bf16[2048,2256]{1,0:T(8,128)(2,1)S(1)}) custom-call(bf16[4752,2048]{1,0:T(8,128)(2,1)} %bitcast.5), custom_call_target="tpu_custom_call" | custom-call | bytes 17367040 | tf_op jit(solution)/shard_map/pallas_call | solution.py:32
  23.4 0.0 collective-permute-done.6.refs_2_
  23.4 0.4 shard_map.52.early_ref
  23.7 1.2 %collective-permute-done.7.block_ref = bf16[16,6656]{1,0:T(8,128)(2,1)S(1)} collective-permute-done((bf16[16,6656]{1,0:T(8,128)(2,1)S(1)}, bf16[16,6656]{1,0:T(8,128)(2,1)S(1)}, u32[]{:S(2)}, u32[]{:S(2)}) %collective-permute-start.7) | collective-permute-done | bytes 213024 | tf_op jit(solution)/shard_map/ppermute | solution.py:326
  24.9 2.3 %shard_map.53 = (bf16[176,2048]{1,0:T(8,128)(2,1)S(1)}, f32[88,2560]{1,0:T(8,128)S(1)}, f32[88,2560]{1,0:T(8,128)S(1)}) custom-call(bf16[176,64]{1,0:T(8,128)(2,1)S(1)} %get-tuple-element.67.chooser_ref, bf16[176,2048]{1,0:T(8,128)(2,1)S(1)} %shard_map.52.early_ref, bf16[16,6656]{1,0:T(8,128)(2,1)S(1)} %collective-permute-done.7.block_ref, ...), custom_call_target="tpu_custom_call" | custom-call | flops 1799356416 | bytes 10223616 | tf_op jit(solution)/shard_map/pallas_call | solution.py:32
  27.2 0.1 collective-permute-start.8
  27.3 1.9 %shard_map.56 = (f32[88,2304]{1,0:T(8,128)S(1)}, f32[88,2304]{1,0:T(8,128)S(1)}) custom-call(bf16[176,2048]{1,0:T(8,128)(2,1)S(1)} %get-tuple-element.79.rows_ref, bf16[2048,2256]{1,0:T(8,128)(2,1)S(1)} %get-tuple-element.80.refs_0_), custom_call_target="tpu_custom_call" | custom-call | flops 1626341376 | bytes 9240576 | tf_op jit(solution)/shard_map/pallas_call | solution.py:32
  29.2 0.6 %collective-permute-start.10 = (f32[88,2304]{1,0:T(8,128)S(1)}, f32[88,2304]{1,0:T(8,128)S(1)}, u32[]{:S(2)}, u32[]{:S(2)}) collective-permute-start(f32[88,2304]{1,0:T(8,128)S(1)} %get-tuple-element.82), channel_id=1, source_target_pairs={{0,1},{1,0},{2,3},{3,2},{4,5},{5,4},{6,7},{7,6},{8,9},{9,8},{10,11... | collective-permute-start | bytes 2433032 | tf_op jit(solution)/shard_map/ppermute | solution.py:326
  29.8 0.0 collective-permute-done.8.got_ref
  29.8 0.3 shard_map.54
  30.0 1.6 %collective-permute-start.9 = (s16[8,14080]{1,0:T(8,128)(2,1)S(1)}, s16[8,14080]{1,0:T(8,128)(2,1)S(1)}, u32[]{:S(2)}, u32[]{:S(2)}) collective-permute-start(s16[8,14080]{1,0:T(8,128)(2,1)S(1)} %get-tuple-element.76), channel_id=1, source_target_pairs={{0,2},{2,0},{1,3},{3,1},{4,6},{6,4},{5,7},{7,5},{8,10},{10,8},{9,1... | collective-permute-start | bytes 675848 | tf_op jit(solution)/shard_map/ppermute | solution.py:326
  31.6 0.1 collective-permute-done.10.got_ref
  31.7 0.2 shard_map.57
  32.0 1.6 %collective-permute-start.11 = (s16[8,12672]{1,0:T(8,128)(2,1)S(1)}, s16[8,12672]{1,0:T(8,128)(2,1)S(1)}, u32[]{:S(2)}, u32[]{:S(2)}) collective-permute-start(s16[8,12672]{1,0:T(8,128)(2,1)S(1)} %get-tuple-element.84), channel_id=1, source_target_pairs={{0,2},{2,0},{1,3},{3,1},{4,6},{6,4},{5,7},{7,5},{8,10},{10,8},{9,1... | collective-permute-start | bytes 608264 | tf_op jit(solution)/shard_map/ppermute | solution.py:326
  33.5 4.9 %collective-permute-done.9.refs_1_ = s16[8,14080]{1,0:T(8,128)(2,1)S(1)} collective-permute-done((s16[8,14080]{1,0:T(8,128)(2,1)S(1)}, s16[8,14080]{1,0:T(8,128)(2,1)S(1)}, u32[]{:S(2)}, u32[]{:S(2)}) %collective-permute-start.9) | collective-permute-done | bytes 225312 | tf_op jit(solution)/shard_map/ppermute | solution.py:326
  38.5 0.4 shard_map.55
  38.9 3.1 %collective-permute-done.11.refs_2_ = s16[8,12672]{1,0:T(8,128)(2,1)S(1)} collective-permute-done((s16[8,12672]{1,0:T(8,128)(2,1)S(1)}, s16[8,12672]{1,0:T(8,128)(2,1)S(1)}, u32[]{:S(2)}, u32[]{:S(2)}) %collective-permute-start.11) | collective-permute-done | bytes 202784 | tf_op jit(solution)/shard_map/ppermute | solution.py:326
  42.0 0.4 shard_map.58
  42.4 0.9 %collective-permute-start.14 = (f32[2,128]{1,0:T(2,128)S(1)}, f32[2,128]{1,0:T(2,128)S(1)}, u32[]{:S(2)}, u32[]{:S(2)}) collective-permute-start(f32[2,128]{1,0:T(2,128)S(1)} %get-tuple-element.86.refs_2_), channel_id=1, source_target_pairs={{0,8},{4,12},{8,0},{12,4},{1,9},{5,13},{9,1},{13,5},{2,10},{6,14},... | collective-permute-start | bytes 3080 | tf_op jit(solution)/shard_map/ppermute | solution.py:490
  43.2 1.9 %collective-permute-start.13 = (f32[2,128]{1,0:T(2,128)S(1)}, f32[2,128]{1,0:T(2,128)S(1)}, u32[]{:S(2)}, u32[]{:S(2)}) collective-permute-start(f32[2,128]{1,0:T(2,128)S(1)} %get-tuple-element.86.refs_2_), channel_id=1, source_target_pairs={{0,12},{4,8},{8,4},{12,0},{1,13},{5,9},{9,5},{13,1},{2,14},{6,10},... | collective-permute-start | bytes 3080 | tf_op jit(solution)/shard_map/ppermute | solution.py:490
  45.1 0.8 %collective-permute-start.12 = (f32[2,128]{1,0:T(2,128)S(1)}, f32[2,128]{1,0:T(2,128)S(1)}, u32[]{:S(2)}, u32[]{:S(2)}) collective-permute-start(f32[2,128]{1,0:T(2,128)S(1)} %get-tuple-element.86.refs_2_), channel_id=1, source_target_pairs={{0,4},{4,0},{8,12},{12,8},{1,5},{5,1},{9,13},{13,9},{2,6},{6,2},{1... | collective-permute-start | bytes 3080 | tf_op jit(solution)/shard_map/ppermute | solution.py:490
  45.9 1.0 %collective-permute-done.14.refs_5_ = f32[2,128]{1,0:T(2,128)S(1)} collective-permute-done((f32[2,128]{1,0:T(2,128)S(1)}, f32[2,128]{1,0:T(2,128)S(1)}, u32[]{:S(2)}, u32[]{:S(2)}) %collective-permute-start.14) | collective-permute-done | bytes 1056 | tf_op jit(solution)/shard_map/ppermute | solution.py:490
  46.9 1.7 %collective-permute-done.13.refs_4_ = f32[2,128]{1,0:T(2,128)S(1)} collective-permute-done((f32[2,128]{1,0:T(2,128)S(1)}, f32[2,128]{1,0:T(2,128)S(1)}, u32[]{:S(2)}, u32[]{:S(2)}) %collective-permute-start.13) | collective-permute-done | bytes 1056 | tf_op jit(solution)/shard_map/ppermute | solution.py:490
  48.6 0.1 collective-permute-done.12.refs_3_
  48.7 1.2 %shard_map.59 = f32[44,4752]{1,0:T(8,128)} custom-call(f32[48,2560]{1,0:T(8,128)S(1)} %get-tuple-element.77.refs_0_, f32[48,2304]{1,0:T(8,128)S(1)} %get-tuple-element.85.refs_1_, f32[2,128]{1,0:T(2,128)S(1)} %get-tuple-element.86.refs_2_, f32[2,128]{1,0:T(2,128)S(1)} %collective-permute-done.12.refs_3_, f32[2,128]{1,0:T(2,128)S(1)} %collective-permute-done.13.refs_4_, ...), custom_call_target="tpu_custom_call" | custom-call | tf_op jit(solution)/shard_map/pallas_call | solution.py:494
  (4 shorter events, 0.1 us)
Async XLA Ops:
  1.3 1.3 %collective-permute-start.3 = (f32[2,64]{1,0:T(2,128)S(1)}, f32[2,64]{1,0:T(2,128)S(1)}, u32[]{:S(2)}, u32[]{:S(2)}) collective-permute-start(f32[2,64]{1,0:T(2,128)S(1)} %get-tuple-element.53), channel_id=1, source_target_pairs={{0,1},{1,0},{2,3},{3,2},{4,5},{5,4},{6,7},{7,6},{8,9},{9,8},{10,11... | collective-permute-start | bytes 1544 | tf_op jit(solution)/shard_map/ppermute | solution.py:326
  2.6 4.4 %collective-permute-start.4 = (f32[2,64]{1,0:T(2,128)S(1)}, f32[2,64]{1,0:T(2,128)S(1)}, u32[]{:S(2)}, u32[]{:S(2)}) collective-permute-start(f32[2,64]{1,0:T(2,128)S(1)} %add.6), channel_id=1, source_target_pairs={{0,2},{2,0},{1,3},{3,1},{4,6},{6,4},{5,7},{7,5},{8,10},{10,8},{9,1... | collective-permute-start | bytes 1544 | tf_op jit(solution)/shard_map/ppermute | solution.py:326
  7.2 9.0 %collective-permute-start.5 = (bf16[16,6656]{1,0:T(8,128)(2,1)S(1)}, bf16[16,6656]{1,0:T(8,128)(2,1)S(1)}, u32[]{:S(2)}, u32[]{:S(2)}) collective-permute-start(bf16[16,6656]{1,0:T(8,128)(2,1)S(1)} %get-tuple-element.69.refs_0_), channel_id=1, source_target_pairs={{0,4},{4,8},{8,12},{12,0},{1,5},{5,9},{9,13},{13,1},{2,6},{6,10},{... | collective-permute-start | bytes 638984 | tf_op jit(solution)/shard_map/ppermute | solution.py:326
  12.0 11.4 %collective-permute-start.6 = (bf16[16,6656]{1,0:T(8,128)(2,1)S(1)}, bf16[16,6656]{1,0:T(8,128)(2,1)S(1)}, u32[]{:S(2)}, u32[]{:S(2)}) collective-permute-start(bf16[16,6656]{1,0:T(8,128)(2,1)S(1)} %get-tuple-element.69.refs_0_), channel_id=1, source_target_pairs={{0,12},{4,0},{8,4},{12,8},{1,13},{5,1},{9,5},{13,9},{2,14},{6,2},{... | collective-permute-start | bytes 638984 | tf_op jit(solution)/shard_map/ppermute | solution.py:326
  16.1 8.8 %collective-permute-start.7 = (bf16[16,6656]{1,0:T(8,128)(2,1)S(1)}, bf16[16,6656]{1,0:T(8,128)(2,1)S(1)}, u32[]{:S(2)}, u32[]{:S(2)}) collective-permute-start(bf16[16,6656]{1,0:T(8,128)(2,1)S(1)} %collective-permute-done.5.refs_1_), channel_id=1, source_target_pairs={{0,4},{4,8},{8,12},{12,0},{1,5},{5,9},{9,13},{13,1},{2,6},{6,10},{... | collective-permute-start | bytes 638984 | tf_op jit(solution)/shard_map/ppermute | solution.py:326
  27.2 2.6 %collective-permute-start.8 = (f32[88,2560]{1,0:T(8,128)S(1)}, f32[88,2560]{1,0:T(8,128)S(1)}, u32[]{:S(2)}, u32[]{:S(2)}) collective-permute-start(f32[88,2560]{1,0:T(8,128)S(1)} %get-tuple-element.74), channel_id=1, source_target_pairs={{0,1},{1,0},{2,3},{3,2},{4,5},{5,4},{6,7},{7,6},{8,9},{9,8},{10,11... | collective-permute-start | bytes 2703368 | tf_op jit(solution)/shard_map/ppermute | solution.py:326
  29.2 2.5 %collective-permute-start.10 = (f32[88,2304]{1,0:T(8,128)S(1)}, f32[88,2304]{1,0:T(8,128)S(1)}, u32[]{:S(2)}, u32[]{:S(2)}) collective-permute-start(f32[88,2304]{1,0:T(8,128)S(1)} %get-tuple-element.82), channel_id=1, source_target_pairs={{0,1},{1,0},{2,3},{3,2},{4,5},{5,4},{6,7},{7,6},{8,9},{9,8},{10,11... | collective-permute-start | bytes 2433032 | tf_op jit(solution)/shard_map/ppermute | solution.py:326
  30.0 8.4 %collective-permute-start.9 = (s16[8,14080]{1,0:T(8,128)(2,1)S(1)}, s16[8,14080]{1,0:T(8,128)(2,1)S(1)}, u32[]{:S(2)}, u32[]{:S(2)}) collective-permute-start(s16[8,14080]{1,0:T(8,128)(2,1)S(1)} %get-tuple-element.76), channel_id=1, source_target_pairs={{0,2},{2,0},{1,3},{3,1},{4,6},{6,4},{5,7},{7,5},{8,10},{10,8},{9,1... | collective-permute-start | bytes 675848 | tf_op jit(solution)/shard_map/ppermute | solution.py:326
  32.0 10.0 %collective-permute-start.11 = (s16[8,12672]{1,0:T(8,128)(2,1)S(1)}, s16[8,12672]{1,0:T(8,128)(2,1)S(1)}, u32[]{:S(2)}, u32[]{:S(2)}) collective-permute-start(s16[8,12672]{1,0:T(8,128)(2,1)S(1)} %get-tuple-element.84), channel_id=1, source_target_pairs={{0,2},{2,0},{1,3},{3,1},{4,6},{6,4},{5,7},{7,5},{8,10},{10,8},{9,1... | collective-permute-start | bytes 608264 | tf_op jit(solution)/shard_map/ppermute | solution.py:326
  42.4 4.5 %collective-permute-start.14 = (f32[2,128]{1,0:T(2,128)S(1)}, f32[2,128]{1,0:T(2,128)S(1)}, u32[]{:S(2)}, u32[]{:S(2)}) collective-permute-start(f32[2,128]{1,0:T(2,128)S(1)} %get-tuple-element.86.refs_2_), channel_id=1, source_target_pairs={{0,8},{4,12},{8,0},{12,4},{1,9},{5,13},{9,1},{13,5},{2,10},{6,14},... | collective-permute-start | bytes 3080 | tf_op jit(solution)/shard_map/ppermute | solution.py:490
  43.2 5.4 %collective-permute-start.13 = (f32[2,128]{1,0:T(2,128)S(1)}, f32[2,128]{1,0:T(2,128)S(1)}, u32[]{:S(2)}, u32[]{:S(2)}) collective-permute-start(f32[2,128]{1,0:T(2,128)S(1)} %get-tuple-element.86.refs_2_), channel_id=1, source_target_pairs={{0,12},{4,8},{8,4},{12,0},{1,13},{5,9},{9,5},{13,1},{2,14},{6,10},... | collective-permute-start | bytes 3080 | tf_op jit(solution)/shard_map/ppermute | solution.py:490
  45.1 3.6 %collective-permute-start.12 = (f32[2,128]{1,0:T(2,128)S(1)}, f32[2,128]{1,0:T(2,128)S(1)}, u32[]{:S(2)}, u32[]{:S(2)}) collective-permute-start(f32[2,128]{1,0:T(2,128)S(1)} %get-tuple-element.86.refs_2_), channel_id=1, source_target_pairs={{0,4},{4,0},{8,12},{12,8},{1,5},{5,1},{9,13},{13,9},{2,6},{6,2},{1... | collective-permute-start | bytes 3080 | tf_op jit(solution)/shard_map/ppermute | solution.py:490

commit v11 on v9

--- a/solution.py
+++ b/solution.py
@@ -206,7 +206,7 @@
     *weights_refs, rows_ref, keep_ref, send_ref = refs
     block = jnp.concatenate(unpacked(block_ref, usual, rows_ref.shape[1]), axis=0)
     last = jnp.dot(chooser_ref[...], block, preferred_element_type=jnp.float32)
-    rows_ref[...] = (early_ref[...].astype(jnp.float32) + last).astype(jnp.bfloat16)
+    rows_ref[...] = early_ref[...] + last.astype(jnp.bfloat16)
     multiply(start, size, rows_ref, weights_refs, keep_ref, send_ref)
 
 

time: 50.1 us -> 50.1 us (level)
  no operation moved by 1% of the time
where the time goes in v11:
time: 50.1 us; the launch traced here: 49.9 us
  Pallas kernels  18.6 us (37%)
  waiting for transfers between devices  15.6 us (31%)
  starting transfers between devices  14.9 us (30%)
  between operations  0.77 us (2%)
    pallas_call x12, Pallas kernels, call(): pl.pallas_call(body, out_shape=[pltpu.VMEM(shape, dtype) for shape, dtype...  16.5 us
    ppermute x9, waiting for transfers between devices, shifted(): lax.ppermute(value, axis, [(i, (i + by) % size) for i in range(size)])  12.8 us
    ppermute x9, starting transfers between devices, shifted(): lax.ppermute(value, axis, [(i, (i + by) % size) for i in range(size)])  11.4 us
    ppermute x3, starting transfers between devices, per_device(): lax.ppermute(stats, 'vocab', [(i, i ^ far) for i in range(n_z)])  3.55 us
    ppermute x3, waiting for transfers between devices, per_device(): lax.ppermute(stats, 'vocab', [(i, i ^ far) for i in range(n_z)])  2.86 us
    pallas_call x1, Pallas kernels, per_device(): pl.pallas_call(functools.partial(final_kernel, [size for _, size in chunk...  1.16 us
  transfers between devices with their start and end apart: 12, of which 10 were waited for; matrix products, arithmetic and copies ran while one was open for 0% of the time, Pallas kernels for 27%

profile of v11, /device:TPU:0, one launch (start us, length us, event | category | flops | bytes accessed | tf_op | source)
XLA Modules:
  0.0 49.9 jit_solution(3894882601499455245)
XLA Ops:
  0.0 1.3 %shard_map.46 = (bf16[2,64,2048]{2,1,0:T(8,128)(2,1)S(1)}, f32[1,2048]{1,0:T(1,128)S(1)}, s32[1,176]{1,0:T(1,128)S(1)}, f32[2,64]{1,0:T(2,128)S(1)}) custom-call(bf16[2,64,2048]{2,1,0:T(8,128)(2,1)} %hidden_far.1, f32[1,2048]{1,0:T(1,128)} %bitcast.6, s32[1,176]{1,0:T(1,128)} %bitcast.7), custom_call_target="tpu_custom_call" | custom-call | tf_op jit(solution)/shard_map/pallas_call | solution.py:32
  1.3 0.5 %collective-permute-start.3 = (f32[2,64]{1,0:T(2,128)S(1)}, f32[2,64]{1,0:T(2,128)S(1)}, u32[]{:S(2)}, u32[]{:S(2)}) collective-permute-start(f32[2,64]{1,0:T(2,128)S(1)} %get-tuple-element.53), channel_id=1, source_target_pairs={{0,1},{1,0},{2,3},{3,2},{4,5},{5,4},{6,7},{7,6},{8,9},{9,8},{10,11... | collective-permute-start | bytes 1544 | tf_op jit(solution)/shard_map/ppermute | solution.py:324
  1.8 0.8 %collective-permute-done.3 = f32[2,64]{1,0:T(2,128)S(1)} collective-permute-done((f32[2,64]{1,0:T(2,128)S(1)}, f32[2,64]{1,0:T(2,128)S(1)}, u32[]{:S(2)}, u32[]{:S(2)}) %collective-permute-start.3) | collective-permute-done | bytes 544 | tf_op jit(solution)/shard_map/ppermute | solution.py:324
  2.6 2.8 %collective-permute-start.4 = (f32[2,64]{1,0:T(2,128)S(1)}, f32[2,64]{1,0:T(2,128)S(1)}, u32[]{:S(2)}, u32[]{:S(2)}) collective-permute-start(f32[2,64]{1,0:T(2,128)S(1)} %add.6), channel_id=1, source_target_pairs={{0,2},{2,0},{1,3},{3,1},{4,6},{6,4},{5,7},{7,5},{8,10},{10,8},{9,1... | collective-permute-start | bytes 1544 | tf_op jit(solution)/shard_map/ppermute | solution.py:324
  5.4 0.9 %shard_map.47 = (f32[64,64]{1,0:T(8,128)S(1)}, bf16[2,64,2048]{2,1,0:T(8,128)(2,1)S(1)}, s32[1,1]{1,0:T(1,128)}) custom-call(s32[1,176]{1,0:T(1,128)S(1)} %get-tuple-element.56.positions_ref, bf16[2,64,2048]{2,1,0:T(8,128)(2,1)S(1)} %get-tuple-element.49.hidden_ref, f32[1,2048]{1,0:T(1,128)S(1)} %get-tuple-element.50.gain_ref), custom_call_target="tpu_custom_call" | custom-call | tf_op jit(solution)/shard_map/pallas_call | solution.py:366
  6.3 0.6 %collective-permute-done.4 = f32[2,64]{1,0:T(2,128)S(1)} collective-permute-done((f32[2,64]{1,0:T(2,128)S(1)}, f32[2,64]{1,0:T(2,128)S(1)}, u32[]{:S(2)}, u32[]{:S(2)}) %collective-permute-start.4) | collective-permute-done | bytes 544 | tf_op jit(solution)/shard_map/ppermute | solution.py:324
  7.0 0.2 shard_map.48
  7.2 2.2 %collective-permute-start.5 = (bf16[16,6656]{1,0:T(8,128)(2,1)S(1)}, bf16[16,6656]{1,0:T(8,128)(2,1)S(1)}, u32[]{:S(2)}, u32[]{:S(2)}) collective-permute-start(bf16[16,6656]{1,0:T(8,128)(2,1)S(1)} %get-tuple-element.69.refs_0_), channel_id=1, source_target_pairs={{0,4},{4,8},{8,12},{12,0},{1,5},{5,9},{9,13},{13,1},{2,6},{6,10},{... | collective-permute-start | bytes 638984 | tf_op jit(solution)/shard_map/ppermute | solution.py:324
  10.0 1.9 %shard_map.50.refs_0_ = bf16[2048,512]{1,0:T(8,128)(2,1)S(1)} custom-call(bf16[4752,2048]{1,0:T(8,128)(2,1)} %bitcast.4), custom_call_target="tpu_custom_call" | custom-call | bytes 2097152 | tf_op jit(solution)/shard_map/pallas_call | solution.py:32
  12.0 2.1 %collective-permute-start.6 = (bf16[16,6656]{1,0:T(8,128)(2,1)S(1)}, bf16[16,6656]{1,0:T(8,128)(2,1)S(1)}, u32[]{:S(2)}, u32[]{:S(2)}) collective-permute-start(bf16[16,6656]{1,0:T(8,128)(2,1)S(1)} %get-tuple-element.69.refs_0_), channel_id=1, source_target_pairs={{0,12},{4,0},{8,4},{12,8},{1,13},{5,1},{9,5},{13,9},{2,14},{6,2},{... | collective-permute-start | bytes 638984 | tf_op jit(solution)/shard_map/ppermute | solution.py:324
  14.1 2.1 %collective-permute-done.5.refs_1_ = bf16[16,6656]{1,0:T(8,128)(2,1)S(1)} collective-permute-done((bf16[16,6656]{1,0:T(8,128)(2,1)S(1)}, bf16[16,6656]{1,0:T(8,128)(2,1)S(1)}, u32[]{:S(2)}, u32[]{:S(2)}) %collective-permute-start.5) | collective-permute-done | bytes 213024 | tf_op jit(solution)/shard_map/ppermute | solution.py:324
  16.2 0.0 collective-permute-start.7
  16.2 0.1 shard_map.49
  16.3 7.1 %shard_map.51 = (bf16[2048,1984]{1,0:T(8,128)(2,1)S(1)}, bf16[2048,2256]{1,0:T(8,128)(2,1)S(1)}) custom-call(bf16[4752,2048]{1,0:T(8,128)(2,1)} %bitcast.5), custom_call_target="tpu_custom_call" | custom-call | bytes 17367040 | tf_op jit(solution)/shard_map/pallas_call | solution.py:32
  23.4 0.0 collective-permute-done.6.refs_2_
  23.4 0.4 shard_map.52.early_ref
  23.8 1.1 %collective-permute-done.7.block_ref = bf16[16,6656]{1,0:T(8,128)(2,1)S(1)} collective-permute-done((bf16[16,6656]{1,0:T(8,128)(2,1)S(1)}, bf16[16,6656]{1,0:T(8,128)(2,1)S(1)}, u32[]{:S(2)}, u32[]{:S(2)}) %collective-permute-start.7) | collective-permute-done | bytes 213024 | tf_op jit(solution)/shard_map/ppermute | solution.py:324
  24.9 2.2 %shard_map.53 = (bf16[176,2048]{1,0:T(8,128)(2,1)S(1)}, f32[88,2560]{1,0:T(8,128)S(1)}, f32[88,2560]{1,0:T(8,128)S(1)}) custom-call(bf16[176,64]{1,0:T(8,128)(2,1)S(1)} %get-tuple-element.67.chooser_ref, bf16[176,2048]{1,0:T(8,128)(2,1)S(1)} %shard_map.52.early_ref, bf16[16,6656]{1,0:T(8,128)(2,1)S(1)} %collective-permute-done.7.block_ref, ...), custom_call_target="tpu_custom_call" | custom-call | flops 1799356416 | bytes 10223616 | tf_op jit(solution)/shard_map/pallas_call | solution.py:32
  27.2 0.1 collective-permute-start.8
  27.3 1.9 %shard_map.56 = (f32[88,2304]{1,0:T(8,128)S(1)}, f32[88,2304]{1,0:T(8,128)S(1)}) custom-call(bf16[176,2048]{1,0:T(8,128)(2,1)S(1)} %get-tuple-element.79.rows_ref, bf16[2048,2256]{1,0:T(8,128)(2,1)S(1)} %get-tuple-element.80.refs_0_), custom_call_target="tpu_custom_call" | custom-call | flops 1626341376 | bytes 9240576 | tf_op jit(solution)/shard_map/pallas_call | solution.py:32
  29.2 0.6 %collective-permute-start.10 = (f32[88,2304]{1,0:T(8,128)S(1)}, f32[88,2304]{1,0:T(8,128)S(1)}, u32[]{:S(2)}, u32[]{:S(2)}) collective-permute-start(f32[88,2304]{1,0:T(8,128)S(1)} %get-tuple-element.82), channel_id=1, source_target_pairs={{0,1},{1,0},{2,3},{3,2},{4,5},{5,4},{6,7},{7,6},{8,9},{9,8},{10,11... | collective-permute-start | bytes 2433032 | tf_op jit(solution)/shard_map/ppermute | solution.py:324
  29.8 0.0 collective-permute-done.8.got_ref
  29.8 0.3 shard_map.54
  30.1 1.6 %collective-permute-start.9 = (s16[8,14080]{1,0:T(8,128)(2,1)S(1)}, s16[8,14080]{1,0:T(8,128)(2,1)S(1)}, u32[]{:S(2)}, u32[]{:S(2)}) collective-permute-start(s16[8,14080]{1,0:T(8,128)(2,1)S(1)} %get-tuple-element.76), channel_id=1, source_target_pairs={{0,2},{2,0},{1,3},{3,1},{4,6},{6,4},{5,7},{7,5},{8,10},{10,8},{9,1... | collective-permute-start | bytes 675848 | tf_op jit(solution)/shard_map/ppermute | solution.py:324
  31.6 0.1 collective-permute-done.10.got_ref
  31.7 0.2 shard_map.57
  32.0 1.6 %collective-permute-start.11 = (s16[8,12672]{1,0:T(8,128)(2,1)S(1)}, s16[8,12672]{1,0:T(8,128)(2,1)S(1)}, u32[]{:S(2)}, u32[]{:S(2)}) collective-permute-start(s16[8,12672]{1,0:T(8,128)(2,1)S(1)} %get-tuple-element.84), channel_id=1, source_target_pairs={{0,2},{2,0},{1,3},{3,1},{4,6},{6,4},{5,7},{7,5},{8,10},{10,8},{9,1... | collective-permute-start | bytes 608264 | tf_op jit(solution)/shard_map/ppermute | solution.py:324
  33.6 4.9 %collective-permute-done.9.refs_1_ = s16[8,14080]{1,0:T(8,128)(2,1)S(1)} collective-permute-done((s16[8,14080]{1,0:T(8,128)(2,1)S(1)}, s16[8,14080]{1,0:T(8,128)(2,1)S(1)}, u32[]{:S(2)}, u32[]{:S(2)}) %collective-permute-start.9) | collective-permute-done | bytes 225312 | tf_op jit(solution)/shard_map/ppermute | solution.py:324
  38.5 0.4 shard_map.55
  38.9 3.1 %collective-permute-done.11.refs_2_ = s16[8,12672]{1,0:T(8,128)(2,1)S(1)} collective-permute-done((s16[8,12672]{1,0:T(8,128)(2,1)S(1)}, s16[8,12672]{1,0:T(8,128)(2,1)S(1)}, u32[]{:S(2)}, u32[]{:S(2)}) %collective-permute-start.11) | collective-permute-done | bytes 202784 | tf_op jit(solution)/shard_map/ppermute | solution.py:324
  42.0 0.4 shard_map.58
  42.4 0.9 %collective-permute-start.14 = (f32[2,128]{1,0:T(2,128)S(1)}, f32[2,128]{1,0:T(2,128)S(1)}, u32[]{:S(2)}, u32[]{:S(2)}) collective-permute-start(f32[2,128]{1,0:T(2,128)S(1)} %get-tuple-element.86.refs_2_), channel_id=1, source_target_pairs={{0,8},{4,12},{8,0},{12,4},{1,9},{5,13},{9,1},{13,5},{2,10},{6,14},... | collective-permute-start | bytes 3080 | tf_op jit(solution)/shard_map/ppermute | solution.py:488
  43.3 1.9 %collective-permute-start.13 = (f32[2,128]{1,0:T(2,128)S(1)}, f32[2,128]{1,0:T(2,128)S(1)}, u32[]{:S(2)}, u32[]{:S(2)}) collective-permute-start(f32[2,128]{1,0:T(2,128)S(1)} %get-tuple-element.86.refs_2_), channel_id=1, source_target_pairs={{0,12},{4,8},{8,4},{12,0},{1,13},{5,9},{9,5},{13,1},{2,14},{6,10},... | collective-permute-start | bytes 3080 | tf_op jit(solution)/shard_map/ppermute | solution.py:488
  45.2 0.7 %collective-permute-start.12 = (f32[2,128]{1,0:T(2,128)S(1)}, f32[2,128]{1,0:T(2,128)S(1)}, u32[]{:S(2)}, u32[]{:S(2)}) collective-permute-start(f32[2,128]{1,0:T(2,128)S(1)} %get-tuple-element.86.refs_2_), channel_id=1, source_target_pairs={{0,4},{4,0},{8,12},{12,8},{1,5},{5,1},{9,13},{13,9},{2,6},{6,2},{1... | collective-permute-start | bytes 3080 | tf_op jit(solution)/shard_map/ppermute | solution.py:488
  45.9 1.0 %collective-permute-done.14.refs_5_ = f32[2,128]{1,0:T(2,128)S(1)} collective-permute-done((f32[2,128]{1,0:T(2,128)S(1)}, f32[2,128]{1,0:T(2,128)S(1)}, u32[]{:S(2)}, u32[]{:S(2)}) %collective-permute-start.14) | collective-permute-done | bytes 1056 | tf_op jit(solution)/shard_map/ppermute | solution.py:488
  46.9 1.7 %collective-permute-done.13.refs_4_ = f32[2,128]{1,0:T(2,128)S(1)} collective-permute-done((f32[2,128]{1,0:T(2,128)S(1)}, f32[2,128]{1,0:T(2,128)S(1)}, u32[]{:S(2)}, u32[]{:S(2)}) %collective-permute-start.13) | collective-permute-done | bytes 1056 | tf_op jit(solution)/shard_map/ppermute | solution.py:488
  48.6 0.1 collective-permute-done.12.refs_3_
  48.8 1.2 %shard_map.59 = f32[44,4752]{1,0:T(8,128)} custom-call(f32[48,2560]{1,0:T(8,128)S(1)} %get-tuple-element.77.refs_0_, f32[48,2304]{1,0:T(8,128)S(1)} %get-tuple-element.85.refs_1_, f32[2,128]{1,0:T(2,128)S(1)} %get-tuple-element.86.refs_2_, f32[2,128]{1,0:T(2,128)S(1)} %collective-permute-done.12.refs_3_, f32[2,128]{1,0:T(2,128)S(1)} %collective-permute-done.13.refs_4_, ...), custom_call_target="tpu_custom_call" | custom-call | tf_op jit(solution)/shard_map/pallas_call | solution.py:492
  (4 shorter events, 0.1 us)
Async XLA Ops:
  1.3 1.3 %collective-permute-start.3 = (f32[2,64]{1,0:T(2,128)S(1)}, f32[2,64]{1,0:T(2,128)S(1)}, u32[]{:S(2)}, u32[]{:S(2)}) collective-permute-start(f32[2,64]{1,0:T(2,128)S(1)} %get-tuple-element.53), channel_id=1, source_target_pairs={{0,1},{1,0},{2,3},{3,2},{4,5},{5,4},{6,7},{7,6},{8,9},{9,8},{10,11... | collective-permute-start | bytes 1544 | tf_op jit(solution)/shard_map/ppermute | solution.py:324
  2.6 4.4 %collective-permute-start.4 = (f32[2,64]{1,0:T(2,128)S(1)}, f32[2,64]{1,0:T(2,128)S(1)}, u32[]{:S(2)}, u32[]{:S(2)}) collective-permute-start(f32[2,64]{1,0:T(2,128)S(1)} %add.6), channel_id=1, source_target_pairs={{0,2},{2,0},{1,3},{3,1},{4,6},{6,4},{5,7},{7,5},{8,10},{10,8},{9,1... | collective-permute-start | bytes 1544 | tf_op jit(solution)/shard_map/ppermute | solution.py:324
  7.2 9.0 %collective-permute-start.5 = (bf16[16,6656]{1,0:T(8,128)(2,1)S(1)}, bf16[16,6656]{1,0:T(8,128)(2,1)S(1)}, u32[]{:S(2)}, u32[]{:S(2)}) collective-permute-start(bf16[16,6656]{1,0:T(8,128)(2,1)S(1)} %get-tuple-element.69.refs_0_), channel_id=1, source_target_pairs={{0,4},{4,8},{8,12},{12,0},{1,5},{5,9},{9,13},{13,1},{2,6},{6,10},{... | collective-permute-start | bytes 638984 | tf_op jit(solution)/shard_map/ppermute | solution.py:324
  12.0 11.5 %collective-permute-start.6 = (bf16[16,6656]{1,0:T(8,128)(2,1)S(1)}, bf16[16,6656]{1,0:T(8,128)(2,1)S(1)}, u32[]{:S(2)}, u32[]{:S(2)}) collective-permute-start(bf16[16,6656]{1,0:T(8,128)(2,1)S(1)} %get-tuple-element.69.refs_0_), channel_id=1, source_target_pairs={{0,12},{4,0},{8,4},{12,8},{1,13},{5,1},{9,5},{13,9},{2,14},{6,2},{... | collective-permute-start | bytes 638984 | tf_op jit(solution)/shard_map/ppermute | solution.py:324
  16.2 8.8 %collective-permute-start.7 = (bf16[16,6656]{1,0:T(8,128)(2,1)S(1)}, bf16[16,6656]{1,0:T(8,128)(2,1)S(1)}, u32[]{:S(2)}, u32[]{:S(2)}) collective-permute-start(bf16[16,6656]{1,0:T(8,128)(2,1)S(1)} %collective-permute-done.5.refs_1_), channel_id=1, source_target_pairs={{0,4},{4,8},{8,12},{12,0},{1,5},{5,9},{9,13},{13,1},{2,6},{6,10},{... | collective-permute-start | bytes 638984 | tf_op jit(solution)/shard_map/ppermute | solution.py:324
  27.2 2.6 %collective-permute-start.8 = (f32[88,2560]{1,0:T(8,128)S(1)}, f32[88,2560]{1,0:T(8,128)S(1)}, u32[]{:S(2)}, u32[]{:S(2)}) collective-permute-start(f32[88,2560]{1,0:T(8,128)S(1)} %get-tuple-element.74), channel_id=1, source_target_pairs={{0,1},{1,0},{2,3},{3,2},{4,5},{5,4},{6,7},{7,6},{8,9},{9,8},{10,11... | collective-permute-start | bytes 2703368 | tf_op jit(solution)/shard_map/ppermute | solution.py:324
  29.2 2.5 %collective-permute-start.10 = (f32[88,2304]{1,0:T(8,128)S(1)}, f32[88,2304]{1,0:T(8,128)S(1)}, u32[]{:S(2)}, u32[]{:S(2)}) collective-permute-start(f32[88,2304]{1,0:T(8,128)S(1)} %get-tuple-element.82), channel_id=1, source_target_pairs={{0,1},{1,0},{2,3},{3,2},{4,5},{5,4},{6,7},{7,6},{8,9},{9,8},{10,11... | collective-permute-start | bytes 2433032 | tf_op jit(solution)/shard_map/ppermute | solution.py:324
  30.1 8.4 %collective-permute-start.9 = (s16[8,14080]{1,0:T(8,128)(2,1)S(1)}, s16[8,14080]{1,0:T(8,128)(2,1)S(1)}, u32[]{:S(2)}, u32[]{:S(2)}) collective-permute-start(s16[8,14080]{1,0:T(8,128)(2,1)S(1)} %get-tuple-element.76), channel_id=1, source_target_pairs={{0,2},{2,0},{1,3},{3,1},{4,6},{6,4},{5,7},{7,5},{8,10},{10,8},{9,1... | collective-permute-start | bytes 675848 | tf_op jit(solution)/shard_map/ppermute | solution.py:324
  32.0 10.0 %collective-permute-start.11 = (s16[8,12672]{1,0:T(8,128)(2,1)S(1)}, s16[8,12672]{1,0:T(8,128)(2,1)S(1)}, u32[]{:S(2)}, u32[]{:S(2)}) collective-permute-start(s16[8,12672]{1,0:T(8,128)(2,1)S(1)} %get-tuple-element.84), channel_id=1, source_target_pairs={{0,2},{2,0},{1,3},{3,1},{4,6},{6,4},{5,7},{7,5},{8,10},{10,8},{9,1... | collective-permute-start | bytes 608264 | tf_op jit(solution)/shard_map/ppermute | solution.py:324
  42.4 4.5 %collective-permute-start.14 = (f32[2,128]{1,0:T(2,128)S(1)}, f32[2,128]{1,0:T(2,128)S(1)}, u32[]{:S(2)}, u32[]{:S(2)}) collective-permute-start(f32[2,128]{1,0:T(2,128)S(1)} %get-tuple-element.86.refs_2_), channel_id=1, source_target_pairs={{0,8},{4,12},{8,0},{12,4},{1,9},{5,13},{9,1},{13,5},{2,10},{6,14},... | collective-permute-start | bytes 3080 | tf_op jit(solution)/shard_map/ppermute | solution.py:488
  43.3 5.4 %collective-permute-start.13 = (f32[2,128]{1,0:T(2,128)S(1)}, f32[2,128]{1,0:T(2,128)S(1)}, u32[]{:S(2)}, u32[]{:S(2)}) collective-permute-start(f32[2,128]{1,0:T(2,128)S(1)} %get-tuple-element.86.refs_2_), channel_id=1, source_target_pairs={{0,12},{4,8},{8,4},{12,0},{1,13},{5,9},{9,5},{13,1},{2,14},{6,10},... | collective-permute-start | bytes 3080 | tf_op jit(solution)/shard_map/ppermute | solution.py:488
  45.2 3.6 %collective-permute-start.12 = (f32[2,128]{1,0:T(2,128)S(1)}, f32[2,128]{1,0:T(2,128)S(1)}, u32[]{:S(2)}, u32[]{:S(2)}) collective-permute-start(f32[2,128]{1,0:T(2,128)S(1)} %get-tuple-element.86.refs_2_), channel_id=1, source_target_pairs={{0,4},{4,0},{8,12},{12,8},{1,5},{5,1},{9,13},{13,9},{2,6},{6,2},{1... | collective-permute-start | bytes 3080 | tf_op jit(solution)/shard_map/ppermute | solution.py:488
